TPU v7x, 512 devices: a whole 4x4x16 slice. The times are simulated.
512 devices in a mesh: rows: 64 (over y, z), cent: 8 (over x, core).
Axes of the slice: x: 4, y: 4, z: 16, core: 2. Of those that a mesh axis runs over, the one named last changes fastest.
Arguments:
- embeddings: bfloat16 [24576, 1024], P('rows'), may hold values from -288 to 288
- centroids: bfloat16 [16384, 1024], P('cent'), may hold values from -12 to 12
- codebook: bfloat16 [8, 4096, 128], P('cent', 'rows'), may hold values from -6 to 6
Outputs:
- residual: bfloat16 [1024, 24576], P('cent', 'rows')
- new_codebook: float32 [8, 4096, 128], P('cent', 'rows')
- pq_error: float32 [8, 24576], P('cent', 'rows')
All inputs are finite; a program needn't handle non-finite values.
Results may differ from a plain program's by a relative error of at most 0.04.
Values may be sent and summed in bfloat16 or wider, within the bound.
No kernel may reach another device: no remote copies, remote signals or barrier semaphores. Data moves between devices by JAX's collectives and lax.ppermute only.
A program may use at most 64 MiB of HBM per device.

v0:
```python
import math

import jax
import jax.numpy as jnp
from jax import lax
from jax.sharding import PartitionSpec as P

smoothing = 1.0


def local(embeddings, centroids, codebook):
    rows_here = embeddings.shape[0]
    model_width = embeddings.shape[1]
    cent_count = lax.axis_size("cent")
    slice_width = model_width // cent_count
    sub_width = codebook.shape[2]
    local_subs = codebook.shape[0]
    book_rows = codebook.shape[1]
    products = lax.dot_general(
        embeddings, centroids, (((1,), (1,)), ((), ())), preferred_element_type=jnp.float32
    )
    cent_wide = centroids.astype(jnp.float32)
    half_norm = 0.5 * jnp.sum(cent_wide * cent_wide, axis=1)
    logits = (products - half_norm[None, :]) * (2.0 / math.sqrt(model_width))
    local_max = jnp.max(logits, axis=1)
    row_max = lax.pmax(local_max, "cent")
    shifted = jnp.exp(logits - row_max[:, None])
    row_total = lax.psum(jnp.sum(shifted, axis=1), "cent")
    coarse_weights = shifted.astype(jnp.bfloat16)
    pulled = lax.psum_scatter(
        lax.dot_general(
            centroids, coarse_weights, (((0,), (1,)), ((), ())), preferred_element_type=jnp.float32
        ).astype(jnp.bfloat16),
        "cent",
        scatter_dimension=0,
        tiled=True,
    ).astype(jnp.float32)
    own_cols = lax.dynamic_slice_in_dim(
        embeddings, lax.axis_index("cent") * slice_width, slice_width, 1
    )
    residual = (own_cols.T.astype(jnp.float32) - pulled / row_total[None, :]).astype(jnp.bfloat16)
    blocks = residual.reshape(local_subs, sub_width, rows_here)
    full_book = lax.all_gather(codebook, "rows", axis=1, tiled=True)
    scores = jnp.einsum("skd,sdr->skr", full_book, blocks, preferred_element_type=jnp.float32)
    book_wide = full_book.astype(jnp.float32)
    book_half = 0.5 * jnp.sum(book_wide * book_wide, axis=2)
    pq_logits = (scores - book_half[:, :, None]) * (2.0 / math.sqrt(sub_width))
    pq_peak = jnp.max(pq_logits, axis=1, keepdims=True)
    raised = jnp.exp(pq_logits - pq_peak)
    pq_probs = raised / jnp.sum(raised, axis=1, keepdims=True)
    pq_weights = pq_probs.astype(jnp.bfloat16)
    rebuilt = jnp.einsum("skd,skr->sdr", full_book, pq_weights, preferred_element_type=jnp.float32)
    pq_error = jnp.mean(jnp.square(blocks.astype(jnp.float32) - rebuilt), axis=1)
    word_sums = jnp.einsum("skr,sdr->skd", pq_weights, blocks, preferred_element_type=jnp.float32)
    counts = jnp.sum(pq_probs, axis=2)
    all_sums, all_counts = lax.psum((word_sums, counts), "rows")
    first_row = lax.axis_index("rows") * book_rows
    own_sums = lax.dynamic_slice_in_dim(all_sums, first_row, book_rows, 1)
    own_counts = lax.dynamic_slice_in_dim(all_counts, first_row, book_rows, 1)
    new_codebook = (own_sums + smoothing * codebook.astype(jnp.float32)) / (
        own_counts[:, :, None] + smoothing
    )
    return (residual, new_codebook, pq_error)


def solution(mesh):
    placed = (P("rows", None), P("cent", None), P("cent", "rows", None))
    return jax.shard_map(
        local,
        mesh=mesh,
        in_specs=placed,
        out_specs=(P("cent", "rows"), P("cent", "rows", None), P("cent", "rows")),
        check_vma=False,
    )
```

profile of v0, /device:TPU:6, one launch (start us, length us, event | category | flops | bytes accessed | tf_op | source)
XLA Modules:
  0.0 482.4 jit_solution(5333590064419053193)
XLA Ops:
  8.0 0.0 copy-start
  8.0 0.0 reduce-scatter.4.cloned.1.call-start
  8.1 0.0 copy-start.3
  8.1 3.2 multiply_reduce_fusion
  11.3 0.4 copy-done.3
  11.7 3.5 fusion.35
  15.2 14.3 %pmax.7 = f32[384]{0:T(512)S(1)} all-reduce(f32[384]{0:T(512)S(1)} %get-tuple-element.8), channel_id=1, replica_groups=mesh['rows'=64,'cent'=8] {'cent'}, use_global_device_ids=true, to_apply=%region_2.0 | all-reduce | flops 384 | bytes 3072 | tf_op jit(solution)/shard_map/pmax | solution.py:26
  29.5 5.0 %fusion.13 = bf16[1024,384]{0,1:T(8,128)(2,1)S(1)} fusion(bf16[2048,1024]{1,0:T(8,128)(2,1)} %param.4, f32[384,2048]{1,0:T(8,128)} %get-tuple-element.9, f32[384]{0:T(512)S(1)} %pmax.7), kind=kOutput, calls=%fused_computation.17 | convolution fusion | flops 1612578816 | bytes 8128000 | tf_op jit(solution)/shard_map/dot_general | solution.py:31
  34.5 1.2 copy.10
  35.7 0.0 reduce-scatter.4.cloned.1.call-update
  35.7 0.0 all-gather.2.cloned.1.call-start
  35.8 0.5 all-gather.2.cloned.1.call-update
  36.3 0.0 all-reduce.2.cloned.1.call-start
  36.4 0.1 copy.12
  36.5 2.5 fusion.2
  39.0 12.4 %psum.21 = f32[384]{0:T(512)S(1)} all-reduce(f32[384]{0:T(512)S(1)} %fusion.2), channel_id=1, replica_groups=mesh['rows'=64,'cent'=8] {'cent'}, use_global_device_ids=true, to_apply=%region_5.0 | all-reduce | flops 384 | bytes 3072 | tf_op jit(solution)/shard_map/psum | solution.py:28
  51.4 22.9 %reduce-scatter.4.cloned.1.call-done = bf16[128,384]{1,0:T(8,128)(2,1)} async-done(((bf16[1024,384]{1,0:T(8,128)(2,1)}), bf16[128,384]{1,0:T(8,128)(2,1)}) %reduce-scatter.4.cloned.1.call-update) | async-done | bytes 98320 | tf_op jit(solution)/shard_map/reduce_scatter | solution.py:30
  74.3 0.9 fusion.30
  75.2 0.0 copy-start.4
  75.2 106.1 %all-gather.2.cloned.1.call-done = bf16[1,4096,128]{2,1,0:T(8,128)(2,1)} async-done(((bf16[1,64,128]{2,1,0:T(8,128)(2,1)}), bf16[1,4096,128]{2,1,0:T(8,128)(2,1)}) %all-gather.2.cloned.1.call-update) | async-done | bytes 1048592 | tf_op jit(solution)/shard_map/all_gather | solution.py:43
  181.3 1.8 multiply_reduce_fusion.1
  183.2 2.4 fusion.36
  185.5 1.0 fusion
  186.5 1.5 fusion.33
  188.0 1.7 copy-done.1
  189.7 2.4 convolution_bitcast_fusion
  192.1 0.0 all-reduce.2.cloned.1.call-update
  192.2 2.9 fusion.25
  195.1 0.6 div.41
  195.7 277.8 %psum.23 = f32[1,4096]{1,0:T(1,128)S(1)} all-reduce(f32[1,4096]{1,0:T(1,128)S(1)} %bitcast.34), channel_id=1, replica_groups=mesh['rows'=64,'cent'=8] {'rows'}, use_global_device_ids=true, to_apply=%region_11.0 | all-reduce | flops 4096 | bytes 32768 | tf_op jit(solution)/shard_map/psum | solution.py:56
  473.4 0.1 fusion.32
  473.5 1.5 add_divide_fusion
  (12 shorter events, 0.1 us)
Async XLA Ops:
  8.0 3.3 copy-start
  8.0 66.3 %reduce-scatter.4.cloned.1.call-start = ((), (), s32[]{:S(2)}) async-start(), calls=%async_computation.3 | async-start | bytes 884736 | tf_op jit(solution)/shard_map/reduce_scatter | solution.py:30
  8.1 3.7 copy-start.3
  35.7 145.6 %all-gather.2.cloned.1.call-start = ((), (), s32[]{:S(2)}) async-start(), calls=%async_computation.1 | async-start | bytes 1064960 | tf_op jit(solution)/shard_map/all_gather | solution.py:43
  36.3 437.2 %all-reduce.2.cloned.1.call-start = ((), (), s32[]{:S(2)}) async-start(), calls=%async_computation.2 | async-start | bytes 4194304 | tf_op jit(solution)/shard_map/psum | solution.py:56
  75.2 116.9 %copy-start.4 = (bf16[128,384]{1,0:T(8,128)(2,1)}, bf16[128,384]{1,0:T(8,128)(2,1)S(1)}, u32[]{:S(2)}) copy-start(bf16[128,384]{1,0:T(8,128)(2,1)S(1)} %fusion.30) | copy-start | bytes 294916
  188.0 1.7 copy-start.1
  189.7 2.5 copy-start.2
  192.1 281.4 %copy-start.5 = (bf16[1,64,128]{2,1,0:T(8,128)(2,1)S(1)}, bf16[1,64,128]{2,1,0:T(8,128)(2,1)}, u32[]{:S(2)}) copy-start(bf16[1,64,128]{2,1,0:T(8,128)(2,1)} %param.5) | copy-start | bytes 49156
Sparse Core Ops, SparseCore 0:
  35.8 38.4 reduce-scatter.3
Sparse Core Ops, SparseCore 1:
  39.5 141.7 all-gather.1
  192.2 274.7 all-reduce.1
where the time goes:
time: 483 us; the launch traced here: 482 us
  blocking collectives  304 us (63%)
  waiting for transfers between devices  130 us (27%)
  matrix products  16.2 us (3%)
  between operations  15.6 us (3%)
  other arithmetic  12.5 us (3%)
    psum x1, blocking collectives, local(): all_sums, all_counts = lax.psum((word_sums, counts), 'rows')  278 us
    all_gather x1, waiting for transfers between devices, local(): full_book = lax.all_gather(codebook, 'rows', axis=1, tiled=True)  106 us
    reduce_scatter x1, waiting for transfers between devices, local(): lax.psum_scatter(lax.dot_general(centroids, coarse_weights, (((0,), (1,))...  22.9 us
    pmax x1, blocking collectives, local(): row_max = lax.pmax(local_max, 'cent')  14.3 us
    psum x1, blocking collectives, local(): row_total = lax.psum(jnp.sum(shifted, axis=1), 'cent')  12.4 us
  transfers between devices with their start and end apart: 3, of which 2 were waited for; matrix products, arithmetic and copies ran while one was open for 1% of the time, Pallas kernels for 0%

commit v1 on v0

v1 whole, which is shorter than its diff:
```python
import math

import jax
import jax.numpy as jnp
from jax import lax
from jax.sharding import Mesh, PartitionSpec as P

smoothing = 1.0
CENT = ("x", "c")


def split(value):
    terms = []
    for _ in range(3):
        term = lax.reduce_precision(value, 8, 7)
        terms.append(term.astype(jnp.bfloat16))
        value = value - term
    return jnp.stack(terms)


def join(terms):
    wide = terms.astype(jnp.float32)
    return (wide[..., 2, :] + wide[..., 1, :]) + wide[..., 0, :]


def exchange(parts, axis):
    return lax.all_to_all(parts, axis, 0, 0, tiled=True)


def local(embeddings, centroids, codebook):
    rows_here, model_width = embeddings.shape
    cent_count = lax.axis_size(CENT)
    slice_width = model_width // cent_count
    _, book_rows, sub_width = codebook.shape
    y_count, z_count = lax.axis_size("y"), lax.axis_size("z")
    words = book_rows * y_count * z_count

    own = codebook.reshape(book_rows, sub_width)
    book = exchange(jnp.broadcast_to(own, (z_count, book_rows, sub_width)), "z")
    book = lax.all_gather(book.reshape(words // y_count, sub_width), "y", axis=0, tiled=True)

    products = lax.dot_general(
        embeddings, centroids, (((1,), (1,)), ((), ())), preferred_element_type=jnp.float32
    )
    cent_wide = centroids.astype(jnp.float32)
    half_norm = 0.5 * jnp.sum(cent_wide * cent_wide, axis=1)
    logits = (products - half_norm[None, :]) * (2.0 / math.sqrt(model_width))
    slab_max = jnp.max(logits, axis=1)
    shifted = jnp.exp(logits - slab_max[:, None])
    slab_total = jnp.sum(shifted, axis=1)
    pulled = lax.dot_general(
        centroids, shifted.astype(jnp.bfloat16), (((0,), (1,)), ((), ())), preferred_element_type=jnp.float32
    )
    pulled = (pulled / slab_total[None, :]).astype(jnp.bfloat16)

    stats = jnp.concatenate([split(slab_max), split(slab_total)])
    stats = jnp.pad(stats, ((0, 10), (0, 0)))
    parts = jnp.concatenate(
        [
            pulled.reshape(cent_count, slice_width, rows_here),
            jnp.broadcast_to(stats, (cent_count,) + stats.shape),
        ],
        axis=1,
    )
    parts = exchange(parts, CENT)
    slab_maxes = join(parts[:, slice_width : slice_width + 3])
    slab_totals = join(parts[:, slice_width + 3 : slice_width + 6])
    row_max = jnp.max(slab_maxes, axis=0)
    shares = jnp.exp(slab_maxes - row_max) * slab_totals
    shares = shares / jnp.sum(shares, axis=0)
    mean = jnp.sum(parts[:, :slice_width].astype(jnp.float32) * shares[:, None, :], axis=0)
    own_cols = lax.dynamic_slice_in_dim(
        embeddings, lax.axis_index(CENT) * slice_width, slice_width, 1
    )
    residual = (own_cols.T.astype(jnp.float32) - mean).astype(jnp.bfloat16)

    scores = jnp.dot(book, residual, preferred_element_type=jnp.float32)
    book_wide = book.astype(jnp.float32)
    book_half = 0.5 * jnp.sum(book_wide * book_wide, axis=1)
    pq_logits = (scores - book_half[:, None]) * (2.0 / math.sqrt(sub_width))
    pq_peak = jnp.max(pq_logits, axis=0, keepdims=True)
    raised = jnp.exp(pq_logits - pq_peak)
    pq_probs = raised / jnp.sum(raised, axis=0, keepdims=True)
    pq_weights = pq_probs.astype(jnp.bfloat16)
    rebuilt = lax.dot_general(
        book, pq_weights, (((0,), (0,)), ((), ())), preferred_element_type=jnp.float32
    )
    pq_error = jnp.mean(jnp.square(residual.astype(jnp.float32) - rebuilt), axis=0)
    word_sums = lax.dot_general(
        pq_weights, residual, (((1,), (1,)), ((), ())), preferred_element_type=jnp.float32
    )
    counts = jnp.sum(pq_probs, axis=1)

    counts = jnp.swapaxes(split(counts).reshape(3, y_count, words // y_count), 0, 1)
    counts = jnp.pad(counts.reshape(y_count, -1, sub_width), ((0, 0), (0, 8), (0, 0)))
    sums = jnp.concatenate(
        [word_sums.astype(jnp.bfloat16).reshape(y_count, words // y_count, sub_width), counts], axis=1
    )
    sums = exchange(sums, "y")
    quarter = words // y_count
    counts = join(sums[:, quarter : quarter + 3 * quarter // sub_width].reshape(y_count, 3, quarter))
    counts = jnp.sum(counts, axis=0)
    sums = jnp.sum(sums[:, :quarter].astype(jnp.float32), axis=0)
    counts = jnp.swapaxes(split(counts).reshape(3, z_count, book_rows), 0, 1)
    counts = jnp.pad(counts.reshape(z_count, 1, 3 * book_rows), ((0, 0), (0, 0), (0, 4 * sub_width - 3 * book_rows)))
    sums = jnp.concatenate(
        [
            sums.astype(jnp.bfloat16).reshape(z_count, book_rows, sub_width),
            counts.reshape(z_count, 4, sub_width),
            jnp.zeros((z_count, 12, sub_width), jnp.bfloat16),
        ],
        axis=1,
    )
    sums = exchange(sums, "z")
    counts = sums[:, book_rows : book_rows + 4].reshape(z_count, -1)[:, : 3 * book_rows]
    counts = jnp.sum(join(counts.reshape(z_count, 3, book_rows)), axis=0)
    sums = jnp.sum(sums[:, :book_rows].astype(jnp.float32), axis=0)
    new_codebook = (sums + smoothing * own.astype(jnp.float32)) / (counts[:, None] + smoothing)
    return (residual, new_codebook[None], pq_error[None])


def solution(mesh):
    sizes = (4, 16, 4, 2)
    wide = Mesh(mesh.devices.reshape(sizes), ("y", "z", "x", "c"))
    rows = ("y", "z")
    placed = (P(rows, None), P(CENT, None), P(CENT, rows, None))
    return jax.shard_map(
        local,
        mesh=wide,
        in_specs=placed,
        out_specs=(P(CENT, rows), P(CENT, rows, None), P(CENT, rows)),
        check_vma=False,
    )
```

time: 483 us -> 146 us (0.30)
  blocking collectives: 304 us -> 0 us
  waiting for transfers between devices: 130 us -> 68.5 us
  starting transfers between devices: 0.12 us -> 35.8 us
  matrix products: 16.2 us -> 10.1 us
    psum x2 -> x0, blocking collectives: 290 us -> none  [the longest x1 278 us: local(): all_sums, all_counts = lax.psum((word_sums, counts), 'rows')]
    all_gather x1, waiting for transfers between devices: 106 us -> 17.2 us  [local(): lax.all_gather(book.reshape(words // y_count, sub_width), 'y', axis=0, ti...]
    all_to_all x0 -> x4, waiting for transfers between devices: none -> 50.8 us  [exchange(): return lax.all_to_all(parts, axis, 0, 0, tiled=True)]
    all_to_all x0 -> x4, starting transfers between devices: none -> 35.8 us  [exchange(): return lax.all_to_all(parts, axis, 0, 0, tiled=True)]
    reduce_scatter x1 -> x0, waiting for transfers between devices: 22.9 us -> none  [local(): lax.psum_scatter(lax.dot_general(centroids, coarse_weights, (((0,), (1,))...]
    pmax x1 -> x0, blocking collectives: 14.3 us -> none  [local(): row_max = lax.pmax(local_max, 'cent')]
  transfers between devices with their start and end apart: 3 -> 5, of which waited for: 2 -> 5; matrix products, arithmetic and copies ran while one was open for 1% -> 9% of each run, Pallas kernels for 0% -> 0%
where the time goes in v1:
time: 146 us; the launch traced here: 145 us
  waiting for transfers between devices  68.5 us (47%)
  starting transfers between devices  35.8 us (25%)
  between operations  14.3 us (10%)
  other arithmetic  12.4 us (8%)
  matrix products  10.1 us (7%)
  local copies, waits for them, and re-layouts  3.99 us (3%)
    all_to_all x4, waiting for transfers between devices, exchange(): return lax.all_to_all(parts, axis, 0, 0, tiled=True)  50.8 us
    all_to_all x4, starting transfers between devices, exchange(): return lax.all_to_all(parts, axis, 0, 0, tiled=True)  35.8 us
    all_gather x1, waiting for transfers between devices, local(): lax.all_gather(book.reshape(words // y_count, sub_width), 'y', axis=0, ti...  17.2 us
    reduce_sum x1, other arithmetic, local(): half_norm = 0.5 * jnp.sum(cent_wide * cent_wide, axis=1)  3.22 us
  transfers between devices with their start and end apart: 5, of which 5 were waited for; matrix products, arithmetic and copies ran while one was open for 9% of the time, Pallas kernels for 0%

profile of v1, /device:TPU:6, one launch (start us, length us, event | category | flops | bytes accessed | tf_op | source)
XLA Modules:
  0.0 145.1 jit_solution(239731901548863075)
XLA Ops:
  7.2 1.5 %broadcast_in_dim.7 = bf16[16,64,128]{2,1,0:T(8,128)(2,1)} broadcast(bf16[64,128]{1,0:T(8,128)(2,1)} %bitcast.58), dimensions={1,2} | broadcast | bytes 278528 | tf_op jit(solution)/shard_map/broadcast_in_dim | solution.py:39
  8.7 15.2 %all-to-all-start.1 = ((bf16[16,64,128]{2,1,0:T(8,128)(2,1)}), bf16[16,64,128]{2,1,0:T(8,128)(2,1)S(1)}, u32[]{:S(2)}, u32[]{:S(2)}) async-start(bf16[16,64,128]{2,1,0:T(8,128)(2,1)} %broadcast_in_dim.7), calls=%async_computation.1 | async-start | bytes 524288 | tf_op jit(solution)/shard_map/all_to_all | solution.py:27
  23.9 3.2 %multiply_reduce_fusion = f32[2048]{0:T(1024)S(1)} fusion(bf16[2048,1024]{1,0:T(8,128)(2,1)} %param.4), kind=kLoop, calls=%fused_computation | loop fusion | flops 6289408 | bytes 4202496 | tf_op jit(solution)/shard_map/reduce_sum | solution.py:46
  27.2 0.2 copy-done.3
  27.4 1.9 %fusion.47 = (f32[384]{0:T(512)S(1)}, f32[384,2048]{1,0:T(8,128)S(1)}) fusion(f32[2048]{0:T(1024)S(1)} %broadcast_multiply_fusion.1, bf16[384,1024]{1,0:T(8,128)(2,1)S(1)} %copy-done, bf16[2048,1024]{1,0:T(8,128)(2,1)S(1)} %copy-done.3), kind=kOutput, calls=%fused_computation.88 | convolution fusion | flops 1612971648 | bytes 8136192 | tf_op jit(solution)/shard_map/dot_general | solution.py:42
  29.3 0.6 fusion.2
  29.9 1.9 %fusion.13 = bf16[1024,384]{0,1:T(8,128)(2,1)S(1)} fusion(bf16[2048,1024]{1,0:T(8,128)(2,1)S(1)} %copy-done.3, f32[384,2048]{1,0:T(8,128)S(1)} %get-tuple-element.22, f32[384]{0:T(512)S(1)} %get-tuple-element.21, f32[384]{0:T(512)S(1)} %fusion.2), kind=kOutput, calls=%fused_computation.20 | convolution fusion | flops 1612972032 | bytes 8129536 | tf_op jit(solution)/shard_map/dot_general | solution.py:51
  31.8 0.4 copy.25
  32.2 1.0 pad_maximum_fusion
  33.2 9.1 %all-to-all-done.1 = bf16[16,64,128]{2,1,0:T(8,128)(2,1)S(1)} async-done(((bf16[16,64,128]{2,1,0:T(8,128)(2,1)}), bf16[16,64,128]{2,1,0:T(8,128)(2,1)S(1)}, u32[]{:S(2)}, u32[]{:S(2)}) %all-to-all-start.1) | async-done | bytes 262176 | tf_op jit(solution)/shard_map/all_to_all | solution.py:27
  42.3 4.8 %all-to-all-start = ((bf16[8,144,384]{2,1,0:T(8,128)(2,1)}), bf16[8,144,384]{2,1,0:T(8,128)(2,1)S(1)}, u32[]{:S(2)}, u32[]{:S(2)}) async-start(bf16[8,144,384]{2,1,0:T(8,128)(2,1)} %pad_maximum_fusion), calls=%async_computation | async-start | bytes 1769472 | tf_op jit(solution)/shard_map/all_to_all | solution.py:27
  47.1 0.1 copy.26
  47.2 0.5 all-gather.2.cloned.1.call-update
  47.8 11.4 %all-to-all-done = bf16[8,144,384]{2,1,0:T(8,128)(2,1)S(1)} async-done(((bf16[8,144,384]{2,1,0:T(8,128)(2,1)}), bf16[8,144,384]{2,1,0:T(8,128)(2,1)S(1)}, u32[]{:S(2)}, u32[]{:S(2)}) %all-to-all-start) | async-done | bytes 884768 | tf_op jit(solution)/shard_map/all_to_all | solution.py:27
  59.3 0.2 multiply_reduce_fusion.2
  59.5 17.2 %all-gather.2.cloned.1.call-done = bf16[4096,128]{1,0:T(8,128)(2,1)} async-done(((bf16[1024,128]{1,0:T(8,128)(2,1)}), bf16[4096,128]{1,0:T(8,128)(2,1)}) %all-gather.2.cloned.1.call-update) | async-done | bytes 1048592 | tf_op jit(solution)/shard_map/all_gather | solution.py:40
  76.7 1.8 %multiply_reduce_fusion.1 = f32[4096]{0:T(1024)S(1)} fusion(bf16[4096,128]{1,0:T(8,128)(2,1)} %all-gather.2.cloned.1.call-done), kind=kLoop, calls=%fused_computation.12 | loop fusion | flops 1568768 | bytes 1064960 | tf_op jit(solution)/shard_map/reduce_sum | solution.py:79
  78.6 2.4 %fusion.48 = (f32[384]{0:T(512)S(1)}, f32[384,4096]{1,0:T(8,128)S(1)}) fusion(f32[4096]{0:T(1024)S(1)} %broadcast_multiply_fusion, bf16[128,384]{1,0:T(8,128)(2,1)S(1)} %fusion.29, bf16[4096,128]{1,0:T(8,128)(2,1)} %all-gather.2.cloned.1.call-done), kind=kOutput, calls=%fused_computation.89 | convolution fusion | flops 407371392 | bytes 7456256 | tf_op jit(solution)/shard_map/dot_general | solution.py:77
  80.9 1.0 fusion
  81.9 1.5 %fusion.43 = (f32[4096]{0:T(1024)S(1)}, bf16[384,4096]{1,0:T(8,128)(2,1)S(1)}) fusion(f32[384]{0:T(512)S(1)} %fusion, f32[384,4096]{1,0:T(8,128)S(1)} %get-tuple-element.24, f32[384]{0:T(512)S(1)} %get-tuple-element.23), kind=kLoop, calls=%fused_computation.85 | loop fusion | flops 6287360 | bytes 9456640 | tf_op jit(solution)/shard_map/reduce_sum | solution.py:92
  83.4 1.0 convolution_convert_fusion
  84.5 0.6 copy-done.1
  85.2 1.1 fusion.28
  86.3 3.5 %all-to-all-start.2 = ((bf16[4,1056,128]{2,1,0:T(8,128)(2,1)}), bf16[4,1056,128]{2,1,0:T(8,128)(2,1)S(1)}, u32[]{:S(2)}, u32[]{:S(2)}) async-start(bf16[4,1056,128]{2,1,0:T(8,128)(2,1)} %fusion.28), calls=%async_computation.2 | async-start | bytes 2162688 | tf_op jit(solution)/shard_map/all_to_all | solution.py:27
  89.9 14.7 %all-to-all-done.2 = bf16[4,1056,128]{2,1,0:T(8,128)(2,1)S(1)} async-done(((bf16[4,1056,128]{2,1,0:T(8,128)(2,1)}), bf16[4,1056,128]{2,1,0:T(8,128)(2,1)S(1)}, u32[]{:S(2)}, u32[]{:S(2)}) %all-to-all-start.2) | async-done | bytes 1081376 | tf_op jit(solution)/shard_map/all_to_all | solution.py:27
  104.9 0.1 slice_reduce_fusion
  105.1 0.9 maximum_maximum_fusion
  105.9 12.3 %all-to-all-start.3 = ((bf16[16,80,128]{2,1,0:T(8,128)(2,1)}), bf16[16,80,128]{2,1,0:T(8,128)(2,1)S(1)}, u32[]{:S(2)}, u32[]{:S(2)}) async-start(bf16[16,80,128]{2,1,0:T(8,128)(2,1)} %maximum_maximum_fusion), calls=%async_computation.3 | async-start | bytes 655360 | tf_op jit(solution)/shard_map/all_to_all | solution.py:27
  118.2 2.9 %fusion.25 = f32[384]{0:T(512)S(1)} fusion(bf16[4096,128]{1,0:T(8,128)(2,1)S(1)} %copy-done.2, bf16[384,4096]{1,0:T(8,128)(2,1)} %copy-done.1, bf16[128,384]{1,0:T(8,128)(2,1)S(1)} %fusion.29), kind=kOutput, calls=%fused_computation.24 | convolution fusion | flops 402849408 | bytes 4294144 | tf_op jit(solution)/shard_map/dot_general | solution.py:85
  121.2 0.6 div.53
  121.7 15.6 %all-to-all-done.3 = bf16[16,80,128]{2,1,0:T(8,128)(2,1)S(1)} async-done(((bf16[16,80,128]{2,1,0:T(8,128)(2,1)}), bf16[16,80,128]{2,1,0:T(8,128)(2,1)S(1)}, u32[]{:S(2)}, u32[]{:S(2)}) %all-to-all-start.3) | async-done | bytes 327712 | tf_op jit(solution)/shard_map/all_to_all | solution.py:27
  137.5 0.7 fusion.30
  (52 shorter events, 0.9 us)
Async XLA Ops:
  7.2 20.0 %copy-start = (bf16[384,1024]{1,0:T(8,128)(2,1)S(1)}, bf16[384,1024]{1,0:T(8,128)(2,1)}, u32[]{:S(2)}) copy-start(bf16[384,1024]{1,0:T(8,128)(2,1)} %param.3) | copy-start | bytes 2359300
  8.7 33.6 %all-to-all-start.1 = ((bf16[16,64,128]{2,1,0:T(8,128)(2,1)}), bf16[16,64,128]{2,1,0:T(8,128)(2,1)S(1)}, u32[]{:S(2)}, u32[]{:S(2)}) async-start(bf16[16,64,128]{2,1,0:T(8,128)(2,1)} %broadcast_in_dim.7), calls=%async_computation.1 | async-start | bytes 524288 | tf_op jit(solution)/shard_map/all_to_all | solution.py:27
  23.9 3.5 %copy-start.3 = (bf16[2048,1024]{1,0:T(8,128)(2,1)S(1)}, bf16[2048,1024]{1,0:T(8,128)(2,1)}, u32[]{:S(2)}) copy-start(bf16[2048,1024]{1,0:T(8,128)(2,1)} %param.4) | copy-start | bytes 12582916
  42.3 4.9 %copy-start.5 = (bf16[16,64,128]{2,1,0:T(8,128)(2,1)}, bf16[16,64,128]{2,1,0:T(8,128)(2,1)S(1)}, u32[]{:S(2)}) copy-start(bf16[16,64,128]{2,1,0:T(8,128)(2,1)S(1)} %all-to-all-done.1) | copy-start | bytes 786436
  42.3 16.9 %all-to-all-start = ((bf16[8,144,384]{2,1,0:T(8,128)(2,1)}), bf16[8,144,384]{2,1,0:T(8,128)(2,1)S(1)}, u32[]{:S(2)}, u32[]{:S(2)}) async-start(bf16[8,144,384]{2,1,0:T(8,128)(2,1)} %pad_maximum_fusion), calls=%async_computation | async-start | bytes 1769472 | tf_op jit(solution)/shard_map/all_to_all | solution.py:27
  47.1 29.7 %all-gather.2.cloned.1.call-start = ((), (), s32[]{:S(2)}) async-start(), calls=%async_computation.4 | async-start | bytes 1310720 | tf_op jit(solution)/shard_map/all_gather | solution.py:40
  59.5 58.7 %copy-start.4 = (bf16[128,384]{1,0:T(8,128)(2,1)}, bf16[128,384]{1,0:T(8,128)(2,1)S(1)}, u32[]{:S(2)}) copy-start(bf16[128,384]{1,0:T(8,128)(2,1)S(1)} %fusion.29) | copy-start | bytes 294916
  83.4 1.7 %copy-start.1 = (bf16[384,4096]{1,0:T(8,128)(2,1)}, bf16[384,4096]{1,0:T(8,128)(2,1)S(1)}, u32[]{:S(2)}) copy-start(bf16[384,4096]{1,0:T(8,128)(2,1)S(1)} %get-tuple-element.4) | copy-start | bytes 9437188
  85.2 33.0 %copy-start.2 = (bf16[4096,128]{1,0:T(8,128)(2,1)S(1)}, bf16[4096,128]{1,0:T(8,128)(2,1)}, u32[]{:S(2)}) copy-start(bf16[4096,128]{1,0:T(8,128)(2,1)} %all-gather.2.cloned.1.call-done) | copy-start | bytes 3145732
  86.3 18.3 %all-to-all-start.2 = ((bf16[4,1056,128]{2,1,0:T(8,128)(2,1)}), bf16[4,1056,128]{2,1,0:T(8,128)(2,1)S(1)}, u32[]{:S(2)}, u32[]{:S(2)}) async-start(bf16[4,1056,128]{2,1,0:T(8,128)(2,1)} %fusion.28), calls=%async_computation.2 | async-start | bytes 2162688 | tf_op jit(solution)/shard_map/all_to_all | solution.py:27
  105.1 32.5 %copy-start.6 = (bf16[1,64,128]{2,1,0:T(8,128)(2,1)S(1)}, bf16[1,64,128]{2,1,0:T(8,128)(2,1)}, u32[]{:S(2)}) copy-start(bf16[1,64,128]{2,1,0:T(8,128)(2,1)} %param.5) | copy-start | bytes 49156
  105.9 31.4 %all-to-all-start.3 = ((bf16[16,80,128]{2,1,0:T(8,128)(2,1)}), bf16[16,80,128]{2,1,0:T(8,128)(2,1)S(1)}, u32[]{:S(2)}, u32[]{:S(2)}) async-start(bf16[16,80,128]{2,1,0:T(8,128)(2,1)} %maximum_maximum_fusion), calls=%async_computation.3 | async-start | bytes 655360 | tf_op jit(solution)/shard_map/all_to_all | solution.py:27
Sparse Core Ops, SparseCore 0:
  50.0 26.6 all-gather.1

commit v2 on v1

--- a/solution.py
+++ b/solution.py
@@ -1,8 +1,11 @@
+import functools
 import math
 
 import jax
 import jax.numpy as jnp
 from jax import lax
+from jax.experimental import pallas as pl
+from jax.experimental.pallas import tpu as pltpu
 from jax.sharding import Mesh, PartitionSpec as P
 
 smoothing = 1.0
@@ -23,8 +26,116 @@
     return (wide[..., 2, :] + wide[..., 1, :]) + wide[..., 0, :]
 
 
+PACKED = 16
+
+
+def packed(largest, total):
+    return jnp.pad(jnp.concatenate([split(largest), split(total)]), ((0, PACKED - 6), (0, 0)))
+
+
+def unpacked(terms):
+    return join(terms[:3]), join(terms[3:6])
+
+
 def exchange(parts, axis):
     return lax.all_to_all(parts, axis, 0, 0, tiled=True)
+
+
+def wide_row(columns):
+    return jnp.transpose(jnp.broadcast_to(columns, (columns.shape[0], 128)))[:1]
+
+
+def coarse_kernel(core_ref, e_ref, c_ref, sent_ref, stats_ref, weights_ref, inverse_ref, logits_ref):
+    rows, width = e_ref.shape
+    chunks, _, chunk = logits_ref.shape
+    used = sent_ref.shape[0] - PACKED
+    scale = 2.0 / math.sqrt(width)
+
+    def score(j, peak):
+        block = c_ref[pl.ds(pl.multiple_of(j * chunk, chunk), chunk), :]
+        wide = block.astype(jnp.float32)
+        half_norm = wide_row(0.5 * jnp.sum(wide * wide, axis=1, keepdims=True))
+        products = lax.dot_general(
+            e_ref[...], block, (((1,), (1,)), ((), ())), preferred_element_type=jnp.float32
+        )
+        logits = (products - half_norm) * scale
+        logits_ref[j] = logits
+        for part in range(chunk // 128):
+            peak = jnp.maximum(peak, logits[:, part * 128 : part * 128 + 128])
+        return peak
+
+    peak = lax.fori_loop(0, chunks, score, jnp.full((rows, 128), -jnp.inf, jnp.float32), unroll=2)
+    peak = jnp.max(peak, axis=1, keepdims=True)
+
+    def raise_(j, total):
+        shifted = jnp.exp(logits_ref[j] - peak)
+        weights_ref[:, pl.ds(pl.multiple_of(j * chunk, chunk), chunk)] = shifted.astype(jnp.bfloat16)
+        for part in range(chunk // 128):
+            total = total + shifted[:, part * 128 : part * 128 + 128]
+        return total
+
+    total = lax.fori_loop(0, chunks, raise_, jnp.zeros((rows, 128), jnp.float32), unroll=2)
+    total = jnp.sum(total, axis=1, keepdims=True)
+    inverse_ref[...] = jnp.broadcast_to(1.0 / total, inverse_ref.shape)
+    pull(1 - core_ref[0], weights_ref, inverse_ref, c_ref, sent_ref)
+    stats = [wide_row(peak), wide_row(total)]
+    stats_ref[...] = jnp.concatenate(stats + [jnp.zeros((6, rows), jnp.float32)], axis=0)
+    terms = []
+    for value in stats:
+        for _ in range(3):
+            term = value.astype(jnp.bfloat16).astype(jnp.float32)
+            terms.append(term)
+            value = value - term
+    terms.append(jnp.zeros((PACKED - len(terms), rows), jnp.float32))
+    sent_ref[used:, :] = jnp.concatenate(terms, axis=0).astype(jnp.bfloat16)
+
+
+def pull(core, weights_ref, inverse_ref, c_ref, out_ref):
+    sub = inverse_ref.shape[1]
+    for pair in range(2):
+        columns = [pl.ds(pl.multiple_of(((2 * pair + k) * 2 + core) * sub, sub), sub) for k in range(2)]
+        block = jnp.concatenate([c_ref[:, column] for column in columns], axis=1)
+        pulled = jnp.dot(weights_ref[...], block, preferred_element_type=jnp.float32)
+        for k in range(2):
+            part = pulled[:, k * sub : k * sub + sub] * inverse_ref[...]
+            row = (2 * pair + k) * sub
+            out_ref[row : row + sub, :] = jnp.transpose(part).astype(out_ref.dtype)
+
+
+def kept_kernel(core_ref, weights_ref, inverse_ref, c_ref, kept_ref):
+    pull(core_ref[0], weights_ref, inverse_ref, c_ref, kept_ref)
+
+
+def coarse(embeddings, centroids, core):
+    rows, width = embeddings.shape
+    count = centroids.shape[0]
+    half, sub, chunk = width // 2, 128, 256
+    vmem, smem = pl.BlockSpec(memory_space=pltpu.VMEM), pl.BlockSpec(memory_space=pltpu.SMEM)
+    params = pltpu.CompilerParams(vmem_limit_bytes=32 * 2**20)
+    core = core.astype(jnp.int32).reshape(1)
+    sent, stats, weights, inverse = pl.pallas_call(
+        coarse_kernel,
+        out_shape=(
+            jax.ShapeDtypeStruct((half + PACKED, rows), jnp.bfloat16),
+            jax.ShapeDtypeStruct((8, rows), jnp.float32),
+            jax.ShapeDtypeStruct((rows, count), jnp.bfloat16),
+            jax.ShapeDtypeStruct((rows, sub), jnp.float32),
+        ),
+        in_specs=[smem, vmem, vmem],
+        out_specs=(vmem,) * 4,
+        scratch_shapes=[pltpu.VMEM((count // chunk, rows, chunk), jnp.float32)],
+        compiler_params=params,
+        cost_estimate=pl.CostEstimate(flops=1, bytes_accessed=1, transcendentals=0),
+    )(core, embeddings, centroids)
+    kept = pl.pallas_call(
+        kept_kernel,
+        out_shape=jax.ShapeDtypeStruct((half, rows), jnp.float32),
+        in_specs=[smem, vmem, vmem, vmem],
+        out_specs=vmem,
+        compiler_params=params,
+        cost_estimate=pl.CostEstimate(flops=1, bytes_accessed=1, transcendentals=0),
+    )(core, weights, inverse, centroids)
+    return kept.reshape(-1, sub, rows), sent, stats[0], stats[1]
 
 
 def local(embeddings, centroids, codebook):
@@ -37,38 +148,39 @@
 
     own = codebook.reshape(book_rows, sub_width)
     book = exchange(jnp.broadcast_to(own, (z_count, book_rows, sub_width)), "z")
-    book = lax.all_gather(book.reshape(words // y_count, sub_width), "y", axis=0, tiled=True)
-
-    products = lax.dot_general(
-        embeddings, centroids, (((1,), (1,)), ((), ())), preferred_element_type=jnp.float32
-    )
-    cent_wide = centroids.astype(jnp.float32)
-    half_norm = 0.5 * jnp.sum(cent_wide * cent_wide, axis=1)
-    logits = (products - half_norm[None, :]) * (2.0 / math.sqrt(model_width))
-    slab_max = jnp.max(logits, axis=1)
-    shifted = jnp.exp(logits - slab_max[:, None])
-    slab_total = jnp.sum(shifted, axis=1)
-    pulled = lax.dot_general(
-        centroids, shifted.astype(jnp.bfloat16), (((0,), (1,)), ((), ())), preferred_element_type=jnp.float32
-    )
-    pulled = (pulled / slab_total[None, :]).astype(jnp.bfloat16)
-
-    stats = jnp.concatenate([split(slab_max), split(slab_total)])
-    stats = jnp.pad(stats, ((0, 10), (0, 0)))
-    parts = jnp.concatenate(
-        [
-            pulled.reshape(cent_count, slice_width, rows_here),
-            jnp.broadcast_to(stats, (cent_count,) + stats.shape),
-        ],
-        axis=1,
-    )
-    parts = exchange(parts, CENT)
-    slab_maxes = join(parts[:, slice_width : slice_width + 3])
-    slab_totals = join(parts[:, slice_width + 3 : slice_width + 6])
-    row_max = jnp.max(slab_maxes, axis=0)
-    shares = jnp.exp(slab_maxes - row_max) * slab_totals
-    shares = shares / jnp.sum(shares, axis=0)
-    mean = jnp.sum(parts[:, :slice_width].astype(jnp.float32) * shares[:, None, :], axis=0)
+    book = book.reshape(words // y_count, sub_width)
+    core, column = lax.axis_index("c"), lax.axis_index("x")
+    kept, sent, slab_max, slab_total = coarse(embeddings, centroids, core)
+
+    got = lax.ppermute(sent, "c", [(0, 1), (1, 0)])
+    book, got, kept = lax.optimization_barrier((book, got, kept))
+    other_max, other_total = unpacked(got[-PACKED:])
+    chip_max = jnp.maximum(slab_max, other_max)
+    own_share = jnp.exp(slab_max - chip_max) * slab_total
+    other_share = jnp.exp(other_max - chip_max) * other_total
+    chip_total = own_share + other_share
+    chip_mean = kept * (own_share / chip_total) + got[:-PACKED].astype(jnp.float32).reshape(kept.shape) * (
+        other_share / chip_total
+    )
+    chip_stats = packed(chip_max, chip_total)
+    book = exchange(jnp.broadcast_to(book, (y_count,) + book.shape), "y").reshape(words, sub_width)
+    count = lax.axis_size("x")
+    means = [lax.dynamic_index_in_dim(chip_mean, column, 0, keepdims=False)]
+    maxes, totals = [chip_max], [chip_total]
+    for step in range(1, count):
+        target = lax.rem(column + step, count)
+        block = lax.dynamic_index_in_dim(chip_mean, target, 0, keepdims=False).astype(jnp.bfloat16)
+        block = jnp.concatenate([block, chip_stats], axis=0)
+        got = lax.ppermute(block, "x", [(i, (i + step) % count) for i in range(count)])
+        slab_max, slab_total = unpacked(got[-PACKED:])
+        means.append(got[:-PACKED].astype(jnp.float32))
+        maxes.append(slab_max)
+        totals.append(slab_total)
+    book, means, maxes, totals = lax.optimization_barrier((book, means, maxes, totals))
+    row_max = functools.reduce(jnp.maximum, maxes)
+    shares = [jnp.exp(largest - row_max) * total for largest, total in zip(maxes, totals)]
+    row_total = sum(shares)
+    mean = sum(part * (share / row_total) for part, share in zip(means, shares))
     own_cols = lax.dynamic_slice_in_dim(
         embeddings, lax.axis_index(CENT) * slice_width, slice_width, 1
     )

time: 146 us -> 126 us (0.86)
  waiting for transfers between devices: 68.5 us -> 43.8 us
  between operations: 14.3 us -> 1.05 us
  starting transfers between devices: 35.8 us -> 48.8 us
  Pallas kernels: 0 us -> 5.85 us
  local copies, waits for them, and re-layouts: 3.99 us -> 8.87 us
  matrix products: 10.1 us -> 5.58 us
  other arithmetic: 12.4 us -> 10.5 us
    all_gather x1 -> x0, waiting for transfers between devices: 17.2 us -> none  [local(): lax.all_gather(book.reshape(words // y_count, sub_width), 'y', axis=0, ti...]
    ppermute x0 -> x4, starting transfers between devices: none -> 11.7 us  [the longest x3 9.76 us: local(): lax.ppermute(block, 'x', [(i, (i + step) % count) for i in range(count)])]
    all_to_all x4, waiting for transfers between devices: 50.8 us -> 43.8 us  [exchange(): return lax.all_to_all(parts, axis, 0, 0, tiled=True)]
    pallas_call x0 -> x2, Pallas kernels: none -> 5.85 us  [the longest x1 4.59 us: coarse(): pl.pallas_call(coarse_kernel, out_shape=(jax.ShapeDtypeStruct((half + PAC...]
    reduce_sum x5 -> x0, other arithmetic: 5.47 us -> none  [the longest x1 3.22 us: local(): half_norm = 0.5 * jnp.sum(cent_wide * cent_wide, axis=1)]
    dot_general x2 -> x0, matrix products: 3.8 us -> none  [the longest x1 1.94 us: local(): lax.dot_general(embeddings, centroids, (((1,), (1,)), ((), ())), preferre...]
    unnamed x16 -> x14, local copies, waits for them, and re-layouts: 0.97 us -> 3.47 us
  transfers between devices with their start and end apart: 5 -> 8, of which waited for: 5 -> 4; matrix products, arithmetic and copies ran while one was open for 9% -> 4% of each run, Pallas kernels for 0% -> 5%
where the time goes in v2:
time: 126 us; the launch traced here: 125 us
  starting transfers between devices  48.8 us (39%)
  waiting for transfers between devices  43.8 us (35%)
  other arithmetic  10.5 us (8%)
  local copies, waits for them, and re-layouts  8.87 us (7%)
  Pallas kernels  5.85 us (5%)
  matrix products  5.58 us (4%)
    all_to_all x4, waiting for transfers between devices, exchange(): return lax.all_to_all(parts, axis, 0, 0, tiled=True)  43.8 us
    all_to_all x4, starting transfers between devices, exchange(): return lax.all_to_all(parts, axis, 0, 0, tiled=True)  37.2 us
    ppermute x3, starting transfers between devices, local(): lax.ppermute(block, 'x', [(i, (i + step) % count) for i in range(count)])  9.76 us
    pallas_call x1, Pallas kernels, coarse(): pl.pallas_call(coarse_kernel, out_shape=(jax.ShapeDtypeStruct((half + PAC...  4.59 us
    unnamed x14, local copies, waits for them, and re-layouts  3.47 us
  transfers between devices with their start and end apart: 8, of which 4 were waited for; matrix products, arithmetic and copies ran while one was open for 4% of the time, Pallas kernels for 5%

profile of v2, /device:TPU:6, one launch (start us, length us, event | category | flops | bytes accessed | tf_op | source)
XLA Modules:
  0.0 124.5 jit_solution(2435359060564436386)
XLA Ops:
  0.6 1.5 %broadcast_in_dim.6 = bf16[16,64,128]{2,1,0:T(8,128)(2,1)} broadcast(bf16[64,128]{1,0:T(8,128)(2,1)} %bitcast.49), dimensions={1,2} | broadcast | bytes 278528 | tf_op jit(solution)/shard_map/broadcast_in_dim | solution.py:150
  2.1 15.2 %all-to-all-start = ((bf16[16,64,128]{2,1,0:T(8,128)(2,1)}), bf16[16,64,128]{2,1,0:T(8,128)(2,1)S(1)}, u32[]{:S(2)}, u32[]{:S(2)}) async-start(bf16[16,64,128]{2,1,0:T(8,128)(2,1)} %broadcast_in_dim.6), calls=%async_computation | async-start | bytes 524288 | tf_op jit(solution)/shard_map/all_to_all | solution.py:41
  17.3 2.2 %copy-done = bf16[2048,1024]{1,0:T(8,128)(2,1)S(1)} copy-done((bf16[2048,1024]{1,0:T(8,128)(2,1)S(1)}, bf16[2048,1024]{1,0:T(8,128)(2,1)}, u32[]{:S(2)}) %copy-start) | copy-done | bytes 4194328
  19.5 1.1 copy-done.2
  20.6 4.6 %shard_map.58 = (bf16[528,384]{1,0:T(8,128)(2,1)S(1)}, f32[8,384]{1,0:T(8,128)S(1)}, bf16[384,2048]{1,0:T(8,128)(2,1)S(1)}, f32[384,128]{1,0:T(8,128)S(1)}) custom-call(s32[1]{0:T(128)} %bitcast.3.core_ref, bf16[384,1024]{1,0:T(8,128)(2,1)S(1)} %copy-done.2, bf16[2048,1024]{1,0:T(8,128)(2,1)S(1)} %copy-done), custom_call_target="tpu_custom_call" | custom-call | flops 1 | bytes 1 | tf_op jit(solution)/shard_map/pallas_call | solution.py:116
  25.2 1.9 %collective-permute-start = (bf16[528,384]{1,0:T(8,128)(2,1)S(1)}, bf16[528,384]{1,0:T(8,128)(2,1)S(1)}, u32[]{:S(2)}, u32[]{:S(2)}) collective-permute-start(bf16[528,384]{1,0:T(8,128)(2,1)S(1)} %get-tuple-element.23), channel_id=1, source_target_pairs={{0,1},{1,0},{2,3},{3,2},{4,5},{5,4},{6,7},{7,6},{8,9},{9,8},{10,11... | collective-permute-start | bytes 1216520 | tf_op jit(solution)/shard_map/ppermute | solution.py:155
  27.2 1.3 %shard_map.59 = f32[512,384]{1,0:T(8,128)S(1)} custom-call(s32[1]{0:T(128)} %bitcast.3.core_ref, bf16[384,2048]{1,0:T(8,128)(2,1)S(1)} %get-tuple-element.24.weights_ref, f32[384,128]{1,0:T(8,128)S(1)} %get-tuple-element.25.inverse_ref, bf16[2048,1024]{1,0:T(8,128)(2,1)S(1)} %copy-done.1), custom_call_target="tpu_custom_call" | custom-call | flops 1 | bytes 1 | tf_op jit(solution)/shard_map/pallas_call | solution.py:130
  28.4 0.9 constant_dynamic-slice_fusion
  29.5 6.1 %all-to-all-done = bf16[16,64,128]{2,1,0:T(8,128)(2,1)S(1)} async-done(((bf16[16,64,128]{2,1,0:T(8,128)(2,1)}), bf16[16,64,128]{2,1,0:T(8,128)(2,1)S(1)}, u32[]{:S(2)}, u32[]{:S(2)}) %all-to-all-start) | async-done | bytes 262176 | tf_op jit(solution)/shard_map/all_to_all | solution.py:41
  36.1 2.7 %collective-permute-start.3 = (bf16[144,384]{1,0:T(8,128)(2,1)S(1)}, bf16[144,384]{1,0:T(8,128)(2,1)S(1)}, u32[]{:S(2)}, u32[]{:S(2)}) collective-permute-start(bf16[144,384]{1,0:T(8,128)(2,1)S(1)} %get-tuple-element.79), channel_id=1, source_target_pairs={{0,6},{2,0},{4,2},{6,4},{1,7},{3,1},{5,3},{7,5},{8,14},{10,8},{12,... | collective-permute-start | bytes 331784 | tf_op jit(solution)/shard_map/ppermute | solution.py:174
  38.8 3.0 %collective-permute-start.2 = (bf16[144,384]{1,0:T(8,128)(2,1)S(1)}, bf16[144,384]{1,0:T(8,128)(2,1)S(1)}, u32[]{:S(2)}, u32[]{:S(2)}) collective-permute-start(bf16[144,384]{1,0:T(8,128)(2,1)S(1)} %get-tuple-element.81), channel_id=1, source_target_pairs={{0,4},{2,6},{4,0},{6,2},{1,5},{3,7},{5,1},{7,3},{8,12},{10,14},{12... | collective-permute-start | bytes 331784 | tf_op jit(solution)/shard_map/ppermute | solution.py:174
  41.8 4.0 %collective-permute-start.1 = (bf16[144,384]{1,0:T(8,128)(2,1)S(1)}, bf16[144,384]{1,0:T(8,128)(2,1)S(1)}, u32[]{:S(2)}, u32[]{:S(2)}) collective-permute-start(bf16[144,384]{1,0:T(8,128)(2,1)S(1)} %get-tuple-element.80), channel_id=1, source_target_pairs={{0,2},{2,4},{4,6},{6,0},{1,3},{3,5},{5,7},{7,1},{8,10},{10,12},{12... | collective-permute-start | bytes 331784 | tf_op jit(solution)/shard_map/ppermute | solution.py:174
  45.9 1.1 broadcast_in_dim.7
  47.0 4.5 %all-to-all-start.1 = ((bf16[4,1024,128]{2,1,0:T(8,128)(2,1)}), bf16[4,1024,128]{2,1,0:T(8,128)(2,1)S(1)}, u32[]{:S(2)}, u32[]{:S(2)}) async-start(bf16[4,1024,128]{2,1,0:T(8,128)(2,1)} %broadcast_in_dim.7), calls=%async_computation.1 | async-start | bytes 2097152 | tf_op jit(solution)/shard_map/all_to_all | solution.py:41
  51.8 10.6 %all-to-all-done.1 = bf16[4,1024,128]{2,1,0:T(8,128)(2,1)S(1)} async-done(((bf16[4,1024,128]{2,1,0:T(8,128)(2,1)}), bf16[4,1024,128]{2,1,0:T(8,128)(2,1)S(1)}, u32[]{:S(2)}, u32[]{:S(2)}) %all-to-all-start.1) | async-done | bytes 1048608 | tf_op jit(solution)/shard_map/all_to_all | solution.py:41
  62.3 0.6 multiply_reduce_fusion
  63.1 1.6 %fusion.42 = (f32[384]{0:T(512)S(1)}, f32[4096,384]{1,0:T(8,128)S(1)}) fusion(f32[4096]{0:T(1024)S(1)} %broadcast_multiply_fusion, bf16[4096,128]{1,0:T(8,128)(2,1)S(1)} %bitcast.43, bf16[128,384]{1,0:T(8,128)(2,1)S(1)} %fusion.10), kind=kOutput, calls=%fused_computation.126 | convolution fusion | flops 407371392 | bytes 7456256 | tf_op jit(solution)/shard_map/dot_general | solution.py:189
  64.7 1.0 fusion.1
  65.7 1.2 fusion.4
  66.9 2.0 %convolution_convert_fusion = bf16[4096,128]{1,0:T(8,128)(2,1)} fusion(bf16[4096,384]{1,0:T(8,128)(2,1)S(1)} %get-tuple-element.55, bf16[128,384]{1,0:T(8,128)(2,1)S(1)} %fusion.10), kind=kOutput, calls=%fused_computation.4 | convolution fusion | flops 403177472 | bytes 4292608 | tf_op jit(solution)/shard_map/dot_general | solution.py:201
  69.1 2.3 %fusion.7 = bf16[4,1056,128]{2,1,0:T(8,128)(2,1)} fusion(bf16[4,24,128]{2,1,0:T(8,128)(2,1)S(1)} %reshape.297, bf16[4,1024,128]{2,1,0:T(8,128)(2,1)} %bitcast.45), kind=kLoop, calls=%fused_computation.13 | loop fusion | flops 3244032 | bytes 2154496 | tf_op jit(solution)/shard_map/concatenate | solution.py:208
  71.4 4.3 %all-to-all-start.2 = ((bf16[4,1056,128]{2,1,0:T(8,128)(2,1)}), bf16[4,1056,128]{2,1,0:T(8,128)(2,1)}, u32[]{:S(2)}, u32[]{:S(2)}) async-start(bf16[4,1056,128]{2,1,0:T(8,128)(2,1)} %fusion.7), calls=%async_computation.2 | async-start | bytes 2162688 | tf_op jit(solution)/shard_map/all_to_all | solution.py:41
  75.7 11.0 %all-to-all-done.2 = bf16[4,1056,128]{2,1,0:T(8,128)(2,1)} async-done(((bf16[4,1056,128]{2,1,0:T(8,128)(2,1)}), bf16[4,1056,128]{2,1,0:T(8,128)(2,1)}, u32[]{:S(2)}, u32[]{:S(2)}) %all-to-all-start.2) | async-done | bytes 1081376 | tf_op jit(solution)/shard_map/all_to_all | solution.py:41
  86.8 0.7 slice_convert_fusion.3
  87.8 1.4 %slice_reduce_fusion = bf16[1024,128]{1,0:T(8,128)(2,1)S(1)} fusion(bf16[4,1056,128]{2,1,0:T(8,128)(2,1)} %all-to-all-done.2), kind=kLoop, calls=%fused_computation.14 | loop fusion | flops 393216 | bytes 1310720 | tf_op jit(solution)/shard_map/reduce_sum | solution.py:215
  89.2 0.9 maximum_maximum_fusion
  90.0 13.2 %all-to-all-start.3 = ((bf16[16,80,128]{2,1,0:T(8,128)(2,1)}), bf16[16,80,128]{2,1,0:T(8,128)(2,1)}, u32[]{:S(2)}, u32[]{:S(2)}) async-start(bf16[16,80,128]{2,1,0:T(8,128)(2,1)} %maximum_maximum_fusion), calls=%async_computation.3 | async-start | bytes 655360 | tf_op jit(solution)/shard_map/all_to_all | solution.py:41
  103.3 2.0 %fusion.6 = f32[384]{0:T(512)S(1)} fusion(bf16[4096,128]{1,0:T(8,128)(2,1)} %bitcast.44, bf16[4096,384]{1,0:T(8,128)(2,1)S(1)} %get-tuple-element.55, bf16[128,384]{1,0:T(8,128)(2,1)S(1)} %fusion.10), kind=kOutput, calls=%fused_computation.12 | convolution fusion | flops 402849408 | bytes 4294144 | tf_op jit(solution)/shard_map/dot_general | solution.py:197
  105.9 16.0 %all-to-all-done.3 = bf16[16,80,128]{2,1,0:T(8,128)(2,1)} async-done(((bf16[16,80,128]{2,1,0:T(8,128)(2,1)}), bf16[16,80,128]{2,1,0:T(8,128)(2,1)}, u32[]{:S(2)}, u32[]{:S(2)}) %all-to-all-start.3) | async-done | bytes 327712 | tf_op jit(solution)/shard_map/all_to_all | solution.py:41
  121.9 0.8 slice.247
  122.8 1.0 convert_reduce_fusion
  123.8 0.7 fusion.17
  (66 shorter events, 2.0 us)
Async XLA Ops:
  2.1 33.6 %all-to-all-start = ((bf16[16,64,128]{2,1,0:T(8,128)(2,1)}), bf16[16,64,128]{2,1,0:T(8,128)(2,1)S(1)}, u32[]{:S(2)}, u32[]{:S(2)}) async-start(bf16[16,64,128]{2,1,0:T(8,128)(2,1)} %broadcast_in_dim.6), calls=%async_computation | async-start | bytes 524288 | tf_op jit(solution)/shard_map/all_to_all | solution.py:41
  17.3 2.2 %copy-start = (bf16[2048,1024]{1,0:T(8,128)(2,1)S(1)}, bf16[2048,1024]{1,0:T(8,128)(2,1)}, u32[]{:S(2)}) copy-start(bf16[2048,1024]{1,0:T(8,128)(2,1)} %c_ref.3) | copy-start | bytes 12582916
  19.5 1.1 copy-start.2
  20.6 6.5 %copy-start.1 = (bf16[2048,1024]{1,0:T(8,128)(2,1)S(1)}, bf16[2048,1024]{1,0:T(8,128)(2,1)}, u32[]{:S(2)}) copy-start(bf16[2048,1024]{1,0:T(8,128)(2,1)} %c_ref.3) | copy-start | bytes 12582916
  25.2 4.3 %collective-permute-start = (bf16[528,384]{1,0:T(8,128)(2,1)S(1)}, bf16[528,384]{1,0:T(8,128)(2,1)S(1)}, u32[]{:S(2)}, u32[]{:S(2)}) collective-permute-start(bf16[528,384]{1,0:T(8,128)(2,1)S(1)} %get-tuple-element.23), channel_id=1, source_target_pairs={{0,1},{1,0},{2,3},{3,2},{4,5},{5,4},{6,7},{7,6},{8,9},{9,8},{10,11... | collective-permute-start | bytes 1216520 | tf_op jit(solution)/shard_map/ppermute | solution.py:155
  36.1 15.4 %collective-permute-start.3 = (bf16[144,384]{1,0:T(8,128)(2,1)S(1)}, bf16[144,384]{1,0:T(8,128)(2,1)S(1)}, u32[]{:S(2)}, u32[]{:S(2)}) collective-permute-start(bf16[144,384]{1,0:T(8,128)(2,1)S(1)} %get-tuple-element.79), channel_id=1, source_target_pairs={{0,6},{2,0},{4,2},{6,4},{1,7},{3,1},{5,3},{7,5},{8,14},{10,8},{12,... | collective-permute-start | bytes 331784 | tf_op jit(solution)/shard_map/ppermute | solution.py:174
  38.8 12.7 %collective-permute-start.2 = (bf16[144,384]{1,0:T(8,128)(2,1)S(1)}, bf16[144,384]{1,0:T(8,128)(2,1)S(1)}, u32[]{:S(2)}, u32[]{:S(2)}) collective-permute-start(bf16[144,384]{1,0:T(8,128)(2,1)S(1)} %get-tuple-element.81), channel_id=1, source_target_pairs={{0,4},{2,6},{4,0},{6,2},{1,5},{3,7},{5,1},{7,3},{8,12},{10,14},{12... | collective-permute-start | bytes 331784 | tf_op jit(solution)/shard_map/ppermute | solution.py:174
  41.8 9.7 %collective-permute-start.1 = (bf16[144,384]{1,0:T(8,128)(2,1)S(1)}, bf16[144,384]{1,0:T(8,128)(2,1)S(1)}, u32[]{:S(2)}, u32[]{:S(2)}) collective-permute-start(bf16[144,384]{1,0:T(8,128)(2,1)S(1)} %get-tuple-element.80), channel_id=1, source_target_pairs={{0,2},{2,4},{4,6},{6,0},{1,3},{3,5},{5,7},{7,1},{8,10},{10,12},{12... | collective-permute-start | bytes 331784 | tf_op jit(solution)/shard_map/ppermute | solution.py:174
  47.0 15.4 %all-to-all-start.1 = ((bf16[4,1024,128]{2,1,0:T(8,128)(2,1)}), bf16[4,1024,128]{2,1,0:T(8,128)(2,1)S(1)}, u32[]{:S(2)}, u32[]{:S(2)}) async-start(bf16[4,1024,128]{2,1,0:T(8,128)(2,1)} %broadcast_in_dim.7), calls=%async_computation.1 | async-start | bytes 2097152 | tf_op jit(solution)/shard_map/all_to_all | solution.py:41
  62.3 2.4 %copy-start.3 = (bf16[4,1024,128]{2,1,0:T(8,128)(2,1)}, bf16[4,1024,128]{2,1,0:T(8,128)(2,1)S(1)}, u32[]{:S(2)}) copy-start(bf16[4,1024,128]{2,1,0:T(8,128)(2,1)S(1)} %all-to-all-done.1) | copy-start | bytes 3145732
  63.1 40.2 %copy-start.4 = (bf16[128,384]{1,0:T(8,128)(2,1)}, bf16[128,384]{1,0:T(8,128)(2,1)S(1)}, u32[]{:S(2)}) copy-start(bf16[128,384]{1,0:T(8,128)(2,1)S(1)} %fusion.10) | copy-start | bytes 294916
  71.4 15.4 %all-to-all-start.2 = ((bf16[4,1056,128]{2,1,0:T(8,128)(2,1)}), bf16[4,1056,128]{2,1,0:T(8,128)(2,1)}, u32[]{:S(2)}, u32[]{:S(2)}) async-start(bf16[4,1056,128]{2,1,0:T(8,128)(2,1)} %fusion.7), calls=%async_computation.2 | async-start | bytes 2162688 | tf_op jit(solution)/shard_map/all_to_all | solution.py:41
  89.2 34.6 %copy-start.5 = (bf16[1,64,128]{2,1,0:T(8,128)(2,1)S(1)}, bf16[1,64,128]{2,1,0:T(8,128)(2,1)}, u32[]{:S(2)}) copy-start(bf16[1,64,128]{2,1,0:T(8,128)(2,1)} %param.5) | copy-start | bytes 49156
  90.0 31.8 %all-to-all-start.3 = ((bf16[16,80,128]{2,1,0:T(8,128)(2,1)}), bf16[16,80,128]{2,1,0:T(8,128)(2,1)}, u32[]{:S(2)}, u32[]{:S(2)}) async-start(bf16[16,80,128]{2,1,0:T(8,128)(2,1)} %maximum_maximum_fusion), calls=%async_computation.3 | async-start | bytes 655360 | tf_op jit(solution)/shard_map/all_to_all | solution.py:41

commit v3 on v2

v3 whole, which is shorter than its diff:
```python
import functools
import math

import jax
import jax.numpy as jnp
from jax import lax
from jax.experimental import pallas as pl
from jax.experimental.pallas import tpu as pltpu
from jax.sharding import Mesh, PartitionSpec as P

smoothing = 1.0
CENT = ("x", "c")


PACKED = 16


def exchange(parts, axis):
    return lax.all_to_all(parts, axis, 0, 0, tiled=True)


def wide_row(columns):
    return jnp.transpose(jnp.broadcast_to(columns, (columns.shape[0], 128)))[:1]


def coarse_kernel(place_ref, e_ref, c_ref, sent_ref, stats_ref, weights_ref, inverse_ref, logits_ref):
    rows, width = e_ref.shape
    chunks, _, chunk = logits_ref.shape
    used = sent_ref.shape[0] - PACKED
    scale = 2.0 / math.sqrt(width)

    def score(j, peak):
        block = c_ref[pl.ds(pl.multiple_of(j * chunk, chunk), chunk), :]
        wide = block.astype(jnp.float32)
        half_norm = wide_row(0.5 * jnp.sum(wide * wide, axis=1, keepdims=True))
        products = lax.dot_general(
            e_ref[...], block, (((1,), (1,)), ((), ())), preferred_element_type=jnp.float32
        )
        logits = (products - half_norm) * scale
        logits_ref[j] = logits
        for part in range(chunk // 128):
            peak = jnp.maximum(peak, logits[:, part * 128 : part * 128 + 128])
        return peak

    peak = lax.fori_loop(0, chunks, score, jnp.full((rows, 128), -jnp.inf, jnp.float32), unroll=2)
    peak = jnp.max(peak, axis=1, keepdims=True)

    def raise_(j, total):
        shifted = jnp.exp(logits_ref[j] - peak)
        weights_ref[:, pl.ds(pl.multiple_of(j * chunk, chunk), chunk)] = shifted.astype(jnp.bfloat16)
        for part in range(chunk // 128):
            total = total + shifted[:, part * 128 : part * 128 + 128]
        return total

    total = lax.fori_loop(0, chunks, raise_, jnp.zeros((rows, 128), jnp.float32), unroll=2)
    total = jnp.sum(total, axis=1, keepdims=True)
    inverse_ref[...] = jnp.broadcast_to(1.0 / total, inverse_ref.shape)
    pull(1 - place_ref[0], weights_ref, inverse_ref, c_ref, sent_ref)
    largest, total = wide_row(peak), wide_row(total)
    stats_ref[...] = jnp.concatenate([largest, total, jnp.zeros((6, rows), jnp.float32)], axis=0)
    sent_ref[used:, :] = packed(largest, total)


def pull(core, weights_ref, inverse_ref, c_ref, out_ref):
    sub = inverse_ref.shape[1]
    for pair in range(2):
        columns = [pl.ds(pl.multiple_of(((2 * pair + k) * 2 + core) * sub, sub), sub) for k in range(2)]
        block = jnp.concatenate([c_ref[:, column] for column in columns], axis=1)
        pulled = jnp.dot(weights_ref[...], block, preferred_element_type=jnp.float32)
        for k in range(2):
            part = pulled[:, k * sub : k * sub + sub] * inverse_ref[...]
            row = (2 * pair + k) * sub
            out_ref[row : row + sub, :] = jnp.transpose(part).astype(out_ref.dtype)


def kept_kernel(place_ref, weights_ref, inverse_ref, c_ref, e_ref, kept_ref, base_ref):
    pull(place_ref[0], weights_ref, inverse_ref, c_ref, kept_ref)
    sub = base_ref.shape[0]
    own = pl.multiple_of((2 * place_ref[1] + place_ref[0]) * sub, sub)
    base_ref[...] = jnp.transpose(e_ref[:, pl.ds(own, sub)].astype(jnp.float32))


def weigh(maxes, totals):
    largest = functools.reduce(jnp.maximum, maxes)
    shares = [jnp.exp(own - largest) * total for own, total in zip(maxes, totals)]
    whole = functools.reduce(jnp.add, shares)
    return [share / whole for share in shares], largest, whole


def terms_of(value, count=3):
    terms = []
    for _ in range(count):
        term = value.astype(jnp.bfloat16).astype(jnp.float32)
        terms.append(term)
        value = value - term
    return terms


def packed(largest, total):
    terms = terms_of(largest) + terms_of(total)
    terms.append(jnp.zeros((PACKED - len(terms), largest.shape[1]), jnp.float32))
    return jnp.concatenate(terms, axis=0).astype(jnp.bfloat16)


def unpacked(rows):
    wide = rows.astype(jnp.float32)
    return (wide[2:3] + wide[1:2]) + wide[0:1], (wide[5:6] + wide[4:5]) + wide[3:4]


def chip_kernel(place_ref, kept_ref, got_ref, stats_ref, mean_ref, chip_ref, *block_refs):
    sub, rows = mean_ref.shape
    count = len(block_refs) + 1
    used = count * sub
    other_max, other_total = unpacked(got_ref[used:, :])
    (own, other), largest, total = weigh(
        [stats_ref[0:1], other_max], [stats_ref[1:2], other_total]
    )
    chip_ref[...] = jnp.concatenate([largest, total, jnp.zeros((6, rows), jnp.float32)], axis=0)
    stats = packed(largest, total)
    for step in range(count):
        at = pl.ds(pl.multiple_of(lax.rem(place_ref[1] + step, count) * sub, sub), sub)
        mean = kept_ref[at, :] * own + got_ref[at, :].astype(jnp.float32) * other
        if step == 0:
            mean_ref[...] = mean
        else:
            block_refs[step - 1][:sub, :] = mean.astype(jnp.bfloat16)
            block_refs[step - 1][sub:, :] = stats


def quantize_kernel(mean_ref, chip_ref, *refs):
    *got_refs, base_ref, book_ref, residual_ref, sums_ref, raised_ref, inverse_ref, gaps_ref = refs
    sub, rows = mean_ref.shape
    parts, held, _ = sums_ref.shape
    words = book_ref.shape[0]
    quarter = words // parts
    scale = 2.0 / math.sqrt(sub)
    stats = [(chip_ref[0:1], chip_ref[1:2])] + [unpacked(got[sub:, :]) for got in got_refs]
    shares, _, _ = weigh(*zip(*stats))
    mean = mean_ref[...] * shares[0]
    for got, share in zip(got_refs, shares[1:]):
        mean = mean + got[:sub, :].astype(jnp.float32) * share
    residual = (base_ref[...] - mean).astype(jnp.bfloat16)
    residual_ref[...] = residual

    chunk = 512

    def score(j, peak):
        at = pl.ds(pl.multiple_of(j * chunk, chunk), chunk)
        block = book_ref[at, :]
        wide = block.astype(jnp.float32)
        half = 0.5 * jnp.sum(wide * wide, axis=1, keepdims=True)
        gap = jnp.dot(block, residual, preferred_element_type=jnp.float32) - half
        gaps_ref[at, :] = gap
        return jnp.maximum(peak, jnp.max(gap.reshape(chunk // 8, 8, rows), axis=0))

    peak = lax.fori_loop(0, words // chunk, score, jnp.full((8, rows), -jnp.inf, jnp.float32), unroll=2)
    peak = jnp.max(peak, axis=0, keepdims=True)

    def raise_(j, total):
        at = pl.ds(pl.multiple_of(j * chunk, chunk), chunk)
        raised = jnp.exp((gaps_ref[at, :] - peak) * scale)
        raised_ref[at, :] = raised.astype(jnp.bfloat16)
        return total + jnp.sum(raised.reshape(chunk // 8, 8, rows), axis=0)

    total = lax.fori_loop(0, words // chunk, raise_, jnp.zeros((8, rows), jnp.float32), unroll=2)
    inverse = 1.0 / jnp.sum(total, axis=0, keepdims=True)
    inverse_ref[...] = jnp.broadcast_to(inverse, inverse_ref.shape)

    scaled = residual.astype(jnp.float32) * inverse
    high, low = (jnp.broadcast_to(term, (sub // 2, rows)) for term in terms_of(inverse, 2))
    sides = jnp.transpose(jnp.concatenate([scaled, high, low], axis=0)).astype(jnp.bfloat16)
    row = lax.broadcasted_iota(jnp.int32, (128, 128), 0)
    diagonal = row == lax.broadcasted_iota(jnp.int32, (128, 128), 1)

    def add(j, _):
        at = pl.ds(pl.multiple_of(j * quarter, quarter), quarter)
        sums = jnp.dot(raised_ref[at, :], sides, preferred_element_type=jnp.float32)
        sums_ref[j, :quarter, :] = sums[:, :sub].astype(jnp.bfloat16)
        counts = sums[:, sub:]
        counts = counts + pltpu.roll(counts, sub // 2, 1)
        counts = jnp.concatenate(
            [
                jnp.sum(jnp.where(diagonal, counts[k * 128 : k * 128 + 128], 0.0), axis=0, keepdims=True)
                for k in range(quarter // 128)
            ],
            axis=0,
        )
        sums_ref[j, quarter:, :] = jnp.concatenate(terms_of(counts, 2), axis=0).astype(jnp.bfloat16)
        return 0

    lax.fori_loop(0, parts, add, 0)


def middle_kernel(sums_ref, out_ref):
    parts, held, sub = sums_ref.shape
    targets, rows, _ = out_ref.shape
    words = rows - 8
    quarter = targets * words
    counts = jnp.zeros((quarter // 128, 128), jnp.float32)
    for part in range(parts):
        pair = sums_ref[part, quarter:, :].astype(jnp.float32)
        counts = counts + (pair[: quarter // 128] + pair[quarter // 128 :])
    high, low = terms_of(counts, 2)
    left = lax.broadcasted_iota(jnp.int32, high.shape, 1) < 64
    even = jnp.where(left, high, pltpu.roll(low, 64, 1))
    odd = jnp.where(left, pltpu.roll(high, 64, 1), low)
    for target in range(targets):
        at = slice(target * words, target * words + words)
        total = sums_ref[0, at, :].astype(jnp.float32)
        for part in range(1, parts):
            total = total + sums_ref[part, at, :].astype(jnp.float32)
        row = (even if target % 2 == 0 else odd)[target // 2 : target // 2 + 1]
        row = jnp.concatenate([row, jnp.zeros((7, sub), jnp.float32)], axis=0)
        out_ref[target] = jnp.concatenate([total, row], axis=0).astype(jnp.bfloat16)


def last_kernel(sums_ref, own_ref, out_ref):
    parts = sums_ref.shape[0]
    words, sub = own_ref.shape
    total = sums_ref[0].astype(jnp.float32)
    for part in range(1, parts):
        total = total + sums_ref[part].astype(jnp.float32)
    pair = total[words : words + 1]
    counts = jnp.broadcast_to(pair + pltpu.roll(pair, 64, 1), (words, sub))
    diagonal = lax.broadcasted_iota(jnp.int32, (words, sub), 0) == lax.broadcasted_iota(jnp.int32, (words, sub), 1)
    counts = jnp.sum(jnp.where(diagonal, counts, 0.0), axis=1, keepdims=True)
    own = own_ref[...].astype(jnp.float32)
    out_ref[...] = (total[:words] + smoothing * own) / (counts + smoothing)


VMEM = pl.BlockSpec(memory_space=pltpu.VMEM)
SMEM = pl.BlockSpec(memory_space=pltpu.SMEM)


def call(kernel, out_shape, ins, *args, scratch=(), flops=1):
    return pl.pallas_call(
        kernel,
        out_shape=out_shape,
        in_specs=ins,
        out_specs=jax.tree.map(lambda _: VMEM, out_shape),
        scratch_shapes=scratch,
        compiler_params=pltpu.CompilerParams(vmem_limit_bytes=40 * 2**20),
        cost_estimate=pl.CostEstimate(flops=flops, bytes_accessed=1, transcendentals=0),
    )(*args)


def array(shape, dtype=jnp.float32):
    return jax.ShapeDtypeStruct(shape, dtype)


def coarse(embeddings, centroids, place):
    rows, width = embeddings.shape
    count = centroids.shape[0]
    half, sub, chunk = width // 2, 128, 256
    sent, stats, weights, inverse = call(
        coarse_kernel,
        (
            array((half + PACKED, rows), jnp.bfloat16),
            array((8, rows)),
            array((rows, count), jnp.bfloat16),
            array((rows, sub)),
        ),
        [SMEM, VMEM, VMEM],
        place,
        embeddings,
        centroids,
        scratch=[pltpu.VMEM((count // chunk, rows, chunk), jnp.float32)],
    )
    kept, base = call(
        kept_kernel,
        (array((half, rows)), array((sub, rows))),
        [SMEM] + [VMEM] * 4,
        place,
        weights,
        inverse,
        centroids,
        embeddings,
    )
    return kept, sent, stats, base


def chip(place, kept, got, stats):
    sub, rows, count = 128, stats.shape[1], 4
    blocks = [array((sub + PACKED, rows), jnp.bfloat16)] * (count - 1)
    return call(
        chip_kernel,
        [array((sub, rows)), array((8, rows))] + blocks,
        [SMEM] + [VMEM] * 3,
        place,
        kept,
        got,
        stats,
    )


def quantize(mean, stats, gots, base, book, parts):
    (sub, rows), words = mean.shape, book.shape[0]
    quarter = words // parts
    return call(
        quantize_kernel,
        (
            array((sub, rows), jnp.bfloat16),
            array((parts, quarter + quarter // 64, sub), jnp.bfloat16),
            array((words, rows), jnp.bfloat16),
            array((8, rows)),
        ),
        [VMEM] * (len(gots) + 4),
        mean,
        stats,
        *gots,
        base,
        book,
        scratch=[pltpu.VMEM((words, rows), jnp.float32)],
    )


def local(embeddings, centroids, codebook):
    _, book_rows, sub_width = codebook.shape
    y_count, z_count, x_count = lax.axis_size("y"), lax.axis_size("z"), lax.axis_size("x")
    words = book_rows * y_count * z_count
    place = jnp.stack([lax.axis_index("c"), lax.axis_index("x")]).astype(jnp.int32)

    own = codebook.reshape(book_rows, sub_width)
    book = exchange(jnp.broadcast_to(own, (z_count, book_rows, sub_width)), "z")
    book = book.reshape(words // y_count, sub_width)

    kept, sent, stats, base = coarse(embeddings, centroids, place)
    got = lax.ppermute(sent, "c", [(0, 1), (1, 0)])
    book, got, kept = lax.optimization_barrier((book, got, kept))
    mean, stats, *blocks = chip(place, kept, got, stats)
    gots = [
        lax.ppermute(block, "x", [(i, (i + step) % x_count) for i in range(x_count)])
        for step, block in enumerate(blocks, 1)
    ]
    book = exchange(jnp.broadcast_to(book, (y_count,) + book.shape), "y").reshape(words, sub_width)
    residual, sums, raised, inverse = quantize(mean, stats, gots, base, book, y_count)

    sums = exchange(sums, "y")
    rebuilt = lax.dot_general(
        book, raised, (((0,), (0,)), ((), ())), preferred_element_type=jnp.float32
    ) * inverse[:1]
    pq_error = jnp.mean(jnp.square(residual.astype(jnp.float32) - rebuilt), axis=0)
    sums, pq_error = lax.optimization_barrier((sums, pq_error))
    sums = call(
        middle_kernel, array((z_count, book_rows + 8, sub_width), jnp.bfloat16), [VMEM], sums
    )
    sums = exchange(sums, "z")
    new_codebook = call(last_kernel, array((book_rows, sub_width)), [VMEM] * 2, sums, own)
    return (residual, new_codebook[None], pq_error[None])


def solution(mesh):
    sizes = (4, 16, 4, 2)
    wide = Mesh(mesh.devices.reshape(sizes), ("y", "z", "x", "c"))
    rows = ("y", "z")
    placed = (P(rows, None), P(CENT, None), P(CENT, rows, None))
    return jax.shard_map(
        local,
        mesh=wide,
        in_specs=placed,
        out_specs=(P(CENT, rows), P(CENT, rows, None), P(CENT, rows)),
        check_vma=False,
    )
```

time: 126 us -> 111 us (0.88)
  other arithmetic: 10.5 us -> 0.08 us
  Pallas kernels: 5.85 us -> 15.9 us
  waiting for transfers between devices: 43.8 us -> 37.3 us
  starting transfers between devices: 48.8 us -> 44.4 us
  matrix products: 5.58 us -> 2.65 us
    all_to_all x4, waiting for transfers between devices: 43.8 us -> 31.3 us  [exchange(): return lax.all_to_all(parts, axis, 0, 0, tiled=True)]
    pallas_call x2 -> x6, Pallas kernels: 5.85 us -> 15.9 us  [call(): pl.pallas_call(kernel, out_shape=out_shape, in_specs=ins, out_specs=jax.t...]
    ppermute x3, waiting for transfers between devices: 0.01 us -> 5.92 us  [local(): lax.ppermute(block, 'x', [(i, (i + step) % x_count) for i in range(x_coun...]
    reduce_sum x6 -> x0, other arithmetic: 4.05 us -> none  [the longest x1 1.37 us: local(): sums = jnp.sum(sums[:, :quarter].astype(jnp.float32), axis=0)]
    all_to_all x4, starting transfers between devices: 37.2 us -> 33.8 us  [exchange(): return lax.all_to_all(parts, axis, 0, 0, tiled=True)]
    concatenate x3 -> x0, other arithmetic: 3.18 us -> none  [the longest x1 2.29 us: local(): jnp.concatenate([word_sums.astype(jnp.bfloat16).reshape(y_count, words //...]
    dot_general x3 -> x1, matrix products: 5.58 us -> 2.65 us  [local(): lax.dot_general(book, raised, (((0,), (0,)), ((), ())), preferred_element...]
    convert_element_type x15 -> x0, other arithmetic: 2.22 us -> none  [the longest x1 1.24 us: local(): pq_weights = pq_probs.astype(jnp.bfloat16)]
  transfers between devices with their start and end apart: 8 -> 8, of which waited for: 4 -> 5; matrix products, arithmetic and copies ran while one was open for 4% -> 3% of each run, Pallas kernels for 5% -> 7%
where the time goes in v3:
time: 111 us; the launch traced here: 109 us
  starting transfers between devices  44.4 us (40%)
  waiting for transfers between devices  37.3 us (34%)
  Pallas kernels  15.9 us (14%)
  local copies, waits for them, and re-layouts  8.13 us (7%)
  matrix products  2.65 us (2%)
    all_to_all x4, starting transfers between devices, exchange(): return lax.all_to_all(parts, axis, 0, 0, tiled=True)  33.8 us
    all_to_all x4, waiting for transfers between devices, exchange(): return lax.all_to_all(parts, axis, 0, 0, tiled=True)  31.3 us
    pallas_call x6, Pallas kernels, call(): pl.pallas_call(kernel, out_shape=out_shape, in_specs=ins, out_specs=jax.t...  15.9 us
    ppermute x3, starting transfers between devices, local(): lax.ppermute(block, 'x', [(i, (i + step) % x_count) for i in range(x_coun...  8.63 us
    ppermute x3, waiting for transfers between devices, local(): lax.ppermute(block, 'x', [(i, (i + step) % x_count) for i in range(x_coun...  5.92 us
    unnamed x8, local copies, waits for them, and re-layouts  4.95 us
    dot_general x1, matrix products, local(): lax.dot_general(book, raised, (((0,), (0,)), ((), ())), preferred_element...  2.65 us
  transfers between devices with their start and end apart: 8, of which 5 were waited for; matrix products, arithmetic and copies ran while one was open for 3% of the time, Pallas kernels for 7%

profile of v3, /device:TPU:6, one launch (start us, length us, event | category | flops | bytes accessed | tf_op | source)
XLA Modules:
  0.0 109.1 jit_solution(8370973561865355267)
XLA Ops:
  0.6 1.5 %broadcast_in_dim.12 = bf16[16,64,128]{2,1,0:T(8,128)(2,1)} broadcast(bf16[64,128]{1,0:T(8,128)(2,1)} %bitcast.10), dimensions={1,2} | broadcast | bytes 278528 | tf_op jit(solution)/shard_map/broadcast_in_dim | solution.py:324
  2.1 15.2 %all-to-all-start = ((bf16[16,64,128]{2,1,0:T(8,128)(2,1)}), bf16[16,64,128]{2,1,0:T(8,128)(2,1)S(1)}, u32[]{:S(2)}, u32[]{:S(2)}) async-start(bf16[16,64,128]{2,1,0:T(8,128)(2,1)} %broadcast_in_dim.12), calls=%async_computation | async-start | bytes 524288 | tf_op jit(solution)/shard_map/all_to_all | solution.py:19
  17.3 0.1 pad_add_fusion.place_ref
  17.4 0.0 copy-start
  17.4 2.2 %copy-done = bf16[2048,1024]{1,0:T(8,128)(2,1)S(1)} copy-done((bf16[2048,1024]{1,0:T(8,128)(2,1)S(1)}, bf16[2048,1024]{1,0:T(8,128)(2,1)}, u32[]{:S(2)}) %copy-start) | copy-done | bytes 4194328
  19.6 1.1 %copy-done.2 = bf16[384,1024]{1,0:T(8,128)(2,1)S(1)} copy-done((bf16[384,1024]{1,0:T(8,128)(2,1)S(1)}, bf16[384,1024]{1,0:T(8,128)(2,1)}, u32[]{:S(2)}) %copy-start.2) | copy-done | bytes 786456
  20.7 5.2 %shard_map.58 = (bf16[528,384]{1,0:T(8,128)(2,1)S(1)}, f32[8,384]{1,0:T(8,128)S(1)}, bf16[384,2048]{1,0:T(8,128)(2,1)S(1)}, f32[384,128]{1,0:T(8,128)S(1)}) custom-call(s32[2]{0:T(128)S(1)} %pad_add_fusion.place_ref, bf16[384,1024]{1,0:T(8,128)(2,1)S(1)} %copy-done.2, bf16[2048,1024]{1,0:T(8,128)(2,1)S(1)} %copy-done), custom_call_target="tpu_custom_call" | custom-call | flops 1 | bytes 1 | tf_op jit(solution)/shard_map/pallas_call | solution.py:236
  26.0 1.9 %collective-permute-start = (bf16[528,384]{1,0:T(8,128)(2,1)S(1)}, bf16[528,384]{1,0:T(8,128)(2,1)S(1)}, u32[]{:S(2)}, u32[]{:S(2)}) collective-permute-start(bf16[528,384]{1,0:T(8,128)(2,1)S(1)} %get-tuple-element.23), channel_id=1, source_target_pairs={{0,1},{1,0},{2,3},{3,2},{4,5},{5,4},{6,7},{7,6},{8,9},{9,8},{10,11... | collective-permute-start | bytes 1216520 | tf_op jit(solution)/shard_map/ppermute | solution.py:328
  27.9 1.8 %shard_map.59 = (f32[512,384]{1,0:T(8,128)S(1)}, f32[128,384]{1,0:T(8,128)S(1)}) custom-call(s32[2]{0:T(128)S(1)} %pad_add_fusion.place_ref, bf16[384,2048]{1,0:T(8,128)(2,1)S(1)} %get-tuple-element.24.weights_ref, f32[384,128]{1,0:T(8,128)S(1)} %get-tuple-element.25.inverse_ref, bf16[2048,1024]{1,0:T(8,128)(2,1)S(1)} %copy-done, bf16[384,1024]{1,0:T(8,128)(2,1)S(1)} %copy-done.2), custom_call_target="tpu_custom_call" | custom-call | flops 1 | bytes 1 | tf_op jit(solution)/shard_map/pallas_call | solution.py:236
  29.7 0.0 collective-permute-done.got_ref
  29.7 5.9 %all-to-all-done = bf16[16,64,128]{2,1,0:T(8,128)(2,1)S(1)} async-done(((bf16[16,64,128]{2,1,0:T(8,128)(2,1)}), bf16[16,64,128]{2,1,0:T(8,128)(2,1)S(1)}, u32[]{:S(2)}, u32[]{:S(2)}) %all-to-all-start) | async-done | bytes 262176 | tf_op jit(solution)/shard_map/all_to_all | solution.py:19
  35.7 1.1 %broadcast_in_dim.13 = bf16[4,1024,128]{2,1,0:T(8,128)(2,1)} broadcast(bf16[1024,128]{1,0:T(8,128)(2,1)S(1)} %bitcast.12), dimensions={1,2} | broadcast | bytes 1310720 | tf_op jit(solution)/shard_map/broadcast_in_dim | solution.py:335
  36.8 4.5 %all-to-all-start.1 = ((bf16[4,1024,128]{2,1,0:T(8,128)(2,1)}), bf16[4,1024,128]{2,1,0:T(8,128)(2,1)S(1)}, u32[]{:S(2)}, u32[]{:S(2)}) async-start(bf16[4,1024,128]{2,1,0:T(8,128)(2,1)} %broadcast_in_dim.13), calls=%async_computation.1 | async-start | bytes 2097152 | tf_op jit(solution)/shard_map/all_to_all | solution.py:19
  41.2 0.7 shard_map.60
  42.0 2.4 %collective-permute-start.1 = (bf16[144,384]{1,0:T(8,128)(2,1)S(1)}, bf16[144,384]{1,0:T(8,128)(2,1)S(1)}, u32[]{:S(2)}, u32[]{:S(2)}) collective-permute-start(bf16[144,384]{1,0:T(8,128)(2,1)S(1)} %get-tuple-element.32), channel_id=1, source_target_pairs={{0,2},{2,4},{4,6},{6,0},{1,3},{3,5},{5,7},{7,1},{8,10},{10,12},{12... | collective-permute-start | bytes 331784 | tf_op jit(solution)/shard_map/ppermute | solution.py:332
  44.4 4.3 %collective-permute-start.2 = (bf16[144,384]{1,0:T(8,128)(2,1)S(1)}, bf16[144,384]{1,0:T(8,128)(2,1)S(1)}, u32[]{:S(2)}, u32[]{:S(2)}) collective-permute-start(bf16[144,384]{1,0:T(8,128)(2,1)S(1)} %get-tuple-element.33), channel_id=1, source_target_pairs={{0,4},{2,6},{4,0},{6,2},{1,5},{3,7},{5,1},{7,3},{8,12},{10,14},{12... | collective-permute-start | bytes 331784 | tf_op jit(solution)/shard_map/ppermute | solution.py:332
  48.7 1.9 %collective-permute-start.3 = (bf16[144,384]{1,0:T(8,128)(2,1)S(1)}, bf16[144,384]{1,0:T(8,128)(2,1)S(1)}, u32[]{:S(2)}, u32[]{:S(2)}) collective-permute-start(bf16[144,384]{1,0:T(8,128)(2,1)S(1)} %get-tuple-element.34), channel_id=1, source_target_pairs={{0,6},{2,0},{4,2},{6,4},{1,7},{3,1},{5,3},{7,5},{8,14},{10,8},{12,... | collective-permute-start | bytes 331784 | tf_op jit(solution)/shard_map/ppermute | solution.py:332
  50.6 0.0 collective-permute-done.1.refs_0_
  50.6 1.9 %collective-permute-done.2.refs_1_ = bf16[144,384]{1,0:T(8,128)(2,1)S(1)} collective-permute-done((bf16[144,384]{1,0:T(8,128)(2,1)S(1)}, bf16[144,384]{1,0:T(8,128)(2,1)S(1)}, u32[]{:S(2)}, u32[]{:S(2)}) %collective-permute-start.2) | collective-permute-done | bytes 110624 | tf_op jit(solution)/shard_map/ppermute | solution.py:332
  52.5 4.0 %collective-permute-done.3.refs_2_ = bf16[144,384]{1,0:T(8,128)(2,1)S(1)} collective-permute-done((bf16[144,384]{1,0:T(8,128)(2,1)S(1)}, bf16[144,384]{1,0:T(8,128)(2,1)S(1)}, u32[]{:S(2)}, u32[]{:S(2)}) %collective-permute-start.3) | collective-permute-done | bytes 110624 | tf_op jit(solution)/shard_map/ppermute | solution.py:332
  56.5 0.0 all-to-all-done.1
  56.5 6.5 %shard_map.61 = (bf16[128,384]{1,0:T(8,128)(2,1)}, bf16[4,1040,128]{2,1,0:T(8,128)(2,1)}, bf16[4096,384]{1,0:T(8,128)(2,1)S(1)}, f32[8,384]{1,0:T(8,128)S(1)}) custom-call(f32[128,384]{1,0:T(8,128)S(1)} %get-tuple-element.30.mean_ref, f32[8,384]{1,0:T(8,128)S(1)} %get-tuple-element.31.chip_ref, bf16[144,384]{1,0:T(8,128)(2,1)S(1)} %collective-permute-done.1.refs_0_, ...), custom_call_target="tpu_custom_call" | custom-call | flops 1 | bytes 1 | tf_op jit(solution)/shard_map/pallas_call | solution.py:236
  63.0 1.6 %copy-done.1 = bf16[4096,384]{1,0:T(8,128)(2,1)} copy-done((bf16[4096,384]{1,0:T(8,128)(2,1)}, bf16[4096,384]{1,0:T(8,128)(2,1)S(1)}, u32[]{:S(2)}) %copy-start.1) | copy-done | bytes 3145752
  64.7 4.8 %all-to-all-start.2 = ((bf16[4,1040,128]{2,1,0:T(8,128)(2,1)}), bf16[4,1040,128]{2,1,0:T(8,128)(2,1)S(1)}, u32[]{:S(2)}, u32[]{:S(2)}) async-start(bf16[4,1040,128]{2,1,0:T(8,128)(2,1)} %get-tuple-element.38), calls=%async_computation.2 | async-start | bytes 2129920 | tf_op jit(solution)/shard_map/all_to_all | solution.py:19
  69.5 2.6 %multiply_reduce_fusion = f32[384]{0:T(512)S(1)} fusion(bf16[128,384]{1,0:T(8,128)(2,1)} %get-tuple-element.20, f32[384]{0:T(512)S(1)} %slice_reduce_fusion, bf16[4096,128]{1,0:T(8,128)(2,1)S(1)} %bitcast.9, bf16[4096,384]{1,0:T(8,128)(2,1)} %copy-done.1), kind=kOutput, calls=%fused_computation.1 | convolution fusion | flops 402898560 | bytes 4295680 | tf_op jit(solution)/shard_map/dot_general | solution.py:339
  72.1 8.3 %all-to-all-done.2.sums_ref = bf16[4,1040,128]{2,1,0:T(8,128)(2,1)S(1)} async-done(((bf16[4,1040,128]{2,1,0:T(8,128)(2,1)}), bf16[4,1040,128]{2,1,0:T(8,128)(2,1)S(1)}, u32[]{:S(2)}, u32[]{:S(2)}) %all-to-all-start.2) | async-done | bytes 1064992 | tf_op jit(solution)/shard_map/all_to_all | solution.py:19
  80.4 0.8 shard_map.62
  81.3 9.4 %all-to-all-start.3 = ((bf16[16,72,128]{2,1,0:T(8,128)(2,1)}), bf16[16,72,128]{2,1,0:T(8,128)(2,1)S(1)}, u32[]{:S(2)}, u32[]{:S(2)}) async-start(bf16[16,72,128]{2,1,0:T(8,128)(2,1)} %shard_map.62), calls=%async_computation.3 | async-start | bytes 589824 | tf_op jit(solution)/shard_map/all_to_all | solution.py:19
  90.7 0.6 broadcast_in_dim.15
  91.2 17.1 %all-to-all-done.3.sums_ref = bf16[16,72,128]{2,1,0:T(8,128)(2,1)S(1)} async-done(((bf16[16,72,128]{2,1,0:T(8,128)(2,1)}), bf16[16,72,128]{2,1,0:T(8,128)(2,1)S(1)}, u32[]{:S(2)}, u32[]{:S(2)}) %all-to-all-start.3) | async-done | bytes 294944 | tf_op jit(solution)/shard_map/all_to_all | solution.py:19
  108.3 0.0 copy-done.3
  108.3 0.8 shard_map.63
  (5 shorter events, 0.0 us)
Async XLA Ops:
  2.1 33.6 %all-to-all-start = ((bf16[16,64,128]{2,1,0:T(8,128)(2,1)}), bf16[16,64,128]{2,1,0:T(8,128)(2,1)S(1)}, u32[]{:S(2)}, u32[]{:S(2)}) async-start(bf16[16,64,128]{2,1,0:T(8,128)(2,1)} %broadcast_in_dim.12), calls=%async_computation | async-start | bytes 524288 | tf_op jit(solution)/shard_map/all_to_all | solution.py:19
  17.4 2.2 %copy-start = (bf16[2048,1024]{1,0:T(8,128)(2,1)S(1)}, bf16[2048,1024]{1,0:T(8,128)(2,1)}, u32[]{:S(2)}) copy-start(bf16[2048,1024]{1,0:T(8,128)(2,1)} %c_ref.3) | copy-start | bytes 12582916
  19.6 1.1 %copy-start.2 = (bf16[384,1024]{1,0:T(8,128)(2,1)S(1)}, bf16[384,1024]{1,0:T(8,128)(2,1)}, u32[]{:S(2)}) copy-start(bf16[384,1024]{1,0:T(8,128)(2,1)} %e_ref.3) | copy-start | bytes 2359300
  26.0 3.8 %collective-permute-start = (bf16[528,384]{1,0:T(8,128)(2,1)S(1)}, bf16[528,384]{1,0:T(8,128)(2,1)S(1)}, u32[]{:S(2)}, u32[]{:S(2)}) collective-permute-start(bf16[528,384]{1,0:T(8,128)(2,1)S(1)} %get-tuple-element.23), channel_id=1, source_target_pairs={{0,1},{1,0},{2,3},{3,2},{4,5},{5,4},{6,7},{7,6},{8,9},{9,8},{10,11... | collective-permute-start | bytes 1216520 | tf_op jit(solution)/shard_map/ppermute | solution.py:328
  36.8 19.8 %all-to-all-start.1 = ((bf16[4,1024,128]{2,1,0:T(8,128)(2,1)}), bf16[4,1024,128]{2,1,0:T(8,128)(2,1)S(1)}, u32[]{:S(2)}, u32[]{:S(2)}) async-start(bf16[4,1024,128]{2,1,0:T(8,128)(2,1)} %broadcast_in_dim.13), calls=%async_computation.1 | async-start | bytes 2097152 | tf_op jit(solution)/shard_map/all_to_all | solution.py:19
  42.0 8.7 %collective-permute-start.1 = (bf16[144,384]{1,0:T(8,128)(2,1)S(1)}, bf16[144,384]{1,0:T(8,128)(2,1)S(1)}, u32[]{:S(2)}, u32[]{:S(2)}) collective-permute-start(bf16[144,384]{1,0:T(8,128)(2,1)S(1)} %get-tuple-element.32), channel_id=1, source_target_pairs={{0,2},{2,4},{4,6},{6,0},{1,3},{3,5},{5,7},{7,1},{8,10},{10,12},{12... | collective-permute-start | bytes 331784 | tf_op jit(solution)/shard_map/ppermute | solution.py:332
  44.4 8.1 %collective-permute-start.2 = (bf16[144,384]{1,0:T(8,128)(2,1)S(1)}, bf16[144,384]{1,0:T(8,128)(2,1)S(1)}, u32[]{:S(2)}, u32[]{:S(2)}) collective-permute-start(bf16[144,384]{1,0:T(8,128)(2,1)S(1)} %get-tuple-element.33), channel_id=1, source_target_pairs={{0,4},{2,6},{4,0},{6,2},{1,5},{3,7},{5,1},{7,3},{8,12},{10,14},{12... | collective-permute-start | bytes 331784 | tf_op jit(solution)/shard_map/ppermute | solution.py:332
  48.7 7.9 %collective-permute-start.3 = (bf16[144,384]{1,0:T(8,128)(2,1)S(1)}, bf16[144,384]{1,0:T(8,128)(2,1)S(1)}, u32[]{:S(2)}, u32[]{:S(2)}) collective-permute-start(bf16[144,384]{1,0:T(8,128)(2,1)S(1)} %get-tuple-element.34), channel_id=1, source_target_pairs={{0,6},{2,0},{4,2},{6,4},{1,7},{3,1},{5,3},{7,5},{8,14},{10,8},{12,... | collective-permute-start | bytes 331784 | tf_op jit(solution)/shard_map/ppermute | solution.py:332
  63.0 1.6 %copy-start.1 = (bf16[4096,384]{1,0:T(8,128)(2,1)}, bf16[4096,384]{1,0:T(8,128)(2,1)S(1)}, u32[]{:S(2)}) copy-start(bf16[4096,384]{1,0:T(8,128)(2,1)S(1)} %get-tuple-element.39) | copy-start | bytes 9437188
  64.7 15.8 %all-to-all-start.2 = ((bf16[4,1040,128]{2,1,0:T(8,128)(2,1)}), bf16[4,1040,128]{2,1,0:T(8,128)(2,1)S(1)}, u32[]{:S(2)}, u32[]{:S(2)}) async-start(bf16[4,1040,128]{2,1,0:T(8,128)(2,1)} %get-tuple-element.38), calls=%async_computation.2 | async-start | bytes 2129920 | tf_op jit(solution)/shard_map/all_to_all | solution.py:19
  69.4 38.9 %copy-start.3 = (bf16[1,64,128]{2,1,0:T(8,128)(2,1)S(1)}, bf16[1,64,128]{2,1,0:T(8,128)(2,1)}, u32[]{:S(2)}) copy-start(bf16[1,64,128]{2,1,0:T(8,128)(2,1)} %param.5) | copy-start | bytes 49156
  81.3 27.1 %all-to-all-start.3 = ((bf16[16,72,128]{2,1,0:T(8,128)(2,1)}), bf16[16,72,128]{2,1,0:T(8,128)(2,1)S(1)}, u32[]{:S(2)}, u32[]{:S(2)}) async-start(bf16[16,72,128]{2,1,0:T(8,128)(2,1)} %shard_map.62), calls=%async_computation.3 | async-start | bytes 589824 | tf_op jit(solution)/shard_map/all_to_all | solution.py:19

commit v4 on v3

--- a/solution.py
+++ b/solution.py
@@ -128,7 +128,7 @@
 
 
 def quantize_kernel(mean_ref, chip_ref, *refs):
-    *got_refs, base_ref, book_ref, residual_ref, sums_ref, raised_ref, inverse_ref, gaps_ref = refs
+    *got_refs, base_ref, book_ref, residual_ref, sums_ref, raised_hbm, inverse_ref, gaps_ref, raised_ref, sems = refs
     sub, rows = mean_ref.shape
     parts, held, _ = sums_ref.shape
     words = book_ref.shape[0]
@@ -156,10 +156,15 @@
     peak = lax.fori_loop(0, words // chunk, score, jnp.full((8, rows), -jnp.inf, jnp.float32), unroll=2)
     peak = jnp.max(peak, axis=0, keepdims=True)
 
+    def store(j):
+        at = pl.ds(pl.multiple_of(j * chunk, chunk), chunk)
+        return pltpu.make_async_copy(raised_ref.at[at, :], raised_hbm.at[at, :], sems.at[j])
+
     def raise_(j, total):
         at = pl.ds(pl.multiple_of(j * chunk, chunk), chunk)
         raised = jnp.exp((gaps_ref[at, :] - peak) * scale)
         raised_ref[at, :] = raised.astype(jnp.bfloat16)
+        store(j).start()
         return total + jnp.sum(raised.reshape(chunk // 8, 8, rows), axis=0)
 
     total = lax.fori_loop(0, words // chunk, raise_, jnp.zeros((8, rows), jnp.float32), unroll=2)
@@ -189,6 +194,8 @@
         return 0
 
     lax.fori_loop(0, parts, add, 0)
+    for j in range(words // chunk):
+        store(j).wait()
 
 
 def middle_kernel(sums_ref, out_ref):
@@ -230,17 +237,18 @@
 
 VMEM = pl.BlockSpec(memory_space=pltpu.VMEM)
 SMEM = pl.BlockSpec(memory_space=pltpu.SMEM)
-
-
-def call(kernel, out_shape, ins, *args, scratch=(), flops=1):
+HBM = pl.BlockSpec(memory_space=pltpu.HBM)
+
+
+def call(kernel, out_shape, ins, *args, outs=None, scratch=(), mib=8):
     return pl.pallas_call(
         kernel,
         out_shape=out_shape,
         in_specs=ins,
-        out_specs=jax.tree.map(lambda _: VMEM, out_shape),
+        out_specs=outs or jax.tree.map(lambda _: VMEM, out_shape),
         scratch_shapes=scratch,
-        compiler_params=pltpu.CompilerParams(vmem_limit_bytes=40 * 2**20),
-        cost_estimate=pl.CostEstimate(flops=flops, bytes_accessed=1, transcendentals=0),
+        compiler_params=pltpu.CompilerParams(vmem_limit_bytes=mib * 2**20),
+        cost_estimate=pl.CostEstimate(flops=1, bytes_accessed=1, transcendentals=0),
     )(*args)
 
 
@@ -265,6 +273,7 @@
         embeddings,
         centroids,
         scratch=[pltpu.VMEM((count // chunk, rows, chunk), jnp.float32)],
+        mib=24,
     )
     kept, base = call(
         kept_kernel,
@@ -275,6 +284,7 @@
         inverse,
         centroids,
         embeddings,
+        mib=24,
     )
     return kept, sent, stats, base
 
@@ -310,7 +320,13 @@
         *gots,
         base,
         book,
-        scratch=[pltpu.VMEM((words, rows), jnp.float32)],
+        outs=(VMEM, VMEM, HBM, VMEM),
+        scratch=[
+            pltpu.VMEM((words, rows), jnp.float32),
+            pltpu.VMEM((words, rows), jnp.bfloat16),
+            pltpu.SemaphoreType.DMA((words // 512,)),
+        ],
+        mib=51,
     )
 
 
@@ -340,13 +356,13 @@
         book, raised, (((0,), (0,)), ((), ())), preferred_element_type=jnp.float32
     ) * inverse[:1]
     pq_error = jnp.mean(jnp.square(residual.astype(jnp.float32) - rebuilt), axis=0)
-    sums, pq_error = lax.optimization_barrier((sums, pq_error))
+    sums, pq_error = lax.optimization_barrier((sums, pq_error[None]))
     sums = call(
         middle_kernel, array((z_count, book_rows + 8, sub_width), jnp.bfloat16), [VMEM], sums
     )
     sums = exchange(sums, "z")
     new_codebook = call(last_kernel, array((book_rows, sub_width)), [VMEM] * 2, sums, own)
-    return (residual, new_codebook[None], pq_error[None])
+    return (residual, new_codebook[None], pq_error)
 
 
 def solution(mesh):

time: 111 us -> 108 us (0.973)
  blocking collectives: 0 us -> 26.9 us
  waiting for transfers between devices: 37.3 us -> 19.6 us
  starting transfers between devices: 44.4 us -> 35 us
  local copies, waits for them, and re-layouts: 8.13 us -> 6.49 us
    all_to_all x0 -> x1, blocking collectives: none -> 26.9 us  [exchange(): return lax.all_to_all(parts, axis, 0, 0, tiled=True)]
    all_to_all x4 -> x3, waiting for transfers between devices: 31.3 us -> 13.7 us  [exchange(): return lax.all_to_all(parts, axis, 0, 0, tiled=True)]
    all_to_all x4 -> x3, starting transfers between devices: 33.8 us -> 24.5 us  [exchange(): return lax.all_to_all(parts, axis, 0, 0, tiled=True)]
    unnamed x8 -> x6, local copies, waits for them, and re-layouts: 4.95 us -> 3.32 us
  transfers between devices with their start and end apart: 8 -> 7, of which waited for: 5 -> 4; matrix products, arithmetic and copies ran while one was open for 3% -> 3% of each run, Pallas kernels for 7% -> 7%
where the time goes in v4:
time: 108 us; the launch traced here: 107 us
  starting transfers between devices  35 us (32%)
  blocking collectives  26.9 us (25%)
  waiting for transfers between devices  19.6 us (18%)
  Pallas kernels  15.3 us (14%)
  local copies, waits for them, and re-layouts  6.49 us (6%)
  matrix products  2.65 us (2%)
    all_to_all x1, blocking collectives, exchange(): return lax.all_to_all(parts, axis, 0, 0, tiled=True)  26.9 us
    all_to_all x3, starting transfers between devices, exchange(): return lax.all_to_all(parts, axis, 0, 0, tiled=True)  24.5 us
    pallas_call x6, Pallas kernels, call(): pl.pallas_call(kernel, out_shape=out_shape, in_specs=ins, out_specs=outs...  15.3 us
    all_to_all x3, waiting for transfers between devices, exchange(): return lax.all_to_all(parts, axis, 0, 0, tiled=True)  13.7 us
    ppermute x3, starting transfers between devices, local(): lax.ppermute(block, 'x', [(i, (i + step) % x_count) for i in range(x_coun...  8.63 us
    ppermute x3, waiting for transfers between devices, local(): lax.ppermute(block, 'x', [(i, (i + step) % x_count) for i in range(x_coun...  5.92 us
    unnamed x6, local copies, waits for them, and re-layouts  3.32 us
    dot_general x1, matrix products, local(): lax.dot_general(book, raised, (((0,), (0,)), ((), ())), preferred_element...  2.65 us
  transfers between devices with their start and end apart: 7, of which 4 were waited for; matrix products, arithmetic and copies ran while one was open for 3% of the time, Pallas kernels for 7%

profile of v4, /device:TPU:6, one launch (start us, length us, event | category | flops | bytes accessed | tf_op | source)
XLA Modules:
  0.0 106.8 jit_solution(5043864877539856383)
XLA Ops:
  0.6 1.5 %broadcast_in_dim.10 = bf16[16,64,128]{2,1,0:T(8,128)(2,1)} broadcast(bf16[64,128]{1,0:T(8,128)(2,1)} %bitcast.10), dimensions={1,2} | broadcast | bytes 278528 | tf_op jit(solution)/shard_map/broadcast_in_dim | solution.py:340
  2.1 15.2 %all-to-all-start = ((bf16[16,64,128]{2,1,0:T(8,128)(2,1)}), bf16[16,64,128]{2,1,0:T(8,128)(2,1)S(1)}, u32[]{:S(2)}, u32[]{:S(2)}) async-start(bf16[16,64,128]{2,1,0:T(8,128)(2,1)} %broadcast_in_dim.10), calls=%async_computation | async-start | bytes 524288 | tf_op jit(solution)/shard_map/all_to_all | solution.py:19
  17.3 0.1 pad_add_fusion.place_ref
  17.4 0.0 copy-start
  17.4 2.2 %copy-done = bf16[2048,1024]{1,0:T(8,128)(2,1)S(1)} copy-done((bf16[2048,1024]{1,0:T(8,128)(2,1)S(1)}, bf16[2048,1024]{1,0:T(8,128)(2,1)}, u32[]{:S(2)}) %copy-start) | copy-done | bytes 4194328
  19.6 0.0 copy-start.1
  19.6 1.1 %copy-done.1 = bf16[384,1024]{1,0:T(8,128)(2,1)S(1)} copy-done((bf16[384,1024]{1,0:T(8,128)(2,1)S(1)}, bf16[384,1024]{1,0:T(8,128)(2,1)}, u32[]{:S(2)}) %copy-start.1) | copy-done | bytes 786456
  20.7 5.2 %shard_map.58 = (bf16[528,384]{1,0:T(8,128)(2,1)S(1)}, f32[8,384]{1,0:T(8,128)S(1)}, bf16[384,2048]{1,0:T(8,128)(2,1)S(1)}, f32[384,128]{1,0:T(8,128)S(1)}) custom-call(s32[2]{0:T(128)S(1)} %pad_add_fusion.place_ref, bf16[384,1024]{1,0:T(8,128)(2,1)S(1)} %copy-done.1, bf16[2048,1024]{1,0:T(8,128)(2,1)S(1)} %copy-done), custom_call_target="tpu_custom_call" | custom-call | flops 1 | bytes 1 | tf_op jit(solution)/shard_map/pallas_call | solution.py:244
  26.0 1.9 %collective-permute-start = (bf16[528,384]{1,0:T(8,128)(2,1)S(1)}, bf16[528,384]{1,0:T(8,128)(2,1)S(1)}, u32[]{:S(2)}, u32[]{:S(2)}) collective-permute-start(bf16[528,384]{1,0:T(8,128)(2,1)S(1)} %get-tuple-element.23), channel_id=1, source_target_pairs={{0,1},{1,0},{2,3},{3,2},{4,5},{5,4},{6,7},{7,6},{8,9},{9,8},{10,11... | collective-permute-start | bytes 1216520 | tf_op jit(solution)/shard_map/ppermute | solution.py:344
  27.9 1.8 %shard_map.59 = (f32[512,384]{1,0:T(8,128)S(1)}, f32[128,384]{1,0:T(8,128)S(1)}) custom-call(s32[2]{0:T(128)S(1)} %pad_add_fusion.place_ref, bf16[384,2048]{1,0:T(8,128)(2,1)S(1)} %get-tuple-element.24.weights_ref, f32[384,128]{1,0:T(8,128)S(1)} %get-tuple-element.25.inverse_ref, bf16[2048,1024]{1,0:T(8,128)(2,1)S(1)} %copy-done, bf16[384,1024]{1,0:T(8,128)(2,1)S(1)} %copy-done.1), custom_call_target="tpu_custom_call" | custom-call | flops 1 | bytes 1 | tf_op jit(solution)/shard_map/pallas_call | solution.py:244
  29.7 0.0 collective-permute-done.got_ref
  29.7 5.9 %all-to-all-done = bf16[16,64,128]{2,1,0:T(8,128)(2,1)S(1)} async-done(((bf16[16,64,128]{2,1,0:T(8,128)(2,1)}), bf16[16,64,128]{2,1,0:T(8,128)(2,1)S(1)}, u32[]{:S(2)}, u32[]{:S(2)}) %all-to-all-start) | async-done | bytes 262176 | tf_op jit(solution)/shard_map/all_to_all | solution.py:19
  35.7 1.1 %broadcast_in_dim.11 = bf16[4,1024,128]{2,1,0:T(8,128)(2,1)} broadcast(bf16[1024,128]{1,0:T(8,128)(2,1)S(1)} %bitcast.12), dimensions={1,2} | broadcast | bytes 1310720 | tf_op jit(solution)/shard_map/broadcast_in_dim | solution.py:351
  36.8 4.5 %all-to-all-start.1 = ((bf16[4,1024,128]{2,1,0:T(8,128)(2,1)}), bf16[4,1024,128]{2,1,0:T(8,128)(2,1)S(1)}, u32[]{:S(2)}, u32[]{:S(2)}) async-start(bf16[4,1024,128]{2,1,0:T(8,128)(2,1)} %broadcast_in_dim.11), calls=%async_computation.1 | async-start | bytes 2097152 | tf_op jit(solution)/shard_map/all_to_all | solution.py:19
  41.2 0.7 shard_map.60
  42.0 2.4 %collective-permute-start.1 = (bf16[144,384]{1,0:T(8,128)(2,1)S(1)}, bf16[144,384]{1,0:T(8,128)(2,1)S(1)}, u32[]{:S(2)}, u32[]{:S(2)}) collective-permute-start(bf16[144,384]{1,0:T(8,128)(2,1)S(1)} %get-tuple-element.32), channel_id=1, source_target_pairs={{0,2},{2,4},{4,6},{6,0},{1,3},{3,5},{5,7},{7,1},{8,10},{10,12},{12... | collective-permute-start | bytes 331784 | tf_op jit(solution)/shard_map/ppermute | solution.py:348
  44.3 4.3 %collective-permute-start.2 = (bf16[144,384]{1,0:T(8,128)(2,1)S(1)}, bf16[144,384]{1,0:T(8,128)(2,1)S(1)}, u32[]{:S(2)}, u32[]{:S(2)}) collective-permute-start(bf16[144,384]{1,0:T(8,128)(2,1)S(1)} %get-tuple-element.33), channel_id=1, source_target_pairs={{0,4},{2,6},{4,0},{6,2},{1,5},{3,7},{5,1},{7,3},{8,12},{10,14},{12... | collective-permute-start | bytes 331784 | tf_op jit(solution)/shard_map/ppermute | solution.py:348
  48.7 1.9 %collective-permute-start.3 = (bf16[144,384]{1,0:T(8,128)(2,1)S(1)}, bf16[144,384]{1,0:T(8,128)(2,1)S(1)}, u32[]{:S(2)}, u32[]{:S(2)}) collective-permute-start(bf16[144,384]{1,0:T(8,128)(2,1)S(1)} %get-tuple-element.34), channel_id=1, source_target_pairs={{0,6},{2,0},{4,2},{6,4},{1,7},{3,1},{5,3},{7,5},{8,14},{10,8},{12,... | collective-permute-start | bytes 331784 | tf_op jit(solution)/shard_map/ppermute | solution.py:348
  50.6 0.0 collective-permute-done.1.refs_0_
  50.6 1.9 %collective-permute-done.2.refs_1_ = bf16[144,384]{1,0:T(8,128)(2,1)S(1)} collective-permute-done((bf16[144,384]{1,0:T(8,128)(2,1)S(1)}, bf16[144,384]{1,0:T(8,128)(2,1)S(1)}, u32[]{:S(2)}, u32[]{:S(2)}) %collective-permute-start.2) | collective-permute-done | bytes 110624 | tf_op jit(solution)/shard_map/ppermute | solution.py:348
  52.5 4.0 %collective-permute-done.3.refs_2_ = bf16[144,384]{1,0:T(8,128)(2,1)S(1)} collective-permute-done((bf16[144,384]{1,0:T(8,128)(2,1)S(1)}, bf16[144,384]{1,0:T(8,128)(2,1)S(1)}, u32[]{:S(2)}, u32[]{:S(2)}) %collective-permute-start.3) | collective-permute-done | bytes 110624 | tf_op jit(solution)/shard_map/ppermute | solution.py:348
  56.5 0.0 all-to-all-done.1
  56.5 6.6 %shard_map.61 = (bf16[128,384]{1,0:T(8,128)(2,1)}, bf16[4,1040,128]{2,1,0:T(8,128)(2,1)}, bf16[4096,384]{1,0:T(8,128)(2,1)}, f32[8,384]{1,0:T(8,128)S(1)}) custom-call(f32[128,384]{1,0:T(8,128)S(1)} %get-tuple-element.30.mean_ref, f32[8,384]{1,0:T(8,128)S(1)} %get-tuple-element.31.chip_ref, bf16[144,384]{1,0:T(8,128)(2,1)S(1)} %collective-permute-done.1.refs_0_, ...), custom_call_target="tpu_custom_call" | custom-call | flops 1 | bytes 1 | tf_op jit(solution)/shard_map/pallas_call | solution.py:244
  63.1 4.8 %all-to-all-start.2 = ((bf16[4,1040,128]{2,1,0:T(8,128)(2,1)}), bf16[4,1040,128]{2,1,0:T(8,128)(2,1)S(1)}, u32[]{:S(2)}, u32[]{:S(2)}) async-start(bf16[4,1040,128]{2,1,0:T(8,128)(2,1)} %get-tuple-element.38), calls=%async_computation.2 | async-start | bytes 2129920 | tf_op jit(solution)/shard_map/all_to_all | solution.py:19
  67.9 0.0 copy-start.2
  68.0 2.6 %multiply_reduce_fusion = f32[384]{0:T(512)S(1)} fusion(bf16[128,384]{1,0:T(8,128)(2,1)} %get-tuple-element.20, f32[384]{0:T(512)S(1)} %slice_reduce_fusion, bf16[4096,128]{1,0:T(8,128)(2,1)S(1)} %bitcast.9, bf16[4096,384]{1,0:T(8,128)(2,1)} %get-tuple-element.39), kind=kOutput, calls=%fused_computation.1 | convolution fusion | flops 402898560 | bytes 4295680 | tf_op jit(solution)/shard_map/dot_general | solution.py:355
  70.6 0.6 div.10
  71.2 7.7 %all-to-all-done.2.sums_ref = bf16[4,1040,128]{2,1,0:T(8,128)(2,1)S(1)} async-done(((bf16[4,1040,128]{2,1,0:T(8,128)(2,1)}), bf16[4,1040,128]{2,1,0:T(8,128)(2,1)S(1)}, u32[]{:S(2)}, u32[]{:S(2)}) %all-to-all-start.2) | async-done | bytes 1064992 | tf_op jit(solution)/shard_map/all_to_all | solution.py:19
  78.9 0.1 shard_map.62
  79.1 26.9 %all_to_all.20.sums_ref = bf16[16,72,128]{2,1,0:T(8,128)(2,1)S(1)} all-to-all(bf16[16,72,128]{2,1,0:T(8,128)(2,1)S(1)} %shard_map.62), channel_id=1, replica_groups=mesh['y'=4,'z'=16,'x'=4,'c'=2] {'z'}, dimensions={0} | all-to-all | bytes 589824 | tf_op jit(solution)/shard_map/all_to_all | solution.py:19
  106.0 0.0 copy-done.2
  106.0 0.8 shard_map.63
  (2 shorter events, 0.0 us)
Async XLA Ops:
  2.1 33.6 %all-to-all-start = ((bf16[16,64,128]{2,1,0:T(8,128)(2,1)}), bf16[16,64,128]{2,1,0:T(8,128)(2,1)S(1)}, u32[]{:S(2)}, u32[]{:S(2)}) async-start(bf16[16,64,128]{2,1,0:T(8,128)(2,1)} %broadcast_in_dim.10), calls=%async_computation | async-start | bytes 524288 | tf_op jit(solution)/shard_map/all_to_all | solution.py:19
  17.4 2.2 %copy-start = (bf16[2048,1024]{1,0:T(8,128)(2,1)S(1)}, bf16[2048,1024]{1,0:T(8,128)(2,1)}, u32[]{:S(2)}) copy-start(bf16[2048,1024]{1,0:T(8,128)(2,1)} %c_ref.3) | copy-start | bytes 12582916
  19.6 1.1 %copy-start.1 = (bf16[384,1024]{1,0:T(8,128)(2,1)S(1)}, bf16[384,1024]{1,0:T(8,128)(2,1)}, u32[]{:S(2)}) copy-start(bf16[384,1024]{1,0:T(8,128)(2,1)} %e_ref.3) | copy-start | bytes 2359300
  26.0 3.8 %collective-permute-start = (bf16[528,384]{1,0:T(8,128)(2,1)S(1)}, bf16[528,384]{1,0:T(8,128)(2,1)S(1)}, u32[]{:S(2)}, u32[]{:S(2)}) collective-permute-start(bf16[528,384]{1,0:T(8,128)(2,1)S(1)} %get-tuple-element.23), channel_id=1, source_target_pairs={{0,1},{1,0},{2,3},{3,2},{4,5},{5,4},{6,7},{7,6},{8,9},{9,8},{10,11... | collective-permute-start | bytes 1216520 | tf_op jit(solution)/shard_map/ppermute | solution.py:344
  36.8 19.8 %all-to-all-start.1 = ((bf16[4,1024,128]{2,1,0:T(8,128)(2,1)}), bf16[4,1024,128]{2,1,0:T(8,128)(2,1)S(1)}, u32[]{:S(2)}, u32[]{:S(2)}) async-start(bf16[4,1024,128]{2,1,0:T(8,128)(2,1)} %broadcast_in_dim.11), calls=%async_computation.1 | async-start | bytes 2097152 | tf_op jit(solution)/shard_map/all_to_all | solution.py:19
  42.0 8.7 %collective-permute-start.1 = (bf16[144,384]{1,0:T(8,128)(2,1)S(1)}, bf16[144,384]{1,0:T(8,128)(2,1)S(1)}, u32[]{:S(2)}, u32[]{:S(2)}) collective-permute-start(bf16[144,384]{1,0:T(8,128)(2,1)S(1)} %get-tuple-element.32), channel_id=1, source_target_pairs={{0,2},{2,4},{4,6},{6,0},{1,3},{3,5},{5,7},{7,1},{8,10},{10,12},{12... | collective-permute-start | bytes 331784 | tf_op jit(solution)/shard_map/ppermute | solution.py:348
  44.3 8.1 %collective-permute-start.2 = (bf16[144,384]{1,0:T(8,128)(2,1)S(1)}, bf16[144,384]{1,0:T(8,128)(2,1)S(1)}, u32[]{:S(2)}, u32[]{:S(2)}) collective-permute-start(bf16[144,384]{1,0:T(8,128)(2,1)S(1)} %get-tuple-element.33), channel_id=1, source_target_pairs={{0,4},{2,6},{4,0},{6,2},{1,5},{3,7},{5,1},{7,3},{8,12},{10,14},{12... | collective-permute-start | bytes 331784 | tf_op jit(solution)/shard_map/ppermute | solution.py:348
  48.7 7.9 %collective-permute-start.3 = (bf16[144,384]{1,0:T(8,128)(2,1)S(1)}, bf16[144,384]{1,0:T(8,128)(2,1)S(1)}, u32[]{:S(2)}, u32[]{:S(2)}) collective-permute-start(bf16[144,384]{1,0:T(8,128)(2,1)S(1)} %get-tuple-element.34), channel_id=1, source_target_pairs={{0,6},{2,0},{4,2},{6,4},{1,7},{3,1},{5,3},{7,5},{8,14},{10,8},{12,... | collective-permute-start | bytes 331784 | tf_op jit(solution)/shard_map/ppermute | solution.py:348
  63.1 15.8 %all-to-all-start.2 = ((bf16[4,1040,128]{2,1,0:T(8,128)(2,1)}), bf16[4,1040,128]{2,1,0:T(8,128)(2,1)S(1)}, u32[]{:S(2)}, u32[]{:S(2)}) async-start(bf16[4,1040,128]{2,1,0:T(8,128)(2,1)} %get-tuple-element.38), calls=%async_computation.2 | async-start | bytes 2129920 | tf_op jit(solution)/shard_map/all_to_all | solution.py:19
  67.9 38.0 %copy-start.2 = (bf16[1,64,128]{2,1,0:T(8,128)(2,1)S(1)}, bf16[1,64,128]{2,1,0:T(8,128)(2,1)}, u32[]{:S(2)}) copy-start(bf16[1,64,128]{2,1,0:T(8,128)(2,1)} %param.5) | copy-start | bytes 49156

commit v5 on v4

--- a/solution.py
+++ b/solution.py
@@ -342,12 +342,15 @@
 
     kept, sent, stats, base = coarse(embeddings, centroids, place)
     got = lax.ppermute(sent, "c", [(0, 1), (1, 0)])
-    book, got, kept = lax.optimization_barrier((book, got, kept))
     mean, stats, *blocks = chip(place, kept, got, stats)
-    gots = [
-        lax.ppermute(block, "x", [(i, (i + step) % x_count) for i in range(x_count)])
-        for step, block in enumerate(blocks, 1)
-    ]
+
+    def along(step):
+        ring = [(i, (i + step) % x_count) for i in range(x_count)]
+        return lax.ppermute(blocks[step - 1], "x", ring)
+
+    gots = {2: along(2)}
+    book, gots[2], blocks[0], blocks[2] = lax.optimization_barrier((book, gots[2], blocks[0], blocks[2]))
+    gots = [along(1), gots[2], along(3)]
     book = exchange(jnp.broadcast_to(book, (y_count,) + book.shape), "y").reshape(words, sub_width)
     residual, sums, raised, inverse = quantize(mean, stats, gots, base, book, y_count)
 

time: 108 us -> 116 us (1.074)
  waiting for transfers between devices: 19.6 us -> 25.6 us
  blocking collectives: 26.9 us -> 29.5 us
    ppermute x3, waiting for transfers between devices: 5.92 us -> 9.93 us  [along(): return lax.ppermute(blocks[step - 1], 'x', ring)]
    all_to_all x1, blocking collectives: 26.9 us -> 29.5 us  [exchange(): return lax.all_to_all(parts, axis, 0, 0, tiled=True)]
    all_to_all x3, waiting for transfers between devices: 13.7 us -> 15.6 us  [exchange(): return lax.all_to_all(parts, axis, 0, 0, tiled=True)]
    all_to_all x3, starting transfers between devices: 24.5 us -> 23.2 us  [exchange(): return lax.all_to_all(parts, axis, 0, 0, tiled=True)]
  transfers between devices with their start and end apart: 7 -> 7, of which waited for: 4 -> 5; matrix products, arithmetic and copies ran while one was open for 3% -> 3% of each run, Pallas kernels for 7% -> 7%
where the time goes in v5:
time: 116 us; the launch traced here: 115 us
  starting transfers between devices  34.3 us (30%)
  blocking collectives  29.5 us (25%)
  waiting for transfers between devices  25.6 us (22%)
  Pallas kernels  15.3 us (13%)
  local copies, waits for them, and re-layouts  6.49 us (6%)
  matrix products  2.67 us (2%)
    all_to_all x1, blocking collectives, exchange(): return lax.all_to_all(parts, axis, 0, 0, tiled=True)  29.5 us
    all_to_all x3, starting transfers between devices, exchange(): return lax.all_to_all(parts, axis, 0, 0, tiled=True)  23.2 us
    all_to_all x3, waiting for transfers between devices, exchange(): return lax.all_to_all(parts, axis, 0, 0, tiled=True)  15.6 us
    pallas_call x6, Pallas kernels, call(): pl.pallas_call(kernel, out_shape=out_shape, in_specs=ins, out_specs=outs...  15.3 us
    ppermute x3, waiting for transfers between devices, along(): return lax.ppermute(blocks[step - 1], 'x', ring)  9.93 us
    ppermute x3, starting transfers between devices, along(): return lax.ppermute(blocks[step - 1], 'x', ring)  9.15 us
    unnamed x6, local copies, waits for them, and re-layouts  3.33 us
    dot_general x1, matrix products, local(): lax.dot_general(book, raised, (((0,), (0,)), ((), ())), preferred_element...  2.67 us
  transfers between devices with their start and end apart: 7, of which 5 were waited for; matrix products, arithmetic and copies ran while one was open for 3% of the time, Pallas kernels for 7%

profile of v5, /device:TPU:6, one launch (start us, length us, event | category | flops | bytes accessed | tf_op | source)
XLA Modules:
  0.0 114.6 jit_solution(14813033165360653609)
XLA Ops:
  0.6 1.5 %broadcast_in_dim.10 = bf16[16,64,128]{2,1,0:T(8,128)(2,1)} broadcast(bf16[64,128]{1,0:T(8,128)(2,1)} %bitcast.10), dimensions={1,2} | broadcast | bytes 278528 | tf_op jit(solution)/shard_map/broadcast_in_dim | solution.py:340
  2.1 15.2 %all-to-all-start = ((bf16[16,64,128]{2,1,0:T(8,128)(2,1)}), bf16[16,64,128]{2,1,0:T(8,128)(2,1)S(1)}, u32[]{:S(2)}, u32[]{:S(2)}) async-start(bf16[16,64,128]{2,1,0:T(8,128)(2,1)} %broadcast_in_dim.10), calls=%async_computation | async-start | bytes 524288 | tf_op jit(solution)/shard_map/all_to_all | solution.py:19
  17.3 0.1 pad_add_fusion.place_ref
  17.4 0.0 copy-start
  17.4 2.2 %copy-done = bf16[2048,1024]{1,0:T(8,128)(2,1)S(1)} copy-done((bf16[2048,1024]{1,0:T(8,128)(2,1)S(1)}, bf16[2048,1024]{1,0:T(8,128)(2,1)}, u32[]{:S(2)}) %copy-start) | copy-done | bytes 4194328
  19.6 0.0 copy-start.1
  19.6 1.1 copy-done.1
  20.7 5.2 %shard_map.58 = (bf16[528,384]{1,0:T(8,128)(2,1)S(1)}, f32[8,384]{1,0:T(8,128)S(1)}, bf16[384,2048]{1,0:T(8,128)(2,1)S(1)}, f32[384,128]{1,0:T(8,128)S(1)}) custom-call(s32[2]{0:T(128)S(1)} %pad_add_fusion.place_ref, bf16[384,1024]{1,0:T(8,128)(2,1)S(1)} %copy-done.1, bf16[2048,1024]{1,0:T(8,128)(2,1)S(1)} %copy-done), custom_call_target="tpu_custom_call" | custom-call | flops 1 | bytes 1 | tf_op jit(solution)/shard_map/pallas_call | solution.py:244
  26.0 1.9 %collective-permute-start = (bf16[528,384]{1,0:T(8,128)(2,1)S(1)}, bf16[528,384]{1,0:T(8,128)(2,1)S(1)}, u32[]{:S(2)}, u32[]{:S(2)}) collective-permute-start(bf16[528,384]{1,0:T(8,128)(2,1)S(1)} %get-tuple-element.27), channel_id=1, source_target_pairs={{0,1},{1,0},{2,3},{3,2},{4,5},{5,4},{6,7},{7,6},{8,9},{9,8},{10,11... | collective-permute-start | bytes 1216520 | tf_op jit(solution)/shard_map/ppermute | solution.py:344
  27.9 1.8 %shard_map.59 = (f32[512,384]{1,0:T(8,128)S(1)}, f32[128,384]{1,0:T(8,128)S(1)}) custom-call(s32[2]{0:T(128)S(1)} %pad_add_fusion.place_ref, bf16[384,2048]{1,0:T(8,128)(2,1)S(1)} %get-tuple-element.24.weights_ref, f32[384,128]{1,0:T(8,128)S(1)} %get-tuple-element.25.inverse_ref, bf16[2048,1024]{1,0:T(8,128)(2,1)S(1)} %copy-done, bf16[384,1024]{1,0:T(8,128)(2,1)S(1)} %copy-done.1), custom_call_target="tpu_custom_call" | custom-call | flops 1 | bytes 1 | tf_op jit(solution)/shard_map/pallas_call | solution.py:244
  29.7 0.0 collective-permute-done.got_ref
  29.7 0.7 shard_map.60
  30.4 3.3 %collective-permute-start.1 = (bf16[144,384]{1,0:T(8,128)(2,1)S(1)}, bf16[144,384]{1,0:T(8,128)(2,1)S(1)}, u32[]{:S(2)}, u32[]{:S(2)}) collective-permute-start(bf16[144,384]{1,0:T(8,128)(2,1)S(1)} %get-tuple-element.31), channel_id=1, source_target_pairs={{0,4},{2,6},{4,0},{6,2},{1,5},{3,7},{5,1},{7,3},{8,12},{10,14},{12... | collective-permute-start | bytes 331784 | tf_op jit(solution)/shard_map/ppermute | solution.py:349
  33.8 5.5 %collective-permute-done.1.refs_1_ = bf16[144,384]{1,0:T(8,128)(2,1)S(1)} collective-permute-done((bf16[144,384]{1,0:T(8,128)(2,1)S(1)}, bf16[144,384]{1,0:T(8,128)(2,1)S(1)}, u32[]{:S(2)}, u32[]{:S(2)}) %collective-permute-start.1) | collective-permute-done | bytes 110624 | tf_op jit(solution)/shard_map/ppermute | solution.py:349
  39.3 0.0 all-to-all-done
  39.3 1.1 broadcast_in_dim.11
  40.4 4.5 %all-to-all-start.1 = ((bf16[4,1024,128]{2,1,0:T(8,128)(2,1)}), bf16[4,1024,128]{2,1,0:T(8,128)(2,1)S(1)}, u32[]{:S(2)}, u32[]{:S(2)}) async-start(bf16[4,1024,128]{2,1,0:T(8,128)(2,1)} %broadcast_in_dim.11), calls=%async_computation.1 | async-start | bytes 2097152 | tf_op jit(solution)/shard_map/all_to_all | solution.py:19
  44.9 2.4 %collective-permute-start.2 = (bf16[144,384]{1,0:T(8,128)(2,1)S(1)}, bf16[144,384]{1,0:T(8,128)(2,1)S(1)}, u32[]{:S(2)}, u32[]{:S(2)}) collective-permute-start(bf16[144,384]{1,0:T(8,128)(2,1)S(1)} %get-tuple-element.34), channel_id=1, source_target_pairs={{0,2},{2,4},{4,6},{6,0},{1,3},{3,5},{5,7},{7,1},{8,10},{10,12},{12... | collective-permute-start | bytes 331784 | tf_op jit(solution)/shard_map/ppermute | solution.py:349
  47.3 3.4 %collective-permute-start.3 = (bf16[144,384]{1,0:T(8,128)(2,1)S(1)}, bf16[144,384]{1,0:T(8,128)(2,1)S(1)}, u32[]{:S(2)}, u32[]{:S(2)}) collective-permute-start(bf16[144,384]{1,0:T(8,128)(2,1)S(1)} %get-tuple-element.36), channel_id=1, source_target_pairs={{0,6},{2,0},{4,2},{6,4},{1,7},{3,1},{5,3},{7,5},{8,14},{10,8},{12,... | collective-permute-start | bytes 331784 | tf_op jit(solution)/shard_map/ppermute | solution.py:349
  50.7 0.8 collective-permute-done.2.refs_0_
  51.5 3.6 %collective-permute-done.3.refs_2_ = bf16[144,384]{1,0:T(8,128)(2,1)S(1)} collective-permute-done((bf16[144,384]{1,0:T(8,128)(2,1)S(1)}, bf16[144,384]{1,0:T(8,128)(2,1)S(1)}, u32[]{:S(2)}, u32[]{:S(2)}) %collective-permute-start.3) | collective-permute-done | bytes 110624 | tf_op jit(solution)/shard_map/ppermute | solution.py:349
  55.1 4.7 %all-to-all-done.1 = bf16[4,1024,128]{2,1,0:T(8,128)(2,1)S(1)} async-done(((bf16[4,1024,128]{2,1,0:T(8,128)(2,1)}), bf16[4,1024,128]{2,1,0:T(8,128)(2,1)S(1)}, u32[]{:S(2)}, u32[]{:S(2)}) %all-to-all-start.1) | async-done | bytes 1048608 | tf_op jit(solution)/shard_map/all_to_all | solution.py:19
  59.9 6.6 %shard_map.61 = (bf16[128,384]{1,0:T(8,128)(2,1)}, bf16[4,1040,128]{2,1,0:T(8,128)(2,1)}, bf16[4096,384]{1,0:T(8,128)(2,1)}, f32[8,384]{1,0:T(8,128)S(1)}) custom-call(f32[128,384]{1,0:T(8,128)S(1)} %get-tuple-element.29.mean_ref, f32[8,384]{1,0:T(8,128)S(1)} %get-tuple-element.30.chip_ref, bf16[144,384]{1,0:T(8,128)(2,1)S(1)} %collective-permute-done.2.refs_0_, ...), custom_call_target="tpu_custom_call" | custom-call | flops 1 | bytes 1 | tf_op jit(solution)/shard_map/pallas_call | solution.py:244
  66.4 3.5 %all-to-all-start.2 = ((bf16[4,1040,128]{2,1,0:T(8,128)(2,1)}), bf16[4,1040,128]{2,1,0:T(8,128)(2,1)S(1)}, u32[]{:S(2)}, u32[]{:S(2)}) async-start(bf16[4,1040,128]{2,1,0:T(8,128)(2,1)} %get-tuple-element.40), calls=%async_computation.2 | async-start | bytes 2129920 | tf_op jit(solution)/shard_map/all_to_all | solution.py:19
  70.0 0.0 copy-start.2
  70.0 2.7 %multiply_reduce_fusion = f32[384]{0:T(512)S(1)} fusion(bf16[128,384]{1,0:T(8,128)(2,1)} %get-tuple-element.21, f32[384]{0:T(512)S(1)} %slice_reduce_fusion, bf16[4096,128]{1,0:T(8,128)(2,1)S(1)} %bitcast.9, bf16[4096,384]{1,0:T(8,128)(2,1)} %get-tuple-element.41), kind=kOutput, calls=%fused_computation.1 | convolution fusion | flops 402898560 | bytes 4295680 | tf_op jit(solution)/shard_map/dot_general | solution.py:358
  72.7 0.6 div.10
  73.3 10.9 %all-to-all-done.2.sums_ref = bf16[4,1040,128]{2,1,0:T(8,128)(2,1)S(1)} async-done(((bf16[4,1040,128]{2,1,0:T(8,128)(2,1)}), bf16[4,1040,128]{2,1,0:T(8,128)(2,1)S(1)}, u32[]{:S(2)}, u32[]{:S(2)}) %all-to-all-start.2) | async-done | bytes 1064992 | tf_op jit(solution)/shard_map/all_to_all | solution.py:19
  84.2 0.1 shard_map.62
  84.3 29.5 %all_to_all.20.sums_ref = bf16[16,72,128]{2,1,0:T(8,128)(2,1)S(1)} all-to-all(bf16[16,72,128]{2,1,0:T(8,128)(2,1)S(1)} %shard_map.62), channel_id=1, replica_groups=mesh['y'=4,'z'=16,'x'=4,'c'=2] {'z'}, dimensions={0} | all-to-all | bytes 589824 | tf_op jit(solution)/shard_map/all_to_all | solution.py:19
  113.8 0.0 copy-done.2
  113.8 0.8 shard_map.63
  (2 shorter events, 0.0 us)
Async XLA Ops:
  2.1 37.2 %all-to-all-start = ((bf16[16,64,128]{2,1,0:T(8,128)(2,1)}), bf16[16,64,128]{2,1,0:T(8,128)(2,1)S(1)}, u32[]{:S(2)}, u32[]{:S(2)}) async-start(bf16[16,64,128]{2,1,0:T(8,128)(2,1)} %broadcast_in_dim.10), calls=%async_computation | async-start | bytes 524288 | tf_op jit(solution)/shard_map/all_to_all | solution.py:19
  17.4 2.2 %copy-start = (bf16[2048,1024]{1,0:T(8,128)(2,1)S(1)}, bf16[2048,1024]{1,0:T(8,128)(2,1)}, u32[]{:S(2)}) copy-start(bf16[2048,1024]{1,0:T(8,128)(2,1)} %c_ref.3) | copy-start | bytes 12582916
  19.6 1.1 copy-start.1
  26.0 3.8 %collective-permute-start = (bf16[528,384]{1,0:T(8,128)(2,1)S(1)}, bf16[528,384]{1,0:T(8,128)(2,1)S(1)}, u32[]{:S(2)}, u32[]{:S(2)}) collective-permute-start(bf16[528,384]{1,0:T(8,128)(2,1)S(1)} %get-tuple-element.27), channel_id=1, source_target_pairs={{0,1},{1,0},{2,3},{3,2},{4,5},{5,4},{6,7},{7,6},{8,9},{9,8},{10,11... | collective-permute-start | bytes 1216520 | tf_op jit(solution)/shard_map/ppermute | solution.py:344
  30.4 8.9 %collective-permute-start.1 = (bf16[144,384]{1,0:T(8,128)(2,1)S(1)}, bf16[144,384]{1,0:T(8,128)(2,1)S(1)}, u32[]{:S(2)}, u32[]{:S(2)}) collective-permute-start(bf16[144,384]{1,0:T(8,128)(2,1)S(1)} %get-tuple-element.31), channel_id=1, source_target_pairs={{0,4},{2,6},{4,0},{6,2},{1,5},{3,7},{5,1},{7,3},{8,12},{10,14},{12... | collective-permute-start | bytes 331784 | tf_op jit(solution)/shard_map/ppermute | solution.py:349
  40.4 19.4 %all-to-all-start.1 = ((bf16[4,1024,128]{2,1,0:T(8,128)(2,1)}), bf16[4,1024,128]{2,1,0:T(8,128)(2,1)S(1)}, u32[]{:S(2)}, u32[]{:S(2)}) async-start(bf16[4,1024,128]{2,1,0:T(8,128)(2,1)} %broadcast_in_dim.11), calls=%async_computation.1 | async-start | bytes 2097152 | tf_op jit(solution)/shard_map/all_to_all | solution.py:19
  44.9 6.6 %collective-permute-start.2 = (bf16[144,384]{1,0:T(8,128)(2,1)S(1)}, bf16[144,384]{1,0:T(8,128)(2,1)S(1)}, u32[]{:S(2)}, u32[]{:S(2)}) collective-permute-start(bf16[144,384]{1,0:T(8,128)(2,1)S(1)} %get-tuple-element.34), channel_id=1, source_target_pairs={{0,2},{2,4},{4,6},{6,0},{1,3},{3,5},{5,7},{7,1},{8,10},{10,12},{12... | collective-permute-start | bytes 331784 | tf_op jit(solution)/shard_map/ppermute | solution.py:349
  47.3 7.9 %collective-permute-start.3 = (bf16[144,384]{1,0:T(8,128)(2,1)S(1)}, bf16[144,384]{1,0:T(8,128)(2,1)S(1)}, u32[]{:S(2)}, u32[]{:S(2)}) collective-permute-start(bf16[144,384]{1,0:T(8,128)(2,1)S(1)} %get-tuple-element.36), channel_id=1, source_target_pairs={{0,6},{2,0},{4,2},{6,4},{1,7},{3,1},{5,3},{7,5},{8,14},{10,8},{12,... | collective-permute-start | bytes 331784 | tf_op jit(solution)/shard_map/ppermute | solution.py:349
  66.4 17.7 %all-to-all-start.2 = ((bf16[4,1040,128]{2,1,0:T(8,128)(2,1)}), bf16[4,1040,128]{2,1,0:T(8,128)(2,1)S(1)}, u32[]{:S(2)}, u32[]{:S(2)}) async-start(bf16[4,1040,128]{2,1,0:T(8,128)(2,1)} %get-tuple-element.40), calls=%async_computation.2 | async-start | bytes 2129920 | tf_op jit(solution)/shard_map/all_to_all | solution.py:19
  70.0 43.8 %copy-start.2 = (bf16[1,64,128]{2,1,0:T(8,128)(2,1)S(1)}, bf16[1,64,128]{2,1,0:T(8,128)(2,1)}, u32[]{:S(2)}) copy-start(bf16[1,64,128]{2,1,0:T(8,128)(2,1)} %param.5) | copy-start | bytes 49156

commit v6 on v3

--- a/solution.py
+++ b/solution.py
@@ -127,13 +127,9 @@
             block_refs[step - 1][sub:, :] = stats
 
 
-def quantize_kernel(mean_ref, chip_ref, *refs):
-    *got_refs, base_ref, book_ref, residual_ref, sums_ref, raised_ref, inverse_ref, gaps_ref = refs
-    sub, rows = mean_ref.shape
-    parts, held, _ = sums_ref.shape
-    words = book_ref.shape[0]
-    quarter = words // parts
-    scale = 2.0 / math.sqrt(sub)
+def residual_kernel(mean_ref, chip_ref, *refs):
+    *got_refs, base_ref, residual_ref, copies_ref = refs
+    sub = mean_ref.shape[0]
     stats = [(chip_ref[0:1], chip_ref[1:2])] + [unpacked(got[sub:, :]) for got in got_refs]
     shares, _, _ = weigh(*zip(*stats))
     mean = mean_ref[...] * shares[0]
@@ -141,77 +137,89 @@
         mean = mean + got[:sub, :].astype(jnp.float32) * share
     residual = (base_ref[...] - mean).astype(jnp.bfloat16)
     residual_ref[...] = residual
-
-    chunk = 512
-
-    def score(j, peak):
-        at = pl.ds(pl.multiple_of(j * chunk, chunk), chunk)
-        block = book_ref[at, :]
-        wide = block.astype(jnp.float32)
+    for copy in range(copies_ref.shape[0]):
+        copies_ref[copy] = residual
+
+
+def score_kernel(book_ref, rows_ref, raised_ref, stats_ref, gaps_ref, half_ref):
+    parts, sub, rows = rows_ref.shape
+    words = book_ref.shape[0]
+    scale = 2.0 / math.sqrt(sub)
+    chunk = 256
+    spans = [slice(at, at + chunk) for at in range(0, words, chunk)]
+    for at in spans:
+        wide = book_ref[at, :].astype(jnp.float32)
         half = 0.5 * jnp.sum(wide * wide, axis=1, keepdims=True)
-        gap = jnp.dot(block, residual, preferred_element_type=jnp.float32) - half
-        gaps_ref[at, :] = gap
-        return jnp.maximum(peak, jnp.max(gap.reshape(chunk // 8, 8, rows), axis=0))
-
-    peak = lax.fori_loop(0, words // chunk, score, jnp.full((8, rows), -jnp.inf, jnp.float32), unroll=2)
-    peak = jnp.max(peak, axis=0, keepdims=True)
-
-    def raise_(j, total):
-        at = pl.ds(pl.multiple_of(j * chunk, chunk), chunk)
-        raised = jnp.exp((gaps_ref[at, :] - peak) * scale)
-        raised_ref[at, :] = raised.astype(jnp.bfloat16)
-        return total + jnp.sum(raised.reshape(chunk // 8, 8, rows), axis=0)
-
-    total = lax.fori_loop(0, words // chunk, raise_, jnp.zeros((8, rows), jnp.float32), unroll=2)
-    inverse = 1.0 / jnp.sum(total, axis=0, keepdims=True)
-    inverse_ref[...] = jnp.broadcast_to(inverse, inverse_ref.shape)
-
-    scaled = residual.astype(jnp.float32) * inverse
-    high, low = (jnp.broadcast_to(term, (sub // 2, rows)) for term in terms_of(inverse, 2))
-    sides = jnp.transpose(jnp.concatenate([scaled, high, low], axis=0)).astype(jnp.bfloat16)
+        half_ref[at, :] = jnp.broadcast_to(half, (chunk, 128))
+    packs = []
+    for part in range(parts):
+        peak = jnp.full((8, rows), -jnp.inf, jnp.float32)
+        for at in spans:
+            gap = jnp.dot(book_ref[at, :], rows_ref[part], preferred_element_type=jnp.float32)
+            gap = gap - jnp.concatenate([half_ref[at, :]] * (rows // 128), axis=1)
+            gaps_ref[part, at, :] = gap
+            peak = jnp.maximum(peak, jnp.max(gap.reshape(chunk // 8, 8, rows), axis=0))
+        peak = jnp.max(peak, axis=0, keepdims=True)
+        total = jnp.zeros((8, rows), jnp.float32)
+        for at in spans:
+            raised = jnp.exp((gaps_ref[part, at, :] - peak) * scale)
+            raised_ref[at, part * rows : part * rows + rows] = raised.astype(jnp.bfloat16)
+            total = total + jnp.sum(raised.reshape(chunk // 8, 8, rows), axis=0)
+        packs.append(packed(peak, jnp.sum(total, axis=0, keepdims=True)))
+    pack = jnp.concatenate(packs, axis=0)
+    for copy in range(stats_ref.shape[0]):
+        stats_ref[copy] = pack
+
+
+def sum_kernel(place_ref, stats_ref, rows_ref, raised_ref, sums_ref, factors_ref, sides_ref):
+    parts, sub, rows = rows_ref.shape
+    targets, held, _ = sums_ref.shape
+    owned = held - 8
+    scale = 2.0 / math.sqrt(sub)
+    for part in range(parts):
+        at = slice(part * PACKED, part * PACKED + PACKED)
+        stats = [unpacked(stats_ref[peer, at, :]) for peer in range(parts)]
+        peak = functools.reduce(jnp.maximum, [own for own, _ in stats])
+        whole = functools.reduce(jnp.add, [jnp.exp((own - peak) * scale) * total for own, total in stats])
+        own, _ = unpacked(stats_ref[place_ref[2], at, :])
+        factor = jnp.exp((own - peak) * scale) / whole
+        factors_ref[:, part * rows : part * rows + rows] = jnp.broadcast_to(factor, (8, rows))
+        scaled = rows_ref[part].astype(jnp.float32) * factor
+        high, low = (jnp.broadcast_to(term, (sub // 2, rows)) for term in terms_of(factor, 2))
+        sides = jnp.transpose(jnp.concatenate([scaled, high, low], axis=0))
+        sides_ref[part * rows : part * rows + rows, :] = sides.astype(jnp.bfloat16)
     row = lax.broadcasted_iota(jnp.int32, (128, 128), 0)
     diagonal = row == lax.broadcasted_iota(jnp.int32, (128, 128), 1)
-
-    def add(j, _):
-        at = pl.ds(pl.multiple_of(j * quarter, quarter), quarter)
-        sums = jnp.dot(raised_ref[at, :], sides, preferred_element_type=jnp.float32)
-        sums_ref[j, :quarter, :] = sums[:, :sub].astype(jnp.bfloat16)
-        counts = sums[:, sub:]
-        counts = counts + pltpu.roll(counts, sub // 2, 1)
-        counts = jnp.concatenate(
-            [
-                jnp.sum(jnp.where(diagonal, counts[k * 128 : k * 128 + 128], 0.0), axis=0, keepdims=True)
-                for k in range(quarter // 128)
-            ],
-            axis=0,
+    left = lax.broadcasted_iota(jnp.int32, (1, 128), 1) < 64
+    empty = jnp.zeros((7, sub), jnp.float32)
+    pair = 2 * owned
+    for at in range(0, targets, 4):
+        sums = jnp.dot(
+            raised_ref[at * owned : (at + 4) * owned, :], sides_ref[...], preferred_element_type=jnp.float32
         )
-        sums_ref[j, quarter:, :] = jnp.concatenate(terms_of(counts, 2), axis=0).astype(jnp.bfloat16)
-        return 0
-
-    lax.fori_loop(0, parts, add, 0)
-
-
-def middle_kernel(sums_ref, out_ref):
-    parts, held, sub = sums_ref.shape
-    targets, rows, _ = out_ref.shape
-    words = rows - 8
-    quarter = targets * words
-    counts = jnp.zeros((quarter // 128, 128), jnp.float32)
-    for part in range(parts):
-        pair = sums_ref[part, quarter:, :].astype(jnp.float32)
-        counts = counts + (pair[: quarter // 128] + pair[quarter // 128 :])
-    high, low = terms_of(counts, 2)
-    left = lax.broadcasted_iota(jnp.int32, high.shape, 1) < 64
-    even = jnp.where(left, high, pltpu.roll(low, 64, 1))
-    odd = jnp.where(left, pltpu.roll(high, 64, 1), low)
-    for target in range(targets):
-        at = slice(target * words, target * words + words)
-        total = sums_ref[0, at, :].astype(jnp.float32)
-        for part in range(1, parts):
-            total = total + sums_ref[part, at, :].astype(jnp.float32)
-        row = (even if target % 2 == 0 else odd)[target // 2 : target // 2 + 1]
-        row = jnp.concatenate([row, jnp.zeros((7, sub), jnp.float32)], axis=0)
-        out_ref[target] = jnp.concatenate([total, row], axis=0).astype(jnp.bfloat16)
+        for k in range(2):
+            both = sums[k * pair : k * pair + pair]
+            counts = both[:, sub:]
+            counts = counts + pltpu.roll(counts, sub // 2, 1)
+            counts = jnp.sum(jnp.where(diagonal, counts, 0.0), axis=0, keepdims=True)
+            high, low = terms_of(counts, 2)
+            even = jnp.where(left, high, pltpu.roll(low, 64, 1))
+            odd = jnp.where(left, pltpu.roll(high, 64, 1), low)
+            for n, extra in enumerate((even, odd)):
+                block = [both[n * owned : n * owned + owned, :sub], extra, empty]
+                sums_ref[at + 2 * k + n] = jnp.concatenate(block, axis=0).astype(jnp.bfloat16)
+
+
+def share_kernel(place_ref, rebuilt_ref, factors_ref, own_ref, *block_refs):
+    sub, rows = own_ref.shape
+    count = len(block_refs) + 1
+    for step in range(count):
+        at = pl.ds(pl.multiple_of(lax.rem(place_ref[2] + step, count) * rows, 128), rows)
+        rebuilt = rebuilt_ref[:, at] * factors_ref[0:1, at]
+        if step == 0:
+            own_ref[...] = rebuilt
+        else:
+            block_refs[step - 1][...] = rebuilt.astype(jnp.bfloat16)
 
 
 def last_kernel(sums_ref, own_ref, out_ref):
@@ -232,15 +240,15 @@
 SMEM = pl.BlockSpec(memory_space=pltpu.SMEM)
 
 
-def call(kernel, out_shape, ins, *args, scratch=(), flops=1):
+def call(kernel, out_shape, ins, *args, scratch=(), mib=8):
     return pl.pallas_call(
         kernel,
         out_shape=out_shape,
         in_specs=ins,
         out_specs=jax.tree.map(lambda _: VMEM, out_shape),
         scratch_shapes=scratch,
-        compiler_params=pltpu.CompilerParams(vmem_limit_bytes=40 * 2**20),
-        cost_estimate=pl.CostEstimate(flops=flops, bytes_accessed=1, transcendentals=0),
+        compiler_params=pltpu.CompilerParams(vmem_limit_bytes=mib * 2**20),
+        cost_estimate=pl.CostEstimate(flops=1, bytes_accessed=1, transcendentals=0),
     )(*args)
 
 
@@ -265,6 +273,7 @@
         embeddings,
         centroids,
         scratch=[pltpu.VMEM((count // chunk, rows, chunk), jnp.float32)],
+        mib=24,
     )
     kept, base = call(
         kept_kernel,
@@ -275,6 +284,7 @@
         inverse,
         centroids,
         embeddings,
+        mib=24,
     )
     return kept, sent, stats, base
 
@@ -293,58 +303,79 @@
     )
 
 
-def quantize(mean, stats, gots, base, book, parts):
-    (sub, rows), words = mean.shape, book.shape[0]
-    quarter = words // parts
-    return call(
-        quantize_kernel,
-        (
-            array((sub, rows), jnp.bfloat16),
-            array((parts, quarter + quarter // 64, sub), jnp.bfloat16),
-            array((words, rows), jnp.bfloat16),
-            array((8, rows)),
-        ),
-        [VMEM] * (len(gots) + 4),
+def local(embeddings, centroids, codebook):
+    _, book_rows, sub_width = codebook.shape
+    y_count, z_count, x_count = lax.axis_size("y"), lax.axis_size("z"), lax.axis_size("x")
+    words = book_rows * z_count
+    place = jnp.stack([lax.axis_index(axis) for axis in ("c", "x", "y")]).astype(jnp.int32)
+
+    own = codebook.reshape(book_rows, sub_width)
+    book = exchange(jnp.broadcast_to(own, (z_count, book_rows, sub_width)), "z")
+    book = book.reshape(words, sub_width)
+
+    def ring(count, step):
+        return [(i, (i + step) % count) for i in range(count)]
+
+    kept, sent, stats, base = coarse(embeddings, centroids, place)
+    got = lax.ppermute(sent, "c", ring(2, 1))
+    mean, stats, *blocks = chip(place, kept, got, stats)
+    gots = [lax.ppermute(block, "x", ring(x_count, step)) for step, block in enumerate(blocks, 1)]
+
+    rows = base.shape[1]
+    residual, copies = call(
+        residual_kernel,
+        (array((sub_width, rows), jnp.bfloat16), array((y_count, sub_width, rows), jnp.bfloat16)),
+        [VMEM] * (len(gots) + 3),
         mean,
         stats,
         *gots,
         base,
+    )
+    book, copies = lax.optimization_barrier((book, copies))
+    wide = exchange(copies, "y")
+
+    raised, stats = call(
+        score_kernel,
+        (
+            array((words, y_count * rows), jnp.bfloat16),
+            array((y_count, y_count * PACKED, rows), jnp.bfloat16),
+        ),
+        [VMEM] * 2,
         book,
-        scratch=[pltpu.VMEM((words, rows), jnp.float32)],
-    )
-
-
-def local(embeddings, centroids, codebook):
-    _, book_rows, sub_width = codebook.shape
-    y_count, z_count, x_count = lax.axis_size("y"), lax.axis_size("z"), lax.axis_size("x")
-    words = book_rows * y_count * z_count
-    place = jnp.stack([lax.axis_index("c"), lax.axis_index("x")]).astype(jnp.int32)
-
-    own = codebook.reshape(book_rows, sub_width)
-    book = exchange(jnp.broadcast_to(own, (z_count, book_rows, sub_width)), "z")
-    book = book.reshape(words // y_count, sub_width)
-
-    kept, sent, stats, base = coarse(embeddings, centroids, place)
-    got = lax.ppermute(sent, "c", [(0, 1), (1, 0)])
-    book, got, kept = lax.optimization_barrier((book, got, kept))
-    mean, stats, *blocks = chip(place, kept, got, stats)
-    gots = [
-        lax.ppermute(block, "x", [(i, (i + step) % x_count) for i in range(x_count)])
-        for step, block in enumerate(blocks, 1)
-    ]
-    book = exchange(jnp.broadcast_to(book, (y_count,) + book.shape), "y").reshape(words, sub_width)
-    residual, sums, raised, inverse = quantize(mean, stats, gots, base, book, y_count)
-
-    sums = exchange(sums, "y")
-    rebuilt = lax.dot_general(
-        book, raised, (((0,), (0,)), ((), ())), preferred_element_type=jnp.float32
-    ) * inverse[:1]
-    pq_error = jnp.mean(jnp.square(residual.astype(jnp.float32) - rebuilt), axis=0)
-    sums, pq_error = lax.optimization_barrier((sums, pq_error))
-    sums = call(
-        middle_kernel, array((z_count, book_rows + 8, sub_width), jnp.bfloat16), [VMEM], sums
-    )
+        wide,
+        scratch=[pltpu.VMEM((y_count, words, rows), jnp.float32), pltpu.VMEM((words, 128), jnp.float32)],
+        mib=24,
+    )
+    stats = exchange(stats, "y")
+    rebuilt = lax.dot_general(book, raised, (((0,), (0,)), ((), ())), preferred_element_type=jnp.float32)
+    stats, rebuilt = lax.optimization_barrier((stats, rebuilt))
+    sums, factors = call(
+        sum_kernel,
+        (
+            array((z_count, book_rows + 8, sub_width), jnp.bfloat16),
+            array((8, y_count * rows)),
+        ),
+        [SMEM] + [VMEM] * 3,
+        place,
+        stats,
+        wide,
+        raised,
+        scratch=[pltpu.VMEM((y_count * rows, 2 * sub_width), jnp.bfloat16)],
+        mib=16,
+    )
+
     sums = exchange(sums, "z")
+    whole, *blocks = call(
+        share_kernel,
+        [array((sub_width, rows))] + [array((sub_width, rows), jnp.bfloat16)] * (y_count - 1),
+        [SMEM] + [VMEM] * 2,
+        place,
+        rebuilt,
+        factors,
+    )
+    for step, block in enumerate(blocks, 1):
+        whole = whole + lax.ppermute(block, "y", ring(y_count, step)).astype(jnp.float32)
+    pq_error = jnp.mean(jnp.square(residual.astype(jnp.float32) - whole), axis=0)
     new_codebook = call(last_kernel, array((book_rows, sub_width)), [VMEM] * 2, sums, own)
     return (residual, new_codebook[None], pq_error[None])
 

time: 111 us -> 110 us (level)
  waiting for transfers between devices: 37.3 us -> 13.9 us
  blocking collectives: 0 us -> 11.6 us
  starting transfers between devices: 44.4 us -> 50.8 us
  local copies, waits for them, and re-layouts: 8.13 us -> 12.3 us
  Pallas kernels: 15.9 us -> 14.5 us
    all_to_all x4 -> x3, waiting for transfers between devices: 31.3 us -> 3.93 us  [exchange(): return lax.all_to_all(parts, axis, 0, 0, tiled=True)]
    all_to_all x0 -> x1, blocking collectives: none -> 11.6 us  [exchange(): return lax.all_to_all(parts, axis, 0, 0, tiled=True)]
    ppermute x4 -> x7, starting transfers between devices: 10.6 us -> 19.6 us  [the longest x3 9 us: local(): lax.ppermute(block, 'y', ring(y_count, step)).astype(jnp.float32)]
    unnamed x8 -> x26, local copies, waits for them, and re-layouts: 4.95 us -> 10.2 us
    ppermute x4 -> x7, waiting for transfers between devices: 5.92 us -> 10 us  [the longest x3 6.07 us: local(): lax.ppermute(block, 'x', ring(x_count, step))]
    all_to_all x4 -> x3, starting transfers between devices: 33.8 us -> 31.2 us  [exchange(): return lax.all_to_all(parts, axis, 0, 0, tiled=True)]
    broadcast_in_dim x2 -> x0, local copies, waits for them, and re-layouts: 1.68 us -> none  [the longest x1 1.12 us: local(): jnp.broadcast_to(book, (y_count,) + book.shape)]
    pallas_call x6 -> x8, Pallas kernels: 15.9 us -> 14.5 us  [call(): pl.pallas_call(kernel, out_shape=out_shape, in_specs=ins, out_specs=jax.t...]
  transfers between devices with their start and end apart: 8 -> 10, of which waited for: 5 -> 5; matrix products, arithmetic and copies ran while one was open for 3% -> 4% of each run, Pallas kernels for 7% -> 9%
where the time goes in v6:
time: 110 us; the launch traced here: 107 us
  starting transfers between devices  50.8 us (46%)
  Pallas kernels  14.5 us (13%)
  waiting for transfers between devices  13.9 us (13%)
  local copies, waits for them, and re-layouts  12.3 us (11%)
  blocking collectives  11.6 us (11%)
  matrix products  2.46 us (2%)
    all_to_all x3, starting transfers between devices, exchange(): return lax.all_to_all(parts, axis, 0, 0, tiled=True)  31.2 us
    pallas_call x8, Pallas kernels, call(): pl.pallas_call(kernel, out_shape=out_shape, in_specs=ins, out_specs=jax.t...  14.5 us
    all_to_all x1, blocking collectives, exchange(): return lax.all_to_all(parts, axis, 0, 0, tiled=True)  11.6 us
    unnamed x26, local copies, waits for them, and re-layouts  10.2 us
    ppermute x3, starting transfers between devices, local(): lax.ppermute(block, 'y', ring(y_count, step)).astype(jnp.float32)  9 us
    ppermute x3, starting transfers between devices, local(): lax.ppermute(block, 'x', ring(x_count, step))  8.64 us
    ppermute x3, waiting for transfers between devices, local(): lax.ppermute(block, 'x', ring(x_count, step))  6.07 us
    ppermute x3, waiting for transfers between devices, local(): lax.ppermute(block, 'y', ring(y_count, step)).astype(jnp.float32)  3.94 us
  transfers between devices with their start and end apart: 10, of which 5 were waited for; matrix products, arithmetic and copies ran while one was open for 4% of the time, Pallas kernels for 9%

profile of v6, /device:TPU:6, one launch (start us, length us, event | category | flops | bytes accessed | tf_op | source)
XLA Modules:
  0.0 107.5 jit_solution(8268800918260402818)
XLA Ops:
  0.6 1.5 %broadcast_in_dim.7 = bf16[16,64,128]{2,1,0:T(8,128)(2,1)} broadcast(bf16[64,128]{1,0:T(8,128)(2,1)} %bitcast.10), dimensions={1,2} | broadcast | bytes 278528 | tf_op jit(solution)/shard_map/broadcast_in_dim | solution.py:313
  2.1 15.2 %all-to-all-start = ((bf16[16,64,128]{2,1,0:T(8,128)(2,1)}), bf16[16,64,128]{2,1,0:T(8,128)(2,1)S(1)}, u32[]{:S(2)}, u32[]{:S(2)}) async-start(bf16[16,64,128]{2,1,0:T(8,128)(2,1)} %broadcast_in_dim.7), calls=%async_computation | async-start | bytes 524288 | tf_op jit(solution)/shard_map/all_to_all | solution.py:19
  17.4 2.2 %copy-done = bf16[2048,1024]{1,0:T(8,128)(2,1)S(1)} copy-done((bf16[2048,1024]{1,0:T(8,128)(2,1)S(1)}, bf16[2048,1024]{1,0:T(8,128)(2,1)}, u32[]{:S(2)}) %copy-start) | copy-done | bytes 4194328
  19.6 1.1 %copy-done.2 = bf16[384,1024]{1,0:T(8,128)(2,1)S(1)} copy-done((bf16[384,1024]{1,0:T(8,128)(2,1)S(1)}, bf16[384,1024]{1,0:T(8,128)(2,1)}, u32[]{:S(2)}) %copy-start.2) | copy-done | bytes 786456
  20.7 5.2 %shard_map.58 = (bf16[528,384]{1,0:T(8,128)(2,1)S(1)}, f32[8,384]{1,0:T(8,128)S(1)}, bf16[384,2048]{1,0:T(8,128)(2,1)S(1)}, f32[384,128]{1,0:T(8,128)S(1)}) custom-call(s32[3]{0:T(128)S(1)} %pad_add_fusion.place_ref, bf16[384,1024]{1,0:T(8,128)(2,1)S(1)} %copy-done.2, bf16[2048,1024]{1,0:T(8,128)(2,1)S(1)} %copy-done), custom_call_target="tpu_custom_call" | custom-call | flops 1 | bytes 1 | tf_op jit(solution)/shard_map/pallas_call | solution.py:244
  25.9 1.9 %collective-permute-start = (bf16[528,384]{1,0:T(8,128)(2,1)S(1)}, bf16[528,384]{1,0:T(8,128)(2,1)S(1)}, u32[]{:S(2)}, u32[]{:S(2)}) collective-permute-start(bf16[528,384]{1,0:T(8,128)(2,1)S(1)} %get-tuple-element.31), channel_id=1, source_target_pairs={{0,1},{1,0},{2,3},{3,2},{4,5},{5,4},{6,7},{7,6},{8,9},{9,8},{10,11... | collective-permute-start | bytes 1216520 | tf_op jit(solution)/shard_map/ppermute | solution.py:320
  27.9 1.8 %shard_map.59 = (f32[512,384]{1,0:T(8,128)S(1)}, f32[128,384]{1,0:T(8,128)S(1)}) custom-call(s32[3]{0:T(128)S(1)} %pad_add_fusion.place_ref, bf16[384,2048]{1,0:T(8,128)(2,1)S(1)} %get-tuple-element.28.weights_ref, f32[384,128]{1,0:T(8,128)S(1)} %get-tuple-element.29.inverse_ref, bf16[2048,1024]{1,0:T(8,128)(2,1)S(1)} %copy-done, bf16[384,1024]{1,0:T(8,128)(2,1)S(1)} %copy-done.2), custom_call_target="tpu_custom_call" | custom-call | flops 1 | bytes 1 | tf_op jit(solution)/shard_map/pallas_call | solution.py:244
  30.5 2.4 %collective-permute-start.1 = (bf16[144,384]{1,0:T(8,128)(2,1)S(1)}, bf16[144,384]{1,0:T(8,128)(2,1)S(1)}, u32[]{:S(2)}, u32[]{:S(2)}) collective-permute-start(bf16[144,384]{1,0:T(8,128)(2,1)S(1)} %get-tuple-element.35), channel_id=1, source_target_pairs={{0,2},{2,4},{4,6},{6,0},{1,3},{3,5},{5,7},{7,1},{8,10},{10,12},{12... | collective-permute-start | bytes 331784 | tf_op jit(solution)/shard_map/ppermute | solution.py:322
  32.9 4.3 %collective-permute-start.2 = (bf16[144,384]{1,0:T(8,128)(2,1)S(1)}, bf16[144,384]{1,0:T(8,128)(2,1)S(1)}, u32[]{:S(2)}, u32[]{:S(2)}) collective-permute-start(bf16[144,384]{1,0:T(8,128)(2,1)S(1)} %get-tuple-element.36), channel_id=1, source_target_pairs={{0,4},{2,6},{4,0},{6,2},{1,5},{3,7},{5,1},{7,3},{8,12},{10,14},{12... | collective-permute-start | bytes 331784 | tf_op jit(solution)/shard_map/ppermute | solution.py:322
  37.2 1.9 %collective-permute-start.3 = (bf16[144,384]{1,0:T(8,128)(2,1)S(1)}, bf16[144,384]{1,0:T(8,128)(2,1)S(1)}, u32[]{:S(2)}, u32[]{:S(2)}) collective-permute-start(bf16[144,384]{1,0:T(8,128)(2,1)S(1)} %get-tuple-element.37), channel_id=1, source_target_pairs={{0,6},{2,0},{4,2},{6,4},{1,7},{3,1},{5,3},{7,5},{8,14},{10,8},{12,... | collective-permute-start | bytes 331784 | tf_op jit(solution)/shard_map/ppermute | solution.py:322
  39.1 2.3 %collective-permute-done.2.refs_1_ = bf16[144,384]{1,0:T(8,128)(2,1)S(1)} collective-permute-done((bf16[144,384]{1,0:T(8,128)(2,1)S(1)}, bf16[144,384]{1,0:T(8,128)(2,1)S(1)}, u32[]{:S(2)}, u32[]{:S(2)}) %collective-permute-start.2) | collective-permute-done | bytes 110624 | tf_op jit(solution)/shard_map/ppermute | solution.py:322
  41.4 3.8 %collective-permute-done.3.refs_2_ = bf16[144,384]{1,0:T(8,128)(2,1)S(1)} collective-permute-done((bf16[144,384]{1,0:T(8,128)(2,1)S(1)}, bf16[144,384]{1,0:T(8,128)(2,1)S(1)}, u32[]{:S(2)}, u32[]{:S(2)}) %collective-permute-start.3) | collective-permute-done | bytes 110624 | tf_op jit(solution)/shard_map/ppermute | solution.py:322
  45.2 0.8 shard_map.61
  46.0 0.7 copy-done.3
  46.7 11.6 %all_to_all.20.rows_ref = bf16[4,128,384]{2,1,0:T(8,128)(2,1)S(1)} all-to-all(bf16[4,128,384]{2,1,0:T(8,128)(2,1)S(1)} %get-tuple-element.42), channel_id=1, replica_groups=mesh['y'=4,'z'=16,'x'=4,'c'=2] {'y'}, dimensions={0} | all-to-all | bytes 786432 | tf_op jit(solution)/shard_map/all_to_all | solution.py:19
  58.3 0.9 copy-done.4
  59.3 2.4 %shard_map.62 = (bf16[1024,1536]{1,0:T(8,128)(2,1)S(1)}, bf16[4,64,384]{2,1,0:T(8,128)(2,1)S(1)}) custom-call(bf16[1024,128]{1,0:T(8,128)(2,1)S(1)} %bitcast.9, bf16[4,128,384]{2,1,0:T(8,128)(2,1)S(1)} %all_to_all.20.rows_ref), custom_call_target="tpu_custom_call" | custom-call | flops 1 | bytes 1 | tf_op jit(solution)/shard_map/pallas_call | solution.py:244
  62.3 4.0 %all-to-all-start.2 = ((bf16[4,64,384]{2,1,0:T(8,128)(2,1)}), bf16[4,64,384]{2,1,0:T(8,128)(2,1)}, u32[]{:S(2)}, u32[]{:S(2)}) async-start(bf16[4,64,384]{2,1,0:T(8,128)(2,1)} %copy-done.6), calls=%async_computation.2 | async-start | bytes 393216 | tf_op jit(solution)/shard_map/all_to_all | solution.py:19
  66.3 2.5 %fusion.rebuilt_ref = f32[128,1536]{1,0:T(8,128)} fusion(bf16[1024,128]{1,0:T(8,128)(2,1)} %bitcast.8, bf16[1024,1536]{1,0:T(8,128)(2,1)S(1)} %get-tuple-element.44.raised_ref), kind=kOutput, calls=%fused_computation.3 | convolution fusion | flops 402653184 | bytes 4194304 | tf_op jit(solution)/shard_map/dot_general | solution.py:350
  68.8 3.9 %all-to-all-done.2.stats_ref = bf16[4,64,384]{2,1,0:T(8,128)(2,1)} async-done(((bf16[4,64,384]{2,1,0:T(8,128)(2,1)}), bf16[4,64,384]{2,1,0:T(8,128)(2,1)}, u32[]{:S(2)}, u32[]{:S(2)}) %all-to-all-start.2) | async-done | bytes 196640 | tf_op jit(solution)/shard_map/all_to_all | solution.py:19
  73.4 2.2 %shard_map.63 = (bf16[16,72,128]{2,1,0:T(8,128)(2,1)S(1)}, f32[8,1536]{1,0:T(8,128)S(1)}) custom-call(s32[3]{0:T(128)S(1)} %copy-done.11, bf16[4,64,384]{2,1,0:T(8,128)(2,1)} %all-to-all-done.2.stats_ref, bf16[4,128,384]{2,1,0:T(8,128)(2,1)S(1)} %all_to_all.20.rows_ref, bf16[1024,1536]{1,0:T(8,128)(2,1)S(1)} %get-tuple-element.44.raised_ref), custom_call_target="tpu_custom_call" | custom-call | flops 1 | bytes 1 | tf_op jit(solution)/shard_map/pallas_call | solution.py:244
  75.6 0.7 copy-done.5
  76.9 12.0 %all-to-all-start.3 = ((bf16[16,72,128]{2,1,0:T(8,128)(2,1)}), bf16[16,72,128]{2,1,0:T(8,128)(2,1)S(1)}, u32[]{:S(2)}, u32[]{:S(2)}) async-start(bf16[16,72,128]{2,1,0:T(8,128)(2,1)} %copy-done.5), calls=%async_computation.3 | async-start | bytes 589824 | tf_op jit(solution)/shard_map/all_to_all | solution.py:19
  89.0 1.1 %copy-done.1 = f32[128,1536]{1,0:T(8,128)S(1)} copy-done((f32[128,1536]{1,0:T(8,128)S(1)}, f32[128,1536]{1,0:T(8,128)}, u32[]{:S(2)}) %copy-start.1) | copy-done | bytes 786456
  90.1 0.8 copy-done.9
  92.2 2.5 %collective-permute-start.4 = (bf16[128,384]{1,0:T(8,128)(2,1)S(1)}, bf16[128,384]{1,0:T(8,128)(2,1)S(1)}, u32[]{:S(2)}, u32[]{:S(2)}) collective-permute-start(bf16[128,384]{1,0:T(8,128)(2,1)S(1)} %get-tuple-element.50), channel_id=1, source_target_pairs={{0,128},{128,256},{256,384},{384,0},{1,129},{129,257},{257,385},{3... | collective-permute-start | bytes 294920 | tf_op jit(solution)/shard_map/ppermute | solution.py:377
  94.6 4.0 %collective-permute-start.5 = (bf16[128,384]{1,0:T(8,128)(2,1)S(1)}, bf16[128,384]{1,0:T(8,128)(2,1)S(1)}, u32[]{:S(2)}, u32[]{:S(2)}) collective-permute-start(bf16[128,384]{1,0:T(8,128)(2,1)S(1)} %get-tuple-element.51), channel_id=1, source_target_pairs={{0,256},{128,384},{256,0},{384,128},{1,257},{129,385},{257,1},{385... | collective-permute-start | bytes 294920 | tf_op jit(solution)/shard_map/ppermute | solution.py:377
  98.6 2.6 %collective-permute-start.6 = (bf16[128,384]{1,0:T(8,128)(2,1)S(1)}, bf16[128,384]{1,0:T(8,128)(2,1)S(1)}, u32[]{:S(2)}, u32[]{:S(2)}) collective-permute-start(bf16[128,384]{1,0:T(8,128)(2,1)S(1)} %get-tuple-element.52), channel_id=1, source_target_pairs={{0,384},{128,0},{256,128},{384,256},{1,385},{129,1},{257,129},{385... | collective-permute-start | bytes 294920 | tf_op jit(solution)/shard_map/ppermute | solution.py:377
  101.2 1.5 %collective-permute-done.5 = bf16[128,384]{1,0:T(8,128)(2,1)S(1)} collective-permute-done((bf16[128,384]{1,0:T(8,128)(2,1)S(1)}, bf16[128,384]{1,0:T(8,128)(2,1)S(1)}, u32[]{:S(2)}, u32[]{:S(2)}) %collective-permute-start.5) | collective-permute-done | bytes 98336 | tf_op jit(solution)/shard_map/ppermute | solution.py:377
  102.7 2.5 %collective-permute-done.6 = bf16[128,384]{1,0:T(8,128)(2,1)S(1)} collective-permute-done((bf16[128,384]{1,0:T(8,128)(2,1)S(1)}, bf16[128,384]{1,0:T(8,128)(2,1)S(1)}, u32[]{:S(2)}, u32[]{:S(2)}) %collective-permute-start.6) | collective-permute-done | bytes 98336 | tf_op jit(solution)/shard_map/ppermute | solution.py:377
  105.1 1.0 multiply_reduce_fusion
  106.7 0.8 shard_map.64
  (29 shorter events, 4.6 us)
Async XLA Ops:
  2.1 43.9 %all-to-all-start = ((bf16[16,64,128]{2,1,0:T(8,128)(2,1)}), bf16[16,64,128]{2,1,0:T(8,128)(2,1)S(1)}, u32[]{:S(2)}, u32[]{:S(2)}) async-start(bf16[16,64,128]{2,1,0:T(8,128)(2,1)} %broadcast_in_dim.7), calls=%async_computation | async-start | bytes 524288 | tf_op jit(solution)/shard_map/all_to_all | solution.py:19
  17.4 2.2 %copy-start = (bf16[2048,1024]{1,0:T(8,128)(2,1)S(1)}, bf16[2048,1024]{1,0:T(8,128)(2,1)}, u32[]{:S(2)}) copy-start(bf16[2048,1024]{1,0:T(8,128)(2,1)} %c_ref.3) | copy-start | bytes 12582916
  19.6 1.1 %copy-start.2 = (bf16[384,1024]{1,0:T(8,128)(2,1)S(1)}, bf16[384,1024]{1,0:T(8,128)(2,1)}, u32[]{:S(2)}) copy-start(bf16[384,1024]{1,0:T(8,128)(2,1)} %e_ref.3) | copy-start | bytes 2359300
  20.7 9.0 %copy-start.10 = (s32[3]{0:T(128)}, s32[3]{0:T(128)S(1)}, u32[]{:S(2)}) copy-start(s32[3]{0:T(128)S(1)} %pad_add_fusion.place_ref) | copy-start | bytes 40
  25.9 3.8 %collective-permute-start = (bf16[528,384]{1,0:T(8,128)(2,1)S(1)}, bf16[528,384]{1,0:T(8,128)(2,1)S(1)}, u32[]{:S(2)}, u32[]{:S(2)}) collective-permute-start(bf16[528,384]{1,0:T(8,128)(2,1)S(1)} %get-tuple-element.31), channel_id=1, source_target_pairs={{0,1},{1,0},{2,3},{3,2},{4,5},{5,4},{6,7},{7,6},{8,9},{9,8},{10,11... | collective-permute-start | bytes 1216520 | tf_op jit(solution)/shard_map/ppermute | solution.py:320
  30.5 8.7 %collective-permute-start.1 = (bf16[144,384]{1,0:T(8,128)(2,1)S(1)}, bf16[144,384]{1,0:T(8,128)(2,1)S(1)}, u32[]{:S(2)}, u32[]{:S(2)}) collective-permute-start(bf16[144,384]{1,0:T(8,128)(2,1)S(1)} %get-tuple-element.35), channel_id=1, source_target_pairs={{0,2},{2,4},{4,6},{6,0},{1,3},{3,5},{5,7},{7,1},{8,10},{10,12},{12... | collective-permute-start | bytes 331784 | tf_op jit(solution)/shard_map/ppermute | solution.py:322
  32.9 8.6 %collective-permute-start.2 = (bf16[144,384]{1,0:T(8,128)(2,1)S(1)}, bf16[144,384]{1,0:T(8,128)(2,1)S(1)}, u32[]{:S(2)}, u32[]{:S(2)}) collective-permute-start(bf16[144,384]{1,0:T(8,128)(2,1)S(1)} %get-tuple-element.36), channel_id=1, source_target_pairs={{0,4},{2,6},{4,0},{6,2},{1,5},{3,7},{5,1},{7,3},{8,12},{10,14},{12... | collective-permute-start | bytes 331784 | tf_op jit(solution)/shard_map/ppermute | solution.py:322
  37.2 8.0 %collective-permute-start.3 = (bf16[144,384]{1,0:T(8,128)(2,1)S(1)}, bf16[144,384]{1,0:T(8,128)(2,1)S(1)}, u32[]{:S(2)}, u32[]{:S(2)}) collective-permute-start(bf16[144,384]{1,0:T(8,128)(2,1)S(1)} %get-tuple-element.37), channel_id=1, source_target_pairs={{0,6},{2,0},{4,2},{6,4},{1,7},{3,1},{5,3},{7,5},{8,14},{10,8},{12,... | collective-permute-start | bytes 331784 | tf_op jit(solution)/shard_map/ppermute | solution.py:322
  46.0 0.7 copy-start.3
  58.3 1.0 copy-start.4
  61.7 0.7 copy-start.6
  62.3 10.4 %all-to-all-start.2 = ((bf16[4,64,384]{2,1,0:T(8,128)(2,1)}), bf16[4,64,384]{2,1,0:T(8,128)(2,1)}, u32[]{:S(2)}, u32[]{:S(2)}) async-start(bf16[4,64,384]{2,1,0:T(8,128)(2,1)} %copy-done.6), calls=%async_computation.2 | async-start | bytes 393216 | tf_op jit(solution)/shard_map/all_to_all | solution.py:19
  68.8 37.9 %copy-start.7 = (bf16[1,64,128]{2,1,0:T(8,128)(2,1)S(1)}, bf16[1,64,128]{2,1,0:T(8,128)(2,1)}, u32[]{:S(2)}) copy-start(bf16[1,64,128]{2,1,0:T(8,128)(2,1)} %param.5) | copy-start | bytes 49156
  72.7 0.7 copy-start.11
  75.6 0.7 copy-start.5
  76.3 0.6 copy-start.8
  76.9 29.8 %all-to-all-start.3 = ((bf16[16,72,128]{2,1,0:T(8,128)(2,1)}), bf16[16,72,128]{2,1,0:T(8,128)(2,1)S(1)}, u32[]{:S(2)}, u32[]{:S(2)}) async-start(bf16[16,72,128]{2,1,0:T(8,128)(2,1)} %copy-done.5), calls=%async_computation.3 | async-start | bytes 589824 | tf_op jit(solution)/shard_map/all_to_all | solution.py:19
  89.0 1.1 %copy-start.1 = (f32[128,1536]{1,0:T(8,128)S(1)}, f32[128,1536]{1,0:T(8,128)}, u32[]{:S(2)}) copy-start(f32[128,1536]{1,0:T(8,128)} %fusion.rebuilt_ref) | copy-start | bytes 2359300
  90.1 0.8 copy-start.9
  90.9 0.7 copy-start.12
  92.2 9.0 %collective-permute-start.4 = (bf16[128,384]{1,0:T(8,128)(2,1)S(1)}, bf16[128,384]{1,0:T(8,128)(2,1)S(1)}, u32[]{:S(2)}, u32[]{:S(2)}) collective-permute-start(bf16[128,384]{1,0:T(8,128)(2,1)S(1)} %get-tuple-element.50), channel_id=1, source_target_pairs={{0,128},{128,256},{256,384},{384,0},{1,129},{129,257},{257,385},{3... | collective-permute-start | bytes 294920 | tf_op jit(solution)/shard_map/ppermute | solution.py:377
  94.6 8.0 %collective-permute-start.5 = (bf16[128,384]{1,0:T(8,128)(2,1)S(1)}, bf16[128,384]{1,0:T(8,128)(2,1)S(1)}, u32[]{:S(2)}, u32[]{:S(2)}) collective-permute-start(bf16[128,384]{1,0:T(8,128)(2,1)S(1)} %get-tuple-element.51), channel_id=1, source_target_pairs={{0,256},{128,384},{256,0},{384,128},{1,257},{129,385},{257,1},{385... | collective-permute-start | bytes 294920 | tf_op jit(solution)/shard_map/ppermute | solution.py:377
  98.6 6.5 %collective-permute-start.6 = (bf16[128,384]{1,0:T(8,128)(2,1)S(1)}, bf16[128,384]{1,0:T(8,128)(2,1)S(1)}, u32[]{:S(2)}, u32[]{:S(2)}) collective-permute-start(bf16[128,384]{1,0:T(8,128)(2,1)S(1)} %get-tuple-element.52), channel_id=1, source_target_pairs={{0,384},{128,0},{256,128},{384,256},{1,385},{129,1},{257,129},{385... | collective-permute-start | bytes 294920 | tf_op jit(solution)/shard_map/ppermute | solution.py:377

commit v7 on v6

--- a/solution.py
+++ b/solution.py
@@ -141,17 +141,19 @@
         copies_ref[copy] = residual
 
 
-def score_kernel(book_ref, rows_ref, raised_ref, stats_ref, gaps_ref, half_ref):
+def half_kernel(book_ref, half_ref):
+    wide = book_ref[...].astype(jnp.float32)
+    half_ref[...] = jnp.broadcast_to(0.5 * jnp.sum(wide * wide, axis=1, keepdims=True), half_ref.shape)
+
+
+def score_kernel(book_ref, half_ref, rows_ref, raised_hbm, stats_ref, own_ref, gaps_ref, raised_ref, sems):
     parts, sub, rows = rows_ref.shape
     words = book_ref.shape[0]
     scale = 2.0 / math.sqrt(sub)
     chunk = 256
     spans = [slice(at, at + chunk) for at in range(0, words, chunk)]
-    for at in spans:
-        wide = book_ref[at, :].astype(jnp.float32)
-        half = 0.5 * jnp.sum(wide * wide, axis=1, keepdims=True)
-        half_ref[at, :] = jnp.broadcast_to(half, (chunk, 128))
     packs = []
+    stores = []
     for part in range(parts):
         peak = jnp.full((8, rows), -jnp.inf, jnp.float32)
         for at in spans:
@@ -163,15 +165,22 @@
         total = jnp.zeros((8, rows), jnp.float32)
         for at in spans:
             raised = jnp.exp((gaps_ref[part, at, :] - peak) * scale)
-            raised_ref[at, part * rows : part * rows + rows] = raised.astype(jnp.bfloat16)
+            raised_ref[part, at, :] = raised.astype(jnp.bfloat16)
             total = total + jnp.sum(raised.reshape(chunk // 8, 8, rows), axis=0)
-        packs.append(packed(peak, jnp.sum(total, axis=0, keepdims=True)))
+        stores.append(pltpu.make_async_copy(raised_ref.at[part], raised_hbm.at[part], sems.at[part]))
+        stores[-1].start()
+        total = jnp.sum(total, axis=0, keepdims=True)
+        packs.append(packed(peak, total))
+        own = jnp.concatenate([peak, 1.0 / total, jnp.zeros((6, rows), jnp.float32)], axis=0)
+        own_ref[:, part * rows : part * rows + rows] = own
     pack = jnp.concatenate(packs, axis=0)
     for copy in range(stats_ref.shape[0]):
         stats_ref[copy] = pack
-
-
-def sum_kernel(place_ref, stats_ref, rows_ref, raised_ref, sums_ref, factors_ref, sides_ref):
+    for store in stores:
+        store.wait()
+
+
+def sum_kernel(stats_ref, own_ref, rows_ref, raised_ref, sums_ref, sides_ref):
     parts, sub, rows = rows_ref.shape
     targets, held, _ = sums_ref.shape
     owned = held - 8
@@ -181,9 +190,8 @@
         stats = [unpacked(stats_ref[peer, at, :]) for peer in range(parts)]
         peak = functools.reduce(jnp.maximum, [own for own, _ in stats])
         whole = functools.reduce(jnp.add, [jnp.exp((own - peak) * scale) * total for own, total in stats])
-        own, _ = unpacked(stats_ref[place_ref[2], at, :])
+        own = own_ref[0:1, part * rows : part * rows + rows]
         factor = jnp.exp((own - peak) * scale) / whole
-        factors_ref[:, part * rows : part * rows + rows] = jnp.broadcast_to(factor, (8, rows))
         scaled = rows_ref[part].astype(jnp.float32) * factor
         high, low = (jnp.broadcast_to(term, (sub // 2, rows)) for term in terms_of(factor, 2))
         sides = jnp.transpose(jnp.concatenate([scaled, high, low], axis=0))
@@ -194,8 +202,9 @@
     empty = jnp.zeros((7, sub), jnp.float32)
     pair = 2 * owned
     for at in range(0, targets, 4):
+        raised = [raised_ref[part, at * owned : (at + 4) * owned, :] for part in range(parts)]
         sums = jnp.dot(
-            raised_ref[at * owned : (at + 4) * owned, :], sides_ref[...], preferred_element_type=jnp.float32
+            jnp.concatenate(raised, axis=1), sides_ref[...], preferred_element_type=jnp.float32
         )
         for k in range(2):
             both = sums[k * pair : k * pair + pair]
@@ -210,16 +219,32 @@
                 sums_ref[at + 2 * k + n] = jnp.concatenate(block, axis=0).astype(jnp.bfloat16)
 
 
-def share_kernel(place_ref, rebuilt_ref, factors_ref, own_ref, *block_refs):
+def share_kernel(place_ref, rebuilt_ref, stats_ref, own_ref, *block_refs):
     sub, rows = own_ref.shape
     count = len(block_refs) + 1
     for step in range(count):
-        at = pl.ds(pl.multiple_of(lax.rem(place_ref[2] + step, count) * rows, 128), rows)
-        rebuilt = rebuilt_ref[:, at] * factors_ref[0:1, at]
+        part = lax.rem(place_ref[2] + step, count)
+        at = pl.ds(pl.multiple_of(part * rows, 128), rows)
+        rebuilt = rebuilt_ref[part] * stats_ref[1:2, at]
         if step == 0:
             own_ref[...] = rebuilt
         else:
             block_refs[step - 1][...] = rebuilt.astype(jnp.bfloat16)
+
+
+def error_kernel(place_ref, stats_ref, residual_ref, own_ref, *refs):
+    *got_refs, error_ref = refs
+    sub, rows = own_ref.shape
+    count = len(got_refs) + 1
+    scale = 2.0 / math.sqrt(sub)
+    at = pl.ds(pl.multiple_of(place_ref[2] * PACKED, PACKED), PACKED)
+    stats = [unpacked(stats_ref[lax.rem(place_ref[2] + count - step, count), at, :]) for step in range(count)]
+    shares, _, _ = weigh([peak * scale for peak, _ in stats], [total for _, total in stats])
+    rebuilt = own_ref[...] * shares[0]
+    for got, share in zip(got_refs, shares[1:]):
+        rebuilt = rebuilt + got[...].astype(jnp.float32) * share
+    gap = residual_ref[...].astype(jnp.float32) - rebuilt
+    error_ref[...] = jnp.sum(gap * gap, axis=0, keepdims=True) * (1.0 / sub)
 
 
 def last_kernel(sums_ref, own_ref, out_ref):
@@ -238,14 +263,15 @@
 
 VMEM = pl.BlockSpec(memory_space=pltpu.VMEM)
 SMEM = pl.BlockSpec(memory_space=pltpu.SMEM)
-
-
-def call(kernel, out_shape, ins, *args, scratch=(), mib=8):
+HBM = pl.BlockSpec(memory_space=pltpu.HBM)
+
+
+def call(kernel, out_shape, ins, *args, outs=None, scratch=(), mib=8):
     return pl.pallas_call(
         kernel,
         out_shape=out_shape,
         in_specs=ins,
-        out_specs=jax.tree.map(lambda _: VMEM, out_shape),
+        out_specs=outs or jax.tree.map(lambda _: VMEM, out_shape),
         scratch_shapes=scratch,
         compiler_params=pltpu.CompilerParams(vmem_limit_bytes=mib * 2**20),
         cost_estimate=pl.CostEstimate(flops=1, bytes_accessed=1, transcendentals=0),
@@ -333,51 +359,58 @@
     )
     book, copies = lax.optimization_barrier((book, copies))
     wide = exchange(copies, "y")
-
-    raised, stats = call(
+    half = call(half_kernel, array((words, 128)), [VMEM], book)
+    wide, half = lax.optimization_barrier((wide, half))
+
+    raised, stats, own_stats = call(
         score_kernel,
         (
-            array((words, y_count * rows), jnp.bfloat16),
+            array((y_count, words, rows), jnp.bfloat16),
             array((y_count, y_count * PACKED, rows), jnp.bfloat16),
-        ),
-        [VMEM] * 2,
-        book,
-        wide,
-        scratch=[pltpu.VMEM((y_count, words, rows), jnp.float32), pltpu.VMEM((words, 128), jnp.float32)],
-        mib=24,
-    )
-    stats = exchange(stats, "y")
-    rebuilt = lax.dot_general(book, raised, (((0,), (0,)), ((), ())), preferred_element_type=jnp.float32)
-    stats, rebuilt = lax.optimization_barrier((stats, rebuilt))
-    sums, factors = call(
-        sum_kernel,
-        (
-            array((z_count, book_rows + 8, sub_width), jnp.bfloat16),
             array((8, y_count * rows)),
         ),
-        [SMEM] + [VMEM] * 3,
-        place,
-        stats,
+        [VMEM] * 3,
+        book,
+        half,
         wide,
-        raised,
-        scratch=[pltpu.VMEM((y_count * rows, 2 * sub_width), jnp.bfloat16)],
-        mib=16,
-    )
-
-    sums = exchange(sums, "z")
+        outs=(HBM, VMEM, VMEM),
+        scratch=[
+            pltpu.VMEM((y_count, words, rows), jnp.float32),
+            pltpu.VMEM((y_count, words, rows), jnp.bfloat16),
+            pltpu.SemaphoreType.DMA((y_count,)),
+        ],
+        mib=51,
+    )
+    stats = exchange(stats, "y")
+    rebuilt = jnp.einsum("kd,pkr->pdr", book, raised, preferred_element_type=jnp.float32)
     whole, *blocks = call(
         share_kernel,
         [array((sub_width, rows))] + [array((sub_width, rows), jnp.bfloat16)] * (y_count - 1),
         [SMEM] + [VMEM] * 2,
         place,
         rebuilt,
-        factors,
-    )
-    for step, block in enumerate(blocks, 1):
-        whole = whole + lax.ppermute(block, "y", ring(y_count, step)).astype(jnp.float32)
-    pq_error = jnp.mean(jnp.square(residual.astype(jnp.float32) - whole), axis=0)
+        own_stats,
+    )
+    stats, whole, *blocks = lax.optimization_barrier((stats, whole, *blocks))
+    sums = call(
+        sum_kernel,
+        array((z_count, book_rows + 8, sub_width), jnp.bfloat16),
+        [VMEM] * 4,
+        stats,
+        own_stats,
+        wide,
+        raised,
+        scratch=[pltpu.VMEM((y_count * rows, 2 * sub_width), jnp.bfloat16)],
+        mib=16,
+    )
+
+    sums = exchange(sums, "z")
+    gots = [lax.ppermute(block, "y", ring(y_count, step)) for step, block in enumerate(blocks, 1)]
+    pq_error = call(
+        error_kernel, array((1, rows)), [SMEM] + [VMEM] * 6, place, stats, residual, whole, *gots
+    )
     new_codebook = call(last_kernel, array((book_rows, sub_width)), [VMEM] * 2, sums, own)
-    return (residual, new_codebook[None], pq_error[None])
+    return (residual, new_codebook[None], pq_error)
 
 
 def solution(mesh):

time: 110 us -> 109 us (level)
  the two profiles are of different devices: /device:TPU:6 before, /device:TPU:34 now
where the time goes in v7:
time: 109 us
  starting transfers between devices  59 us (54%)
  Pallas kernels  18.3 us (17%)
  waiting for transfers between devices  17.8 us (16%)
  local copies, waits for them, and re-layouts  10.1 us (9%)
  matrix products  2.51 us (2%)
    all_to_all x4, starting transfers between devices, exchange(): return lax.all_to_all(parts, axis, 0, 0, tiled=True)  36 us
    pallas_call x10, Pallas kernels, call(): pl.pallas_call(kernel, out_shape=out_shape, in_specs=ins, out_specs=outs...  18.3 us
    all_to_all x4, waiting for transfers between devices, exchange(): return lax.all_to_all(parts, axis, 0, 0, tiled=True)  10.8 us
    ppermute x3, starting transfers between devices, local(): lax.ppermute(block, 'y', ring(y_count, step))  10.6 us
    ppermute x3, starting transfers between devices, local(): lax.ppermute(block, 'x', ring(x_count, step))  10.5 us
    unnamed x26, local copies, waits for them, and re-layouts  8.65 us
    ppermute x3, waiting for transfers between devices, local(): lax.ppermute(block, 'x', ring(x_count, step))  3.84 us
    ppermute x3, waiting for transfers between devices, local(): lax.ppermute(block, 'y', ring(y_count, step))  3.12 us
  transfers between devices with their start and end apart: 11, of which 6 were waited for; matrix products, arithmetic and copies ran while one was open for 2% of the time, Pallas kernels for 10%

profile of v7, /device:TPU:34, one launch (start us, length us, event | category | flops | bytes accessed | tf_op | source)
XLA Modules:
  0.0 108.5 jit_solution(11326836699456987283)
XLA Ops:
  0.6 1.5 %broadcast_in_dim.6 = bf16[16,64,128]{2,1,0:T(8,128)(2,1)} broadcast(bf16[64,128]{1,0:T(8,128)(2,1)} %bitcast.15), dimensions={1,2} | broadcast | bytes 278528 | tf_op jit(solution)/shard_map/broadcast_in_dim | solution.py:339
  2.1 15.2 %all-to-all-start = ((bf16[16,64,128]{2,1,0:T(8,128)(2,1)}), bf16[16,64,128]{2,1,0:T(8,128)(2,1)S(1)}, u32[]{:S(2)}, u32[]{:S(2)}) async-start(bf16[16,64,128]{2,1,0:T(8,128)(2,1)} %broadcast_in_dim.6), calls=%async_computation | async-start | bytes 524288 | tf_op jit(solution)/shard_map/all_to_all | solution.py:19
  17.4 2.2 %copy-done = bf16[2048,1024]{1,0:T(8,128)(2,1)S(1)} copy-done((bf16[2048,1024]{1,0:T(8,128)(2,1)S(1)}, bf16[2048,1024]{1,0:T(8,128)(2,1)}, u32[]{:S(2)}) %copy-start) | copy-done | bytes 4194328
  19.6 1.1 %copy-done.4 = bf16[384,1024]{1,0:T(8,128)(2,1)S(1)} copy-done((bf16[384,1024]{1,0:T(8,128)(2,1)S(1)}, bf16[384,1024]{1,0:T(8,128)(2,1)}, u32[]{:S(2)}) %copy-start.4) | copy-done | bytes 786456
  20.7 5.2 %shard_map.58 = (bf16[528,384]{1,0:T(8,128)(2,1)S(1)}, f32[8,384]{1,0:T(8,128)S(1)}, bf16[384,2048]{1,0:T(8,128)(2,1)S(1)}, f32[384,128]{1,0:T(8,128)S(1)}) custom-call(s32[3]{0:T(128)S(1)} %pad_add_fusion.place_ref, bf16[384,1024]{1,0:T(8,128)(2,1)S(1)} %copy-done.4, bf16[2048,1024]{1,0:T(8,128)(2,1)S(1)} %copy-done), custom_call_target="tpu_custom_call" | custom-call | flops 1 | bytes 1 | tf_op jit(solution)/shard_map/pallas_call | solution.py:270
  25.9 1.9 %collective-permute-start = (bf16[528,384]{1,0:T(8,128)(2,1)S(1)}, bf16[528,384]{1,0:T(8,128)(2,1)S(1)}, u32[]{:S(2)}, u32[]{:S(2)}) collective-permute-start(bf16[528,384]{1,0:T(8,128)(2,1)S(1)} %get-tuple-element.35), channel_id=1, source_target_pairs={{0,1},{1,0},{2,3},{3,2},{4,5},{5,4},{6,7},{7,6},{8,9},{9,8},{10,11... | collective-permute-start | bytes 1216520 | tf_op jit(solution)/shard_map/ppermute | solution.py:346
  27.9 1.8 %shard_map.59 = (f32[512,384]{1,0:T(8,128)S(1)}, f32[128,384]{1,0:T(8,128)S(1)}) custom-call(s32[3]{0:T(128)S(1)} %pad_add_fusion.place_ref, bf16[384,2048]{1,0:T(8,128)(2,1)S(1)} %get-tuple-element.32.weights_ref, f32[384,128]{1,0:T(8,128)S(1)} %get-tuple-element.33.inverse_ref, bf16[2048,1024]{1,0:T(8,128)(2,1)S(1)} %copy-done, bf16[384,1024]{1,0:T(8,128)(2,1)S(1)} %copy-done.4), custom_call_target="tpu_custom_call" | custom-call | flops 1 | bytes 1 | tf_op jit(solution)/shard_map/pallas_call | solution.py:270
  29.7 0.7 shard_map.60
  30.4 3.4 %collective-permute-start.1 = (bf16[144,384]{1,0:T(8,128)(2,1)S(1)}, bf16[144,384]{1,0:T(8,128)(2,1)S(1)}, u32[]{:S(2)}, u32[]{:S(2)}) collective-permute-start(bf16[144,384]{1,0:T(8,128)(2,1)S(1)} %get-tuple-element.39), channel_id=1, source_target_pairs={{0,2},{2,4},{4,6},{6,0},{1,3},{3,5},{5,7},{7,1},{8,10},{10,12},{12... | collective-permute-start | bytes 331784 | tf_op jit(solution)/shard_map/ppermute | solution.py:348
  33.8 3.0 %collective-permute-start.2 = (bf16[144,384]{1,0:T(8,128)(2,1)S(1)}, bf16[144,384]{1,0:T(8,128)(2,1)S(1)}, u32[]{:S(2)}, u32[]{:S(2)}) collective-permute-start(bf16[144,384]{1,0:T(8,128)(2,1)S(1)} %get-tuple-element.40), channel_id=1, source_target_pairs={{0,4},{2,6},{4,0},{6,2},{1,5},{3,7},{5,1},{7,3},{8,12},{10,14},{12... | collective-permute-start | bytes 331784 | tf_op jit(solution)/shard_map/ppermute | solution.py:348
  36.9 4.1 %collective-permute-start.3 = (bf16[144,384]{1,0:T(8,128)(2,1)S(1)}, bf16[144,384]{1,0:T(8,128)(2,1)S(1)}, u32[]{:S(2)}, u32[]{:S(2)}) collective-permute-start(bf16[144,384]{1,0:T(8,128)(2,1)S(1)} %get-tuple-element.41), channel_id=1, source_target_pairs={{0,6},{2,0},{4,2},{6,4},{1,7},{3,1},{5,3},{7,5},{8,14},{10,8},{12,... | collective-permute-start | bytes 331784 | tf_op jit(solution)/shard_map/ppermute | solution.py:348
  41.0 1.9 %collective-permute-done.2.refs_1_ = bf16[144,384]{1,0:T(8,128)(2,1)S(1)} collective-permute-done((bf16[144,384]{1,0:T(8,128)(2,1)S(1)}, bf16[144,384]{1,0:T(8,128)(2,1)S(1)}, u32[]{:S(2)}, u32[]{:S(2)}) %collective-permute-start.2) | collective-permute-done | bytes 110624 | tf_op jit(solution)/shard_map/ppermute | solution.py:348
  42.8 2.0 %collective-permute-done.3.refs_2_ = bf16[144,384]{1,0:T(8,128)(2,1)S(1)} collective-permute-done((bf16[144,384]{1,0:T(8,128)(2,1)S(1)}, bf16[144,384]{1,0:T(8,128)(2,1)S(1)}, u32[]{:S(2)}, u32[]{:S(2)}) %collective-permute-start.3) | collective-permute-done | bytes 110624 | tf_op jit(solution)/shard_map/ppermute | solution.py:348
  44.8 0.9 shard_map.61
  45.7 4.5 %all-to-all-start.1 = ((bf16[4,128,384]{2,1,0:T(8,128)(2,1)}), bf16[4,128,384]{2,1,0:T(8,128)(2,1)S(1)}, u32[]{:S(2)}, u32[]{:S(2)}) async-start(bf16[4,128,384]{2,1,0:T(8,128)(2,1)} %get-tuple-element.46), calls=%async_computation.1 | async-start | bytes 786432 | tf_op jit(solution)/shard_map/all_to_all | solution.py:19
  50.4 8.0 %all-to-all-done.1.rows_ref = bf16[4,128,384]{2,1,0:T(8,128)(2,1)S(1)} async-done(((bf16[4,128,384]{2,1,0:T(8,128)(2,1)}), bf16[4,128,384]{2,1,0:T(8,128)(2,1)S(1)}, u32[]{:S(2)}, u32[]{:S(2)}) %all-to-all-start.1) | async-done | bytes 393248 | tf_op jit(solution)/shard_map/all_to_all | solution.py:19
  58.4 3.4 %shard_map.63 = (bf16[4,1024,384]{2,1,0:T(8,128)(2,1)}, bf16[4,64,384]{2,1,0:T(8,128)(2,1)S(1)}, f32[8,1536]{1,0:T(8,128)S(1)}) custom-call(bf16[1024,128]{1,0:T(8,128)(2,1)S(1)} %bitcast.13, f32[1024,128]{1,0:T(8,128)S(1)} %shard_map.62.half_ref, bf16[4,128,384]{2,1,0:T(8,128)(2,1)S(1)} %all-to-all-done.1.rows_ref), custom_call_target="tpu_custom_call" | custom-call | flops 1 | bytes 1 | tf_op jit(solution)/shard_map/pallas_call | solution.py:270
  61.8 0.7 copy-done.2
  63.2 4.3 %all-to-all-start.2 = ((bf16[4,64,384]{2,1,0:T(8,128)(2,1)}), bf16[4,64,384]{2,1,0:T(8,128)(2,1)}, u32[]{:S(2)}, u32[]{:S(2)}) async-start(bf16[4,64,384]{2,1,0:T(8,128)(2,1)} %copy-done.5), calls=%async_computation.2 | async-start | bytes 393216 | tf_op jit(solution)/shard_map/all_to_all | solution.py:19
  67.5 2.5 %convolution_bitcast_fusion.rebuilt_ref = f32[4,128,384]{2,1,0:T(8,128)S(1)} fusion(bf16[4,1024,384]{2,1,0:T(8,128)(2,1)} %get-tuple-element.50.raised_ref, bf16[1024,128]{1,0:T(8,128)(2,1)S(1)} %bitcast.14), kind=kOutput, calls=%fused_computation | convolution fusion | flops 402653184 | bytes 4194304 | tf_op jit(solution)/shard_map/kd,pkr->pdr/dot_general | solution.py:385
  72.6 1.2 %all-to-all-done.2.stats_ref = bf16[4,64,384]{2,1,0:T(8,128)(2,1)} async-done(((bf16[4,64,384]{2,1,0:T(8,128)(2,1)}), bf16[4,64,384]{2,1,0:T(8,128)(2,1)}, u32[]{:S(2)}, u32[]{:S(2)}) %all-to-all-start.2) | async-done | bytes 196640 | tf_op jit(solution)/shard_map/all_to_all | solution.py:19
  73.9 1.0 copy-done.3
  74.9 2.9 %shard_map.65 = bf16[16,72,128]{2,1,0:T(8,128)(2,1)} custom-call(bf16[4,64,384]{2,1,0:T(8,128)(2,1)} %all-to-all-done.2.stats_ref, f32[8,1536]{1,0:T(8,128)S(1)} %get-tuple-element.51.stats_ref.own_ref, bf16[4,128,384]{2,1,0:T(8,128)(2,1)S(1)} %copy-done.3, bf16[4,1024,384]{2,1,0:T(8,128)(2,1)S(1)} %copy-done.1), custom_call_target="tpu_custom_call" | custom-call | flops 1 | bytes 1 | tf_op jit(solution)/shard_map/pallas_call | solution.py:270
  77.8 12.0 %all-to-all-start.3 = ((bf16[16,72,128]{2,1,0:T(8,128)(2,1)}), bf16[16,72,128]{2,1,0:T(8,128)(2,1)S(1)}, u32[]{:S(2)}, u32[]{:S(2)}) async-start(bf16[16,72,128]{2,1,0:T(8,128)(2,1)} %shard_map.65), calls=%async_computation.3 | async-start | bytes 589824 | tf_op jit(solution)/shard_map/all_to_all | solution.py:19
  89.8 2.6 %collective-permute-start.4 = (bf16[128,384]{1,0:T(8,128)(2,1)}, bf16[128,384]{1,0:T(8,128)(2,1)S(1)}, u32[]{:S(2)}, u32[]{:S(2)}) collective-permute-start(bf16[128,384]{1,0:T(8,128)(2,1)} %copy-done.12), channel_id=1, source_target_pairs={{0,128},{128,256},{256,384},{384,0},{1,129},{129,257},{257,385},{3... | collective-permute-start | bytes 294920 | tf_op jit(solution)/shard_map/ppermute | solution.py:408
  92.5 4.6 %collective-permute-start.5 = (bf16[128,384]{1,0:T(8,128)(2,1)S(1)}, bf16[128,384]{1,0:T(8,128)(2,1)S(1)}, u32[]{:S(2)}, u32[]{:S(2)}) collective-permute-start(bf16[128,384]{1,0:T(8,128)(2,1)S(1)} %get-tuple-element.59), channel_id=1, source_target_pairs={{0,256},{128,384},{256,0},{384,128},{1,257},{129,385},{257,1},{385... | collective-permute-start | bytes 294920 | tf_op jit(solution)/shard_map/ppermute | solution.py:408
  97.1 3.4 %collective-permute-start.6 = (bf16[128,384]{1,0:T(8,128)(2,1)S(1)}, bf16[128,384]{1,0:T(8,128)(2,1)S(1)}, u32[]{:S(2)}, u32[]{:S(2)}) collective-permute-start(bf16[128,384]{1,0:T(8,128)(2,1)S(1)} %get-tuple-element.60), channel_id=1, source_target_pairs={{0,384},{128,0},{256,128},{384,256},{1,385},{129,1},{257,129},{385... | collective-permute-start | bytes 294920 | tf_op jit(solution)/shard_map/ppermute | solution.py:408
  100.5 3.1 %collective-permute-done.6.refs_2_ = bf16[128,384]{1,0:T(8,128)(2,1)S(1)} collective-permute-done((bf16[128,384]{1,0:T(8,128)(2,1)S(1)}, bf16[128,384]{1,0:T(8,128)(2,1)S(1)}, u32[]{:S(2)}, u32[]{:S(2)}) %collective-permute-start.6) | collective-permute-done | bytes 98336 | tf_op jit(solution)/shard_map/ppermute | solution.py:408
  103.6 0.9 copy-done.7
  104.5 1.7 %shard_map.67 = f32[1,384]{1,0:T(1,128)} custom-call(s32[3]{0:T(128)S(1)} %copy-done.11, bf16[4,64,384]{2,1,0:T(8,128)(2,1)} %all-to-all-done.2.stats_ref, bf16[128,384]{1,0:T(8,128)(2,1)S(1)} %copy-done.8, f32[128,384]{1,0:T(8,128)S(1)} %copy-done.7, bf16[128,384]{1,0:T(8,128)(2,1)S(1)} %collective-permute-done.4.refs_0_, ...), custom_call_target="tpu_custom_call" | custom-call | flops 1 | bytes 1 | tf_op jit(solution)/shard_map/pallas_call | solution.py:270
  106.2 1.6 %all-to-all-done.3.sums_ref = bf16[16,72,128]{2,1,0:T(8,128)(2,1)S(1)} async-done(((bf16[16,72,128]{2,1,0:T(8,128)(2,1)}), bf16[16,72,128]{2,1,0:T(8,128)(2,1)S(1)}, u32[]{:S(2)}, u32[]{:S(2)}) %all-to-all-start.3) | async-done | bytes 294944 | tf_op jit(solution)/shard_map/all_to_all | solution.py:19
  107.7 0.8 shard_map.66
  (29 shorter events, 3.6 us)
Async XLA Ops:
  2.1 43.6 %all-to-all-start = ((bf16[16,64,128]{2,1,0:T(8,128)(2,1)}), bf16[16,64,128]{2,1,0:T(8,128)(2,1)S(1)}, u32[]{:S(2)}, u32[]{:S(2)}) async-start(bf16[16,64,128]{2,1,0:T(8,128)(2,1)} %broadcast_in_dim.6), calls=%async_computation | async-start | bytes 524288 | tf_op jit(solution)/shard_map/all_to_all | solution.py:19
  17.4 2.2 %copy-start = (bf16[2048,1024]{1,0:T(8,128)(2,1)S(1)}, bf16[2048,1024]{1,0:T(8,128)(2,1)}, u32[]{:S(2)}) copy-start(bf16[2048,1024]{1,0:T(8,128)(2,1)} %c_ref.3) | copy-start | bytes 12582916
  19.6 1.1 %copy-start.4 = (bf16[384,1024]{1,0:T(8,128)(2,1)S(1)}, bf16[384,1024]{1,0:T(8,128)(2,1)}, u32[]{:S(2)}) copy-start(bf16[384,1024]{1,0:T(8,128)(2,1)} %e_ref.3) | copy-start | bytes 2359300
  20.7 9.0 %copy-start.10 = (s32[3]{0:T(128)}, s32[3]{0:T(128)S(1)}, u32[]{:S(2)}) copy-start(s32[3]{0:T(128)S(1)} %pad_add_fusion.place_ref) | copy-start | bytes 40
  25.9 3.8 %collective-permute-start = (bf16[528,384]{1,0:T(8,128)(2,1)S(1)}, bf16[528,384]{1,0:T(8,128)(2,1)S(1)}, u32[]{:S(2)}, u32[]{:S(2)}) collective-permute-start(bf16[528,384]{1,0:T(8,128)(2,1)S(1)} %get-tuple-element.35), channel_id=1, source_target_pairs={{0,1},{1,0},{2,3},{3,2},{4,5},{5,4},{6,7},{7,6},{8,9},{9,8},{10,11... | collective-permute-start | bytes 1216520 | tf_op jit(solution)/shard_map/ppermute | solution.py:346
  30.4 10.5 %collective-permute-start.1 = (bf16[144,384]{1,0:T(8,128)(2,1)S(1)}, bf16[144,384]{1,0:T(8,128)(2,1)S(1)}, u32[]{:S(2)}, u32[]{:S(2)}) collective-permute-start(bf16[144,384]{1,0:T(8,128)(2,1)S(1)} %get-tuple-element.39), channel_id=1, source_target_pairs={{0,2},{2,4},{4,6},{6,0},{1,3},{3,5},{5,7},{7,1},{8,10},{10,12},{12... | collective-permute-start | bytes 331784 | tf_op jit(solution)/shard_map/ppermute | solution.py:348
  33.8 9.0 %collective-permute-start.2 = (bf16[144,384]{1,0:T(8,128)(2,1)S(1)}, bf16[144,384]{1,0:T(8,128)(2,1)S(1)}, u32[]{:S(2)}, u32[]{:S(2)}) collective-permute-start(bf16[144,384]{1,0:T(8,128)(2,1)S(1)} %get-tuple-element.40), channel_id=1, source_target_pairs={{0,4},{2,6},{4,0},{6,2},{1,5},{3,7},{5,1},{7,3},{8,12},{10,14},{12... | collective-permute-start | bytes 331784 | tf_op jit(solution)/shard_map/ppermute | solution.py:348
  36.9 7.9 %collective-permute-start.3 = (bf16[144,384]{1,0:T(8,128)(2,1)S(1)}, bf16[144,384]{1,0:T(8,128)(2,1)S(1)}, u32[]{:S(2)}, u32[]{:S(2)}) collective-permute-start(bf16[144,384]{1,0:T(8,128)(2,1)S(1)} %get-tuple-element.41), channel_id=1, source_target_pairs={{0,6},{2,0},{4,2},{6,4},{1,7},{3,1},{5,3},{7,5},{8,14},{10,8},{12,... | collective-permute-start | bytes 331784 | tf_op jit(solution)/shard_map/ppermute | solution.py:348
  45.7 12.7 %all-to-all-start.1 = ((bf16[4,128,384]{2,1,0:T(8,128)(2,1)}), bf16[4,128,384]{2,1,0:T(8,128)(2,1)S(1)}, u32[]{:S(2)}, u32[]{:S(2)}) async-start(bf16[4,128,384]{2,1,0:T(8,128)(2,1)} %get-tuple-element.46), calls=%async_computation.1 | async-start | bytes 786432 | tf_op jit(solution)/shard_map/all_to_all | solution.py:19
  61.8 0.7 copy-start.2
  62.6 0.7 copy-start.5
  63.2 10.7 %copy-start.1 = (bf16[4,1024,384]{2,1,0:T(8,128)(2,1)S(1)}, bf16[4,1024,384]{2,1,0:T(8,128)(2,1)}, u32[]{:S(2)}) copy-start(bf16[4,1024,384]{2,1,0:T(8,128)(2,1)} %get-tuple-element.50.raised_ref) | copy-start | bytes 9437188
  63.2 10.7 %all-to-all-start.2 = ((bf16[4,64,384]{2,1,0:T(8,128)(2,1)}), bf16[4,64,384]{2,1,0:T(8,128)(2,1)}, u32[]{:S(2)}, u32[]{:S(2)}) async-start(bf16[4,64,384]{2,1,0:T(8,128)(2,1)} %copy-done.5), calls=%async_computation.2 | async-start | bytes 393216 | tf_op jit(solution)/shard_map/all_to_all | solution.py:19
  70.0 33.6 %copy-start.8 = (bf16[128,384]{1,0:T(8,128)(2,1)S(1)}, bf16[128,384]{1,0:T(8,128)(2,1)}, u32[]{:S(2)}) copy-start(bf16[128,384]{1,0:T(8,128)(2,1)} %get-tuple-element.29.residual_ref) | copy-start | bytes 294916
  70.0 0.7 copy-start.11
  70.7 37.0 %copy-start.9 = (bf16[1,64,128]{2,1,0:T(8,128)(2,1)S(1)}, bf16[1,64,128]{2,1,0:T(8,128)(2,1)}, u32[]{:S(2)}) copy-start(bf16[1,64,128]{2,1,0:T(8,128)(2,1)} %param.5) | copy-start | bytes 49156
  71.3 0.7 copy-start.6
  72.0 0.6 copy-start.12
  73.9 1.0 copy-start.3
  77.8 29.9 %all-to-all-start.3 = ((bf16[16,72,128]{2,1,0:T(8,128)(2,1)}), bf16[16,72,128]{2,1,0:T(8,128)(2,1)S(1)}, u32[]{:S(2)}, u32[]{:S(2)}) async-start(bf16[16,72,128]{2,1,0:T(8,128)(2,1)} %shard_map.65), calls=%async_computation.3 | async-start | bytes 589824 | tf_op jit(solution)/shard_map/all_to_all | solution.py:19
  89.8 10.6 %collective-permute-start.4 = (bf16[128,384]{1,0:T(8,128)(2,1)}, bf16[128,384]{1,0:T(8,128)(2,1)S(1)}, u32[]{:S(2)}, u32[]{:S(2)}) collective-permute-start(bf16[128,384]{1,0:T(8,128)(2,1)} %copy-done.12), channel_id=1, source_target_pairs={{0,128},{128,256},{256,384},{384,0},{1,129},{129,257},{257,385},{3... | collective-permute-start | bytes 294920 | tf_op jit(solution)/shard_map/ppermute | solution.py:408
  92.5 8.0 %collective-permute-start.5 = (bf16[128,384]{1,0:T(8,128)(2,1)S(1)}, bf16[128,384]{1,0:T(8,128)(2,1)S(1)}, u32[]{:S(2)}, u32[]{:S(2)}) collective-permute-start(bf16[128,384]{1,0:T(8,128)(2,1)S(1)} %get-tuple-element.59), channel_id=1, source_target_pairs={{0,256},{128,384},{256,0},{384,128},{1,257},{129,385},{257,1},{385... | collective-permute-start | bytes 294920 | tf_op jit(solution)/shard_map/ppermute | solution.py:408
  97.1 6.5 %collective-permute-start.6 = (bf16[128,384]{1,0:T(8,128)(2,1)S(1)}, bf16[128,384]{1,0:T(8,128)(2,1)S(1)}, u32[]{:S(2)}, u32[]{:S(2)}) collective-permute-start(bf16[128,384]{1,0:T(8,128)(2,1)S(1)} %get-tuple-element.60), channel_id=1, source_target_pairs={{0,384},{128,0},{256,128},{384,256},{1,385},{129,1},{257,129},{385... | collective-permute-start | bytes 294920 | tf_op jit(solution)/shard_map/ppermute | solution.py:408
  103.6 0.9 copy-start.7

commit v8 on v4

--- a/solution.py
+++ b/solution.py
@@ -142,32 +142,26 @@
     residual = (base_ref[...] - mean).astype(jnp.bfloat16)
     residual_ref[...] = residual
 
-    chunk = 512
-
-    def score(j, peak):
-        at = pl.ds(pl.multiple_of(j * chunk, chunk), chunk)
+    spans = [slice(at, at + 256) for at in range(0, words, 256)]
+    peak = jnp.full((8, rows), -jnp.inf, jnp.float32)
+    for at in spans:
         block = book_ref[at, :]
         wide = block.astype(jnp.float32)
         half = 0.5 * jnp.sum(wide * wide, axis=1, keepdims=True)
         gap = jnp.dot(block, residual, preferred_element_type=jnp.float32) - half
         gaps_ref[at, :] = gap
-        return jnp.maximum(peak, jnp.max(gap.reshape(chunk // 8, 8, rows), axis=0))
-
-    peak = lax.fori_loop(0, words // chunk, score, jnp.full((8, rows), -jnp.inf, jnp.float32), unroll=2)
+        peak = jnp.maximum(peak, jnp.max(gap.reshape(32, 8, rows), axis=0))
     peak = jnp.max(peak, axis=0, keepdims=True)
-
-    def store(j):
-        at = pl.ds(pl.multiple_of(j * chunk, chunk), chunk)
-        return pltpu.make_async_copy(raised_ref.at[at, :], raised_hbm.at[at, :], sems.at[j])
-
-    def raise_(j, total):
-        at = pl.ds(pl.multiple_of(j * chunk, chunk), chunk)
+    total = jnp.zeros((8, rows), jnp.float32)
+    stores = []
+    for j, at in enumerate(spans):
         raised = jnp.exp((gaps_ref[at, :] - peak) * scale)
         raised_ref[at, :] = raised.astype(jnp.bfloat16)
-        store(j).start()
-        return total + jnp.sum(raised.reshape(chunk // 8, 8, rows), axis=0)
-
-    total = lax.fori_loop(0, words // chunk, raise_, jnp.zeros((8, rows), jnp.float32), unroll=2)
+        total = total + jnp.sum(raised.reshape(32, 8, rows), axis=0)
+        if j % 4 == 3:
+            at = slice((j - 3) * 256, (j + 1) * 256)
+            stores.append(pltpu.make_async_copy(raised_ref.at[at, :], raised_hbm.at[at, :], sems.at[j // 4]))
+            stores[-1].start()
     inverse = 1.0 / jnp.sum(total, axis=0, keepdims=True)
     inverse_ref[...] = jnp.broadcast_to(inverse, inverse_ref.shape)
 
@@ -176,26 +170,21 @@
     sides = jnp.transpose(jnp.concatenate([scaled, high, low], axis=0)).astype(jnp.bfloat16)
     row = lax.broadcasted_iota(jnp.int32, (128, 128), 0)
     diagonal = row == lax.broadcasted_iota(jnp.int32, (128, 128), 1)
-
-    def add(j, _):
-        at = pl.ds(pl.multiple_of(j * quarter, quarter), quarter)
-        sums = jnp.dot(raised_ref[at, :], sides, preferred_element_type=jnp.float32)
-        sums_ref[j, :quarter, :] = sums[:, :sub].astype(jnp.bfloat16)
-        counts = sums[:, sub:]
-        counts = counts + pltpu.roll(counts, sub // 2, 1)
-        counts = jnp.concatenate(
-            [
-                jnp.sum(jnp.where(diagonal, counts[k * 128 : k * 128 + 128], 0.0), axis=0, keepdims=True)
-                for k in range(quarter // 128)
-            ],
-            axis=0,
-        )
-        sums_ref[j, quarter:, :] = jnp.concatenate(terms_of(counts, 2), axis=0).astype(jnp.bfloat16)
-        return 0
-
-    lax.fori_loop(0, parts, add, 0)
-    for j in range(words // chunk):
-        store(j).wait()
+    for part in range(parts):
+        lines = []
+        for at in range(0, quarter, 256):
+            span = slice(part * quarter + at, part * quarter + at + 256)
+            sums = jnp.dot(raised_ref[span, :], sides, preferred_element_type=jnp.float32)
+            sums_ref[part, at : at + 256, :] = sums[:, :sub].astype(jnp.bfloat16)
+            counts = sums[:, sub:]
+            counts = counts + pltpu.roll(counts, sub // 2, 1)
+            for k in range(2):
+                tile = counts[k * 128 : k * 128 + 128]
+                lines.append(jnp.sum(jnp.where(diagonal, tile, 0.0), axis=0, keepdims=True))
+        counts = jnp.concatenate(lines, axis=0)
+        sums_ref[part, quarter:, :] = jnp.concatenate(terms_of(counts, 2), axis=0).astype(jnp.bfloat16)
+    for store in stores:
+        store.wait()
 
 
 def middle_kernel(sums_ref, out_ref):
@@ -324,7 +313,7 @@
         scratch=[
             pltpu.VMEM((words, rows), jnp.float32),
             pltpu.VMEM((words, rows), jnp.bfloat16),
-            pltpu.SemaphoreType.DMA((words // 512,)),
+            pltpu.SemaphoreType.DMA((parts,)),
         ],
         mib=51,
     )
@@ -342,8 +331,8 @@
 
     kept, sent, stats, base = coarse(embeddings, centroids, place)
     got = lax.ppermute(sent, "c", [(0, 1), (1, 0)])
-    book, got, kept = lax.optimization_barrier((book, got, kept))
     mean, stats, *blocks = chip(place, kept, got, stats)
+    book, *blocks = lax.optimization_barrier((book, *blocks))
     gots = [
         lax.ppermute(block, "x", [(i, (i + step) % x_count) for i in range(x_count)])
         for step, block in enumerate(blocks, 1)

time: 108 us -> 107 us (level)
  blocking collectives: 26.9 us -> 28.9 us
  Pallas kernels: 15.3 us -> 13.9 us
    all_to_all x1, blocking collectives: 26.9 us -> 28.9 us  [exchange(): return lax.all_to_all(parts, axis, 0, 0, tiled=True)]
    pallas_call x6, Pallas kernels: 15.3 us -> 13.9 us  [call(): pl.pallas_call(kernel, out_shape=out_shape, in_specs=ins, out_specs=outs...]
where the time goes in v8:
time: 107 us
  starting transfers between devices  35 us (33%)
  blocking collectives  28.9 us (27%)
  waiting for transfers between devices  18.9 us (18%)
  Pallas kernels  13.9 us (13%)
  local copies, waits for them, and re-layouts  6.49 us (6%)
  matrix products  2.65 us (2%)
    all_to_all x1, blocking collectives, exchange(): return lax.all_to_all(parts, axis, 0, 0, tiled=True)  28.9 us
    all_to_all x3, starting transfers between devices, exchange(): return lax.all_to_all(parts, axis, 0, 0, tiled=True)  24.5 us
    pallas_call x6, Pallas kernels, call(): pl.pallas_call(kernel, out_shape=out_shape, in_specs=ins, out_specs=outs...  13.9 us
    all_to_all x3, waiting for transfers between devices, exchange(): return lax.all_to_all(parts, axis, 0, 0, tiled=True)  12.9 us
    ppermute x3, starting transfers between devices, local(): lax.ppermute(block, 'x', [(i, (i + step) % x_count) for i in range(x_coun...  8.62 us
    ppermute x3, waiting for transfers between devices, local(): lax.ppermute(block, 'x', [(i, (i + step) % x_count) for i in range(x_coun...  5.92 us
    unnamed x6, local copies, waits for them, and re-layouts  3.32 us
    dot_general x1, matrix products, local(): lax.dot_general(book, raised, (((0,), (0,)), ((), ())), preferred_element...  2.65 us
  transfers between devices with their start and end apart: 7, of which 4 were waited for; matrix products, arithmetic and copies ran while one was open for 3% of the time, Pallas kernels for 7%

profile of v8, /device:TPU:6, one launch (start us, length us, event | category | flops | bytes accessed | tf_op | source)
XLA Modules:
  0.0 106.7 jit_solution(10233984657928491787)
XLA Ops:
  0.6 1.5 %broadcast_in_dim.10 = bf16[16,64,128]{2,1,0:T(8,128)(2,1)} broadcast(bf16[64,128]{1,0:T(8,128)(2,1)} %bitcast.10), dimensions={1,2} | broadcast | bytes 278528 | tf_op jit(solution)/shard_map/broadcast_in_dim | solution.py:329
  2.1 15.2 %all-to-all-start = ((bf16[16,64,128]{2,1,0:T(8,128)(2,1)}), bf16[16,64,128]{2,1,0:T(8,128)(2,1)S(1)}, u32[]{:S(2)}, u32[]{:S(2)}) async-start(bf16[16,64,128]{2,1,0:T(8,128)(2,1)} %broadcast_in_dim.10), calls=%async_computation | async-start | bytes 524288 | tf_op jit(solution)/shard_map/all_to_all | solution.py:19
  17.3 0.1 pad_add_fusion.place_ref
  17.4 0.0 copy-start
  17.4 2.2 %copy-done = bf16[2048,1024]{1,0:T(8,128)(2,1)S(1)} copy-done((bf16[2048,1024]{1,0:T(8,128)(2,1)S(1)}, bf16[2048,1024]{1,0:T(8,128)(2,1)}, u32[]{:S(2)}) %copy-start) | copy-done | bytes 4194328
  19.6 0.0 copy-start.1
  19.6 1.1 %copy-done.1 = bf16[384,1024]{1,0:T(8,128)(2,1)S(1)} copy-done((bf16[384,1024]{1,0:T(8,128)(2,1)S(1)}, bf16[384,1024]{1,0:T(8,128)(2,1)}, u32[]{:S(2)}) %copy-start.1) | copy-done | bytes 786456
  20.7 5.2 %shard_map.58 = (bf16[528,384]{1,0:T(8,128)(2,1)S(1)}, f32[8,384]{1,0:T(8,128)S(1)}, bf16[384,2048]{1,0:T(8,128)(2,1)S(1)}, f32[384,128]{1,0:T(8,128)S(1)}) custom-call(s32[2]{0:T(128)S(1)} %pad_add_fusion.place_ref, bf16[384,1024]{1,0:T(8,128)(2,1)S(1)} %copy-done.1, bf16[2048,1024]{1,0:T(8,128)(2,1)S(1)} %copy-done), custom_call_target="tpu_custom_call" | custom-call | flops 1 | bytes 1 | tf_op jit(solution)/shard_map/pallas_call | solution.py:233
  26.0 1.9 %collective-permute-start = (bf16[528,384]{1,0:T(8,128)(2,1)S(1)}, bf16[528,384]{1,0:T(8,128)(2,1)S(1)}, u32[]{:S(2)}, u32[]{:S(2)}) collective-permute-start(bf16[528,384]{1,0:T(8,128)(2,1)S(1)} %get-tuple-element.27), channel_id=1, source_target_pairs={{0,1},{1,0},{2,3},{3,2},{4,5},{5,4},{6,7},{7,6},{8,9},{9,8},{10,11... | collective-permute-start | bytes 1216520 | tf_op jit(solution)/shard_map/ppermute | solution.py:333
  27.9 1.8 %shard_map.59 = (f32[512,384]{1,0:T(8,128)S(1)}, f32[128,384]{1,0:T(8,128)S(1)}) custom-call(s32[2]{0:T(128)S(1)} %pad_add_fusion.place_ref, bf16[384,2048]{1,0:T(8,128)(2,1)S(1)} %get-tuple-element.24.weights_ref, f32[384,128]{1,0:T(8,128)S(1)} %get-tuple-element.25.inverse_ref, bf16[2048,1024]{1,0:T(8,128)(2,1)S(1)} %copy-done, bf16[384,1024]{1,0:T(8,128)(2,1)S(1)} %copy-done.1), custom_call_target="tpu_custom_call" | custom-call | flops 1 | bytes 1 | tf_op jit(solution)/shard_map/pallas_call | solution.py:233
  29.7 0.0 collective-permute-done.got_ref
  29.7 0.7 shard_map.60
  30.5 5.2 %all-to-all-done = bf16[16,64,128]{2,1,0:T(8,128)(2,1)S(1)} async-done(((bf16[16,64,128]{2,1,0:T(8,128)(2,1)}), bf16[16,64,128]{2,1,0:T(8,128)(2,1)S(1)}, u32[]{:S(2)}, u32[]{:S(2)}) %all-to-all-start) | async-done | bytes 262176 | tf_op jit(solution)/shard_map/all_to_all | solution.py:19
  35.7 1.1 %broadcast_in_dim.11 = bf16[4,1024,128]{2,1,0:T(8,128)(2,1)} broadcast(bf16[1024,128]{1,0:T(8,128)(2,1)S(1)} %bitcast.12), dimensions={1,2} | broadcast | bytes 1310720 | tf_op jit(solution)/shard_map/broadcast_in_dim | solution.py:340
  36.8 4.5 %all-to-all-start.1 = ((bf16[4,1024,128]{2,1,0:T(8,128)(2,1)}), bf16[4,1024,128]{2,1,0:T(8,128)(2,1)S(1)}, u32[]{:S(2)}, u32[]{:S(2)}) async-start(bf16[4,1024,128]{2,1,0:T(8,128)(2,1)} %broadcast_in_dim.11), calls=%async_computation.1 | async-start | bytes 2097152 | tf_op jit(solution)/shard_map/all_to_all | solution.py:19
  41.2 2.4 %collective-permute-start.1 = (bf16[144,384]{1,0:T(8,128)(2,1)S(1)}, bf16[144,384]{1,0:T(8,128)(2,1)S(1)}, u32[]{:S(2)}, u32[]{:S(2)}) collective-permute-start(bf16[144,384]{1,0:T(8,128)(2,1)S(1)} %get-tuple-element.34), channel_id=1, source_target_pairs={{0,2},{2,4},{4,6},{6,0},{1,3},{3,5},{5,7},{7,1},{8,10},{10,12},{12... | collective-permute-start | bytes 331784 | tf_op jit(solution)/shard_map/ppermute | solution.py:337
  43.6 4.3 %collective-permute-start.2 = (bf16[144,384]{1,0:T(8,128)(2,1)S(1)}, bf16[144,384]{1,0:T(8,128)(2,1)S(1)}, u32[]{:S(2)}, u32[]{:S(2)}) collective-permute-start(bf16[144,384]{1,0:T(8,128)(2,1)S(1)} %get-tuple-element.35), channel_id=1, source_target_pairs={{0,4},{2,6},{4,0},{6,2},{1,5},{3,7},{5,1},{7,3},{8,12},{10,14},{12... | collective-permute-start | bytes 331784 | tf_op jit(solution)/shard_map/ppermute | solution.py:337
  48.0 1.9 %collective-permute-start.3 = (bf16[144,384]{1,0:T(8,128)(2,1)S(1)}, bf16[144,384]{1,0:T(8,128)(2,1)S(1)}, u32[]{:S(2)}, u32[]{:S(2)}) collective-permute-start(bf16[144,384]{1,0:T(8,128)(2,1)S(1)} %get-tuple-element.36), channel_id=1, source_target_pairs={{0,6},{2,0},{4,2},{6,4},{1,7},{3,1},{5,3},{7,5},{8,14},{10,8},{12,... | collective-permute-start | bytes 331784 | tf_op jit(solution)/shard_map/ppermute | solution.py:337
  49.9 0.0 collective-permute-done.1.refs_0_
  49.9 1.9 %collective-permute-done.2.refs_1_ = bf16[144,384]{1,0:T(8,128)(2,1)S(1)} collective-permute-done((bf16[144,384]{1,0:T(8,128)(2,1)S(1)}, bf16[144,384]{1,0:T(8,128)(2,1)S(1)}, u32[]{:S(2)}, u32[]{:S(2)}) %collective-permute-start.2) | collective-permute-done | bytes 110624 | tf_op jit(solution)/shard_map/ppermute | solution.py:337
  51.8 4.0 %collective-permute-done.3.refs_2_ = bf16[144,384]{1,0:T(8,128)(2,1)S(1)} collective-permute-done((bf16[144,384]{1,0:T(8,128)(2,1)S(1)}, bf16[144,384]{1,0:T(8,128)(2,1)S(1)}, u32[]{:S(2)}, u32[]{:S(2)}) %collective-permute-start.3) | collective-permute-done | bytes 110624 | tf_op jit(solution)/shard_map/ppermute | solution.py:337
  55.8 0.0 all-to-all-done.1
  55.8 5.2 %shard_map.61 = (bf16[128,384]{1,0:T(8,128)(2,1)}, bf16[4,1040,128]{2,1,0:T(8,128)(2,1)}, bf16[4096,384]{1,0:T(8,128)(2,1)}, f32[8,384]{1,0:T(8,128)S(1)}) custom-call(f32[128,384]{1,0:T(8,128)S(1)} %get-tuple-element.29.mean_ref, f32[8,384]{1,0:T(8,128)S(1)} %get-tuple-element.30.chip_ref, bf16[144,384]{1,0:T(8,128)(2,1)S(1)} %collective-permute-done.1.refs_0_, ...), custom_call_target="tpu_custom_call" | custom-call | flops 1 | bytes 1 | tf_op jit(solution)/shard_map/pallas_call | solution.py:233
  61.0 4.8 %all-to-all-start.2 = ((bf16[4,1040,128]{2,1,0:T(8,128)(2,1)}), bf16[4,1040,128]{2,1,0:T(8,128)(2,1)S(1)}, u32[]{:S(2)}, u32[]{:S(2)}) async-start(bf16[4,1040,128]{2,1,0:T(8,128)(2,1)} %get-tuple-element.40), calls=%async_computation.2 | async-start | bytes 2129920 | tf_op jit(solution)/shard_map/all_to_all | solution.py:19
  65.8 0.0 copy-start.2
  65.9 2.7 %multiply_reduce_fusion = f32[384]{0:T(512)S(1)} fusion(bf16[128,384]{1,0:T(8,128)(2,1)} %get-tuple-element.21, f32[384]{0:T(512)S(1)} %slice_reduce_fusion, bf16[4096,128]{1,0:T(8,128)(2,1)S(1)} %bitcast.9, bf16[4096,384]{1,0:T(8,128)(2,1)} %get-tuple-element.41), kind=kOutput, calls=%fused_computation.1 | convolution fusion | flops 402898560 | bytes 4295680 | tf_op jit(solution)/shard_map/dot_general | solution.py:344
  68.5 0.6 div.10
  69.1 7.7 %all-to-all-done.2.sums_ref = bf16[4,1040,128]{2,1,0:T(8,128)(2,1)S(1)} async-done(((bf16[4,1040,128]{2,1,0:T(8,128)(2,1)}), bf16[4,1040,128]{2,1,0:T(8,128)(2,1)S(1)}, u32[]{:S(2)}, u32[]{:S(2)}) %all-to-all-start.2) | async-done | bytes 1064992 | tf_op jit(solution)/shard_map/all_to_all | solution.py:19
  76.8 0.1 shard_map.62
  77.0 28.9 %all_to_all.20.sums_ref = bf16[16,72,128]{2,1,0:T(8,128)(2,1)S(1)} all-to-all(bf16[16,72,128]{2,1,0:T(8,128)(2,1)S(1)} %shard_map.62), channel_id=1, replica_groups=mesh['y'=4,'z'=16,'x'=4,'c'=2] {'z'}, dimensions={0} | all-to-all | bytes 589824 | tf_op jit(solution)/shard_map/all_to_all | solution.py:19
  105.9 0.0 copy-done.2
  105.9 0.8 shard_map.63
  (2 shorter events, 0.0 us)
Async XLA Ops:
  2.1 33.6 %all-to-all-start = ((bf16[16,64,128]{2,1,0:T(8,128)(2,1)}), bf16[16,64,128]{2,1,0:T(8,128)(2,1)S(1)}, u32[]{:S(2)}, u32[]{:S(2)}) async-start(bf16[16,64,128]{2,1,0:T(8,128)(2,1)} %broadcast_in_dim.10), calls=%async_computation | async-start | bytes 524288 | tf_op jit(solution)/shard_map/all_to_all | solution.py:19
  17.4 2.2 %copy-start = (bf16[2048,1024]{1,0:T(8,128)(2,1)S(1)}, bf16[2048,1024]{1,0:T(8,128)(2,1)}, u32[]{:S(2)}) copy-start(bf16[2048,1024]{1,0:T(8,128)(2,1)} %c_ref.3) | copy-start | bytes 12582916
  19.6 1.1 %copy-start.1 = (bf16[384,1024]{1,0:T(8,128)(2,1)S(1)}, bf16[384,1024]{1,0:T(8,128)(2,1)}, u32[]{:S(2)}) copy-start(bf16[384,1024]{1,0:T(8,128)(2,1)} %e_ref.3) | copy-start | bytes 2359300
  26.0 3.8 %collective-permute-start = (bf16[528,384]{1,0:T(8,128)(2,1)S(1)}, bf16[528,384]{1,0:T(8,128)(2,1)S(1)}, u32[]{:S(2)}, u32[]{:S(2)}) collective-permute-start(bf16[528,384]{1,0:T(8,128)(2,1)S(1)} %get-tuple-element.27), channel_id=1, source_target_pairs={{0,1},{1,0},{2,3},{3,2},{4,5},{5,4},{6,7},{7,6},{8,9},{9,8},{10,11... | collective-permute-start | bytes 1216520 | tf_op jit(solution)/shard_map/ppermute | solution.py:333
  36.8 19.0 %all-to-all-start.1 = ((bf16[4,1024,128]{2,1,0:T(8,128)(2,1)}), bf16[4,1024,128]{2,1,0:T(8,128)(2,1)S(1)}, u32[]{:S(2)}, u32[]{:S(2)}) async-start(bf16[4,1024,128]{2,1,0:T(8,128)(2,1)} %broadcast_in_dim.11), calls=%async_computation.1 | async-start | bytes 2097152 | tf_op jit(solution)/shard_map/all_to_all | solution.py:19
  41.2 8.6 %collective-permute-start.1 = (bf16[144,384]{1,0:T(8,128)(2,1)S(1)}, bf16[144,384]{1,0:T(8,128)(2,1)S(1)}, u32[]{:S(2)}, u32[]{:S(2)}) collective-permute-start(bf16[144,384]{1,0:T(8,128)(2,1)S(1)} %get-tuple-element.34), channel_id=1, source_target_pairs={{0,2},{2,4},{4,6},{6,0},{1,3},{3,5},{5,7},{7,1},{8,10},{10,12},{12... | collective-permute-start | bytes 331784 | tf_op jit(solution)/shard_map/ppermute | solution.py:337
  43.6 8.1 %collective-permute-start.2 = (bf16[144,384]{1,0:T(8,128)(2,1)S(1)}, bf16[144,384]{1,0:T(8,128)(2,1)S(1)}, u32[]{:S(2)}, u32[]{:S(2)}) collective-permute-start(bf16[144,384]{1,0:T(8,128)(2,1)S(1)} %get-tuple-element.35), channel_id=1, source_target_pairs={{0,4},{2,6},{4,0},{6,2},{1,5},{3,7},{5,1},{7,3},{8,12},{10,14},{12... | collective-permute-start | bytes 331784 | tf_op jit(solution)/shard_map/ppermute | solution.py:337
  48.0 7.9 %collective-permute-start.3 = (bf16[144,384]{1,0:T(8,128)(2,1)S(1)}, bf16[144,384]{1,0:T(8,128)(2,1)S(1)}, u32[]{:S(2)}, u32[]{:S(2)}) collective-permute-start(bf16[144,384]{1,0:T(8,128)(2,1)S(1)} %get-tuple-element.36), channel_id=1, source_target_pairs={{0,6},{2,0},{4,2},{6,4},{1,7},{3,1},{5,3},{7,5},{8,14},{10,8},{12,... | collective-permute-start | bytes 331784 | tf_op jit(solution)/shard_map/ppermute | solution.py:337
  61.0 15.8 %all-to-all-start.2 = ((bf16[4,1040,128]{2,1,0:T(8,128)(2,1)}), bf16[4,1040,128]{2,1,0:T(8,128)(2,1)S(1)}, u32[]{:S(2)}, u32[]{:S(2)}) async-start(bf16[4,1040,128]{2,1,0:T(8,128)(2,1)} %get-tuple-element.40), calls=%async_computation.2 | async-start | bytes 2129920 | tf_op jit(solution)/shard_map/all_to_all | solution.py:19
  65.8 40.1 %copy-start.2 = (bf16[1,64,128]{2,1,0:T(8,128)(2,1)S(1)}, bf16[1,64,128]{2,1,0:T(8,128)(2,1)}, u32[]{:S(2)}) copy-start(bf16[1,64,128]{2,1,0:T(8,128)(2,1)} %param.5) | copy-start | bytes 49156

commit v9 on v8

--- a/solution.py
+++ b/solution.py
@@ -23,14 +23,26 @@
     return jnp.transpose(jnp.broadcast_to(columns, (columns.shape[0], 128)))[:1]
 
 
-def coarse_kernel(place_ref, e_ref, c_ref, sent_ref, stats_ref, weights_ref, inverse_ref, logits_ref):
+def coarse_kernel(
+    place_ref, e_hbm, c_hbm, sent_ref, stats_ref, weights_ref, inverse_ref, e_ref, c_ref, logits_ref, e_sem, c_sems
+):
     rows, width = e_ref.shape
     chunks, _, chunk = logits_ref.shape
     used = sent_ref.shape[0] - PACKED
     scale = 2.0 / math.sqrt(width)
-
-    def score(j, peak):
-        block = c_ref[pl.ds(pl.multiple_of(j * chunk, chunk), chunk), :]
+    spans = [slice(j * chunk, j * chunk + chunk) for j in range(chunks)]
+    whole = pltpu.make_async_copy(e_hbm, e_ref, e_sem)
+    whole.start()
+    copies = [
+        pltpu.make_async_copy(c_hbm.at[at, :], c_ref.at[at, :], c_sems.at[j]) for j, at in enumerate(spans)
+    ]
+    for copy in copies:
+        copy.start()
+    whole.wait()
+    peak = jnp.full((rows, 128), -jnp.inf, jnp.float32)
+    for j, at in enumerate(spans):
+        copies[j].wait()
+        block = c_ref[at, :]
         wide = block.astype(jnp.float32)
         half_norm = wide_row(0.5 * jnp.sum(wide * wide, axis=1, keepdims=True))
         products = lax.dot_general(
@@ -40,44 +52,51 @@
         logits_ref[j] = logits
         for part in range(chunk // 128):
             peak = jnp.maximum(peak, logits[:, part * 128 : part * 128 + 128])
-        return peak
-
-    peak = lax.fori_loop(0, chunks, score, jnp.full((rows, 128), -jnp.inf, jnp.float32), unroll=2)
     peak = jnp.max(peak, axis=1, keepdims=True)
-
-    def raise_(j, total):
+    total = jnp.zeros((rows, 128), jnp.float32)
+    for j, at in enumerate(spans):
         shifted = jnp.exp(logits_ref[j] - peak)
-        weights_ref[:, pl.ds(pl.multiple_of(j * chunk, chunk), chunk)] = shifted.astype(jnp.bfloat16)
+        weights_ref[:, at] = shifted.astype(jnp.bfloat16)
         for part in range(chunk // 128):
             total = total + shifted[:, part * 128 : part * 128 + 128]
-        return total
-
-    total = lax.fori_loop(0, chunks, raise_, jnp.zeros((rows, 128), jnp.float32), unroll=2)
     total = jnp.sum(total, axis=1, keepdims=True)
     inverse_ref[...] = jnp.broadcast_to(1.0 / total, inverse_ref.shape)
-    pull(1 - place_ref[0], weights_ref, inverse_ref, c_ref, sent_ref)
+    sub = inverse_ref.shape[1]
+    blocks = [c_ref.at[:, owned(place_ref, 1 - place_ref[0], k, sub)] for k in range(4)]
+    pull(blocks, weights_ref, inverse_ref, sent_ref)
     largest, total = wide_row(peak), wide_row(total)
     stats_ref[...] = jnp.concatenate([largest, total, jnp.zeros((6, rows), jnp.float32)], axis=0)
     sent_ref[used:, :] = packed(largest, total)
 
 
-def pull(core, weights_ref, inverse_ref, c_ref, out_ref):
+def owned(place_ref, core, column, sub):
+    return pl.ds(pl.multiple_of((2 * column + core) * sub, sub), sub)
+
+
+def pull(blocks, weights_ref, inverse_ref, out_ref):
     sub = inverse_ref.shape[1]
-    for pair in range(2):
-        columns = [pl.ds(pl.multiple_of(((2 * pair + k) * 2 + core) * sub, sub), sub) for k in range(2)]
-        block = jnp.concatenate([c_ref[:, column] for column in columns], axis=1)
+    for pair in range(0, len(blocks), 2):
+        block = jnp.concatenate([blocks[pair][...], blocks[pair + 1][...]], axis=1)
         pulled = jnp.dot(weights_ref[...], block, preferred_element_type=jnp.float32)
         for k in range(2):
             part = pulled[:, k * sub : k * sub + sub] * inverse_ref[...]
-            row = (2 * pair + k) * sub
+            row = (pair + k) * sub
             out_ref[row : row + sub, :] = jnp.transpose(part).astype(out_ref.dtype)
 
 
-def kept_kernel(place_ref, weights_ref, inverse_ref, c_ref, e_ref, kept_ref, base_ref):
-    pull(place_ref[0], weights_ref, inverse_ref, c_ref, kept_ref)
+def kept_kernel(place_ref, weights_ref, inverse_ref, c_hbm, e_hbm, kept_ref, base_ref, c_ref, e_ref, sems, e_sem):
     sub = base_ref.shape[0]
-    own = pl.multiple_of((2 * place_ref[1] + place_ref[0]) * sub, sub)
-    base_ref[...] = jnp.transpose(e_ref[:, pl.ds(own, sub)].astype(jnp.float32))
+    core = place_ref[0]
+    copies = [
+        pltpu.make_async_copy(c_hbm.at[:, owned(place_ref, core, k, sub)], c_ref.at[k], sems.at[k]) for k in range(4)
+    ]
+    copies.append(pltpu.make_async_copy(e_hbm.at[:, owned(place_ref, core, place_ref[1], sub)], e_ref, e_sem))
+    for copy in copies:
+        copy.start()
+    for copy in copies:
+        copy.wait()
+    pull([c_ref.at[k] for k in range(4)], weights_ref, inverse_ref, kept_ref)
+    base_ref[...] = jnp.transpose(e_ref[...].astype(jnp.float32))
 
 
 def weigh(maxes, totals):
@@ -249,6 +268,7 @@
     rows, width = embeddings.shape
     count = centroids.shape[0]
     half, sub, chunk = width // 2, 128, 256
+    chunks = count // chunk
     sent, stats, weights, inverse = call(
         coarse_kernel,
         (
@@ -257,23 +277,35 @@
             array((rows, count), jnp.bfloat16),
             array((rows, sub)),
         ),
-        [SMEM, VMEM, VMEM],
+        [SMEM, HBM, HBM],
         place,
         embeddings,
         centroids,
-        scratch=[pltpu.VMEM((count // chunk, rows, chunk), jnp.float32)],
-        mib=24,
+        scratch=[
+            pltpu.VMEM((rows, width), jnp.bfloat16),
+            pltpu.VMEM((count, width), jnp.bfloat16),
+            pltpu.VMEM((chunks, rows, chunk), jnp.float32),
+            pltpu.SemaphoreType.DMA,
+            pltpu.SemaphoreType.DMA((chunks,)),
+        ],
+        mib=56,
     )
     kept, base = call(
         kept_kernel,
         (array((half, rows)), array((sub, rows))),
-        [SMEM] + [VMEM] * 4,
+        [SMEM, VMEM, VMEM, HBM, HBM],
         place,
         weights,
         inverse,
         centroids,
         embeddings,
-        mib=24,
+        scratch=[
+            pltpu.VMEM((4, count, sub), jnp.bfloat16),
+            pltpu.VMEM((rows, sub), jnp.bfloat16),
+            pltpu.SemaphoreType.DMA((4,)),
+            pltpu.SemaphoreType.DMA,
+        ],
+        mib=56,
     )
     return kept, sent, stats, base
 

time: 107 us -> 114 us (1.065)
  Pallas kernels: 13.9 us -> 22.5 us
  local copies, waits for them, and re-layouts: 6.49 us -> 4.33 us
  blocking collectives: 28.9 us -> 30.1 us
  starting transfers between devices: 35 us -> 33.8 us
    pallas_call x6, Pallas kernels: 13.9 us -> 22.5 us  [call(): pl.pallas_call(kernel, out_shape=out_shape, in_specs=ins, out_specs=outs...]
    unnamed x6 -> x10, local copies, waits for them, and re-layouts: 3.32 us -> 1.15 us
    all_to_all x3, starting transfers between devices: 24.5 us -> 23.3 us  [exchange(): return lax.all_to_all(parts, axis, 0, 0, tiled=True)]
    all_to_all x1, blocking collectives: 28.9 us -> 30.1 us  [exchange(): return lax.all_to_all(parts, axis, 0, 0, tiled=True)]
  transfers between devices with their start and end apart: 7 -> 7, of which waited for: 4 -> 4; matrix products, arithmetic and copies ran while one was open for 3% -> 3% of each run, Pallas kernels for 7% -> 14%
where the time goes in v9:
time: 114 us
  starting transfers between devices  33.8 us (30%)
  blocking collectives  30.1 us (26%)
  Pallas kernels  22.5 us (20%)
  waiting for transfers between devices  18.9 us (17%)
  local copies, waits for them, and re-layouts  4.33 us (4%)
  matrix products  2.65 us (2%)
    all_to_all x1, blocking collectives, exchange(): return lax.all_to_all(parts, axis, 0, 0, tiled=True)  30.1 us
    all_to_all x3, starting transfers between devices, exchange(): return lax.all_to_all(parts, axis, 0, 0, tiled=True)  23.3 us
    pallas_call x6, Pallas kernels, call(): pl.pallas_call(kernel, out_shape=out_shape, in_specs=ins, out_specs=outs...  22.5 us
    all_to_all x3, waiting for transfers between devices, exchange(): return lax.all_to_all(parts, axis, 0, 0, tiled=True)  12.9 us
    ppermute x3, starting transfers between devices, local(): lax.ppermute(block, 'x', [(i, (i + step) % x_count) for i in range(x_coun...  8.62 us
    ppermute x3, waiting for transfers between devices, local(): lax.ppermute(block, 'x', [(i, (i + step) % x_count) for i in range(x_coun...  5.92 us
    dot_general x1, matrix products, local(): lax.dot_general(book, raised, (((0,), (0,)), ((), ())), preferred_element...  2.65 us
  transfers between devices with their start and end apart: 7, of which 4 were waited for; matrix products, arithmetic and copies ran while one was open for 3% of the time, Pallas kernels for 14%

profile of v9, /device:TPU:6, one launch (start us, length us, event | category | flops | bytes accessed | tf_op | source)
XLA Modules:
  0.0 113.6 jit_solution(11350413901184049567)
XLA Ops:
  0.6 1.5 %broadcast_in_dim.10 = bf16[16,64,128]{2,1,0:T(8,128)(2,1)} broadcast(bf16[64,128]{1,0:T(8,128)(2,1)} %bitcast.10), dimensions={1,2} | broadcast | bytes 278528 | tf_op jit(solution)/shard_map/broadcast_in_dim | solution.py:361
  2.1 15.2 %all-to-all-start = ((bf16[16,64,128]{2,1,0:T(8,128)(2,1)}), bf16[16,64,128]{2,1,0:T(8,128)(2,1)S(1)}, u32[]{:S(2)}, u32[]{:S(2)}) async-start(bf16[16,64,128]{2,1,0:T(8,128)(2,1)} %broadcast_in_dim.10), calls=%async_computation | async-start | bytes 524288 | tf_op jit(solution)/shard_map/all_to_all | solution.py:19
  17.3 0.6 pad_add_fusion.place_ref
  17.9 10.5 %shard_map.58 = (bf16[528,384]{1,0:T(8,128)(2,1)}, f32[8,384]{1,0:T(8,128)}, bf16[384,2048]{1,0:T(8,128)(2,1)}, f32[384,128]{1,0:T(8,128)}) custom-call(s32[2]{0:T(128)} %pad_add_fusion.place_ref, bf16[384,1024]{1,0:T(8,128)(2,1)} %e_hbm.3, bf16[2048,1024]{1,0:T(8,128)(2,1)} %c_hbm.3), custom_call_target="tpu_custom_call" | custom-call | flops 1 | bytes 1 | tf_op jit(solution)/shard_map/pallas_call | solution.py:252
  28.4 1.9 %collective-permute-start = (bf16[528,384]{1,0:T(8,128)(2,1)}, bf16[528,384]{1,0:T(8,128)(2,1)S(1)}, u32[]{:S(2)}, u32[]{:S(2)}) collective-permute-start(bf16[528,384]{1,0:T(8,128)(2,1)} %get-tuple-element.27), channel_id=1, source_target_pairs={{0,1},{1,0},{2,3},{3,2},{4,5},{5,4},{6,7},{7,6},{8,9},{9,8},{10,11... | collective-permute-start | bytes 1216520 | tf_op jit(solution)/shard_map/ppermute | solution.py:365
  30.3 0.0 copy-start.3
  30.3 0.0 copy-start.4
  30.3 5.2 %shard_map.59 = (f32[512,384]{1,0:T(8,128)}, f32[128,384]{1,0:T(8,128)}) custom-call(s32[2]{0:T(128)} %pad_add_fusion.place_ref, bf16[384,2048]{1,0:T(8,128)(2,1)} %get-tuple-element.24.weights_ref, f32[384,128]{1,0:T(8,128)} %get-tuple-element.25.inverse_ref, bf16[2048,1024]{1,0:T(8,128)(2,1)} %c_hbm.3, bf16[384,1024]{1,0:T(8,128)(2,1)} %e_hbm.3), custom_call_target="tpu_custom_call" | custom-call | flops 1 | bytes 1 | tf_op jit(solution)/shard_map/pallas_call | solution.py:252
  35.5 0.0 collective-permute-done.got_ref
  35.5 0.0 copy-done.3
  35.5 0.0 copy-done.4
  35.5 0.0 copy-start
  35.6 1.1 copy-done
  36.7 0.7 shard_map.60
  37.4 0.0 all-to-all-done
  37.4 1.1 broadcast_in_dim.11
  38.5 4.5 %all-to-all-start.1 = ((bf16[4,1024,128]{2,1,0:T(8,128)(2,1)}), bf16[4,1024,128]{2,1,0:T(8,128)(2,1)S(1)}, u32[]{:S(2)}, u32[]{:S(2)}) async-start(bf16[4,1024,128]{2,1,0:T(8,128)(2,1)} %broadcast_in_dim.11), calls=%async_computation.1 | async-start | bytes 2097152 | tf_op jit(solution)/shard_map/all_to_all | solution.py:19
  43.0 2.4 %collective-permute-start.1 = (bf16[144,384]{1,0:T(8,128)(2,1)S(1)}, bf16[144,384]{1,0:T(8,128)(2,1)S(1)}, u32[]{:S(2)}, u32[]{:S(2)}) collective-permute-start(bf16[144,384]{1,0:T(8,128)(2,1)S(1)} %get-tuple-element.34), channel_id=1, source_target_pairs={{0,2},{2,4},{4,6},{6,0},{1,3},{3,5},{5,7},{7,1},{8,10},{10,12},{12... | collective-permute-start | bytes 331784 | tf_op jit(solution)/shard_map/ppermute | solution.py:369
  45.4 4.3 %collective-permute-start.2 = (bf16[144,384]{1,0:T(8,128)(2,1)S(1)}, bf16[144,384]{1,0:T(8,128)(2,1)S(1)}, u32[]{:S(2)}, u32[]{:S(2)}) collective-permute-start(bf16[144,384]{1,0:T(8,128)(2,1)S(1)} %get-tuple-element.35), channel_id=1, source_target_pairs={{0,4},{2,6},{4,0},{6,2},{1,5},{3,7},{5,1},{7,3},{8,12},{10,14},{12... | collective-permute-start | bytes 331784 | tf_op jit(solution)/shard_map/ppermute | solution.py:369
  49.7 1.9 %collective-permute-start.3 = (bf16[144,384]{1,0:T(8,128)(2,1)S(1)}, bf16[144,384]{1,0:T(8,128)(2,1)S(1)}, u32[]{:S(2)}, u32[]{:S(2)}) collective-permute-start(bf16[144,384]{1,0:T(8,128)(2,1)S(1)} %get-tuple-element.36), channel_id=1, source_target_pairs={{0,6},{2,0},{4,2},{6,4},{1,7},{3,1},{5,3},{7,5},{8,14},{10,8},{12,... | collective-permute-start | bytes 331784 | tf_op jit(solution)/shard_map/ppermute | solution.py:369
  51.6 0.0 collective-permute-done.1.refs_0_
  51.6 2.0 %collective-permute-done.2.refs_1_ = bf16[144,384]{1,0:T(8,128)(2,1)S(1)} collective-permute-done((bf16[144,384]{1,0:T(8,128)(2,1)S(1)}, bf16[144,384]{1,0:T(8,128)(2,1)S(1)}, u32[]{:S(2)}, u32[]{:S(2)}) %collective-permute-start.2) | collective-permute-done | bytes 110624 | tf_op jit(solution)/shard_map/ppermute | solution.py:369
  53.7 3.9 %collective-permute-done.3.refs_2_ = bf16[144,384]{1,0:T(8,128)(2,1)S(1)} collective-permute-done((bf16[144,384]{1,0:T(8,128)(2,1)S(1)}, bf16[144,384]{1,0:T(8,128)(2,1)S(1)}, u32[]{:S(2)}, u32[]{:S(2)}) %collective-permute-start.3) | collective-permute-done | bytes 110624 | tf_op jit(solution)/shard_map/ppermute | solution.py:369
  57.5 1.2 %all-to-all-done.1 = bf16[4,1024,128]{2,1,0:T(8,128)(2,1)S(1)} async-done(((bf16[4,1024,128]{2,1,0:T(8,128)(2,1)}), bf16[4,1024,128]{2,1,0:T(8,128)(2,1)S(1)}, u32[]{:S(2)}, u32[]{:S(2)}) %all-to-all-start.1) | async-done | bytes 1048608 | tf_op jit(solution)/shard_map/all_to_all | solution.py:19
  58.7 5.2 %shard_map.61 = (bf16[128,384]{1,0:T(8,128)(2,1)}, bf16[4,1040,128]{2,1,0:T(8,128)(2,1)}, bf16[4096,384]{1,0:T(8,128)(2,1)}, f32[8,384]{1,0:T(8,128)S(1)}) custom-call(f32[128,384]{1,0:T(8,128)S(1)} %get-tuple-element.29.mean_ref, f32[8,384]{1,0:T(8,128)S(1)} %get-tuple-element.30.chip_ref, bf16[144,384]{1,0:T(8,128)(2,1)S(1)} %collective-permute-done.1.refs_0_, ...), custom_call_target="tpu_custom_call" | custom-call | flops 1 | bytes 1 | tf_op jit(solution)/shard_map/pallas_call | solution.py:252
  64.0 3.6 %all-to-all-start.2 = ((bf16[4,1040,128]{2,1,0:T(8,128)(2,1)}), bf16[4,1040,128]{2,1,0:T(8,128)(2,1)S(1)}, u32[]{:S(2)}, u32[]{:S(2)}) async-start(bf16[4,1040,128]{2,1,0:T(8,128)(2,1)} %get-tuple-element.40), calls=%async_computation.2 | async-start | bytes 2129920 | tf_op jit(solution)/shard_map/all_to_all | solution.py:19
  67.6 2.6 %multiply_reduce_fusion = f32[384]{0:T(512)S(1)} fusion(bf16[128,384]{1,0:T(8,128)(2,1)} %get-tuple-element.21, f32[384]{0:T(512)S(1)} %slice_reduce_fusion, bf16[4096,128]{1,0:T(8,128)(2,1)S(1)} %bitcast.9, bf16[4096,384]{1,0:T(8,128)(2,1)} %get-tuple-element.41), kind=kOutput, calls=%fused_computation.1 | convolution fusion | flops 402898560 | bytes 4295680 | tf_op jit(solution)/shard_map/dot_general | solution.py:376
  70.3 0.6 div.10
  70.8 11.7 %all-to-all-done.2.sums_ref = bf16[4,1040,128]{2,1,0:T(8,128)(2,1)S(1)} async-done(((bf16[4,1040,128]{2,1,0:T(8,128)(2,1)}), bf16[4,1040,128]{2,1,0:T(8,128)(2,1)S(1)}, u32[]{:S(2)}, u32[]{:S(2)}) %all-to-all-start.2) | async-done | bytes 1064992 | tf_op jit(solution)/shard_map/all_to_all | solution.py:19
  82.6 0.1 shard_map.62
  82.7 30.1 %all_to_all.20.sums_ref = bf16[16,72,128]{2,1,0:T(8,128)(2,1)S(1)} all-to-all(bf16[16,72,128]{2,1,0:T(8,128)(2,1)S(1)} %shard_map.62), channel_id=1, replica_groups=mesh['y'=4,'z'=16,'x'=4,'c'=2] {'z'}, dimensions={0} | all-to-all | bytes 589824 | tf_op jit(solution)/shard_map/all_to_all | solution.py:19
  112.8 0.8 shard_map.63
  (6 shorter events, 0.0 us)
Async XLA Ops:
  2.1 35.3 %all-to-all-start = ((bf16[16,64,128]{2,1,0:T(8,128)(2,1)}), bf16[16,64,128]{2,1,0:T(8,128)(2,1)S(1)}, u32[]{:S(2)}, u32[]{:S(2)}) async-start(bf16[16,64,128]{2,1,0:T(8,128)(2,1)} %broadcast_in_dim.10), calls=%async_computation | async-start | bytes 524288 | tf_op jit(solution)/shard_map/all_to_all | solution.py:19
  28.4 7.1 %collective-permute-start = (bf16[528,384]{1,0:T(8,128)(2,1)}, bf16[528,384]{1,0:T(8,128)(2,1)S(1)}, u32[]{:S(2)}, u32[]{:S(2)}) collective-permute-start(bf16[528,384]{1,0:T(8,128)(2,1)} %get-tuple-element.27), channel_id=1, source_target_pairs={{0,1},{1,0},{2,3},{3,2},{4,5},{5,4},{6,7},{7,6},{8,9},{9,8},{10,11... | collective-permute-start | bytes 1216520 | tf_op jit(solution)/shard_map/ppermute | solution.py:365
  30.3 5.2 %copy-start.3 = (f32[8,384]{1,0:T(8,128)S(1)}, f32[8,384]{1,0:T(8,128)}, u32[]{:S(2)}) copy-start(f32[8,384]{1,0:T(8,128)} %get-tuple-element.28.stats_ref) | copy-start | bytes 36868
  30.3 5.2 %copy-start.4 = (s32[2]{0:T(128)S(1)}, s32[2]{0:T(128)}, u32[]{:S(2)}) copy-start(s32[2]{0:T(128)} %pad_add_fusion.place_ref) | copy-start | bytes 28
  35.5 1.1 copy-start
  36.7 22.1 %copy-start.1 = (f32[128,384]{1,0:T(8,128)S(1)}, f32[128,384]{1,0:T(8,128)}, u32[]{:S(2)}) copy-start(f32[128,384]{1,0:T(8,128)} %get-tuple-element.37.refs_3_) | copy-start | bytes 589828
  38.5 20.2 %all-to-all-start.1 = ((bf16[4,1024,128]{2,1,0:T(8,128)(2,1)}), bf16[4,1024,128]{2,1,0:T(8,128)(2,1)S(1)}, u32[]{:S(2)}, u32[]{:S(2)}) async-start(bf16[4,1024,128]{2,1,0:T(8,128)(2,1)} %broadcast_in_dim.11), calls=%async_computation.1 | async-start | bytes 2097152 | tf_op jit(solution)/shard_map/all_to_all | solution.py:19
  43.0 8.6 %collective-permute-start.1 = (bf16[144,384]{1,0:T(8,128)(2,1)S(1)}, bf16[144,384]{1,0:T(8,128)(2,1)S(1)}, u32[]{:S(2)}, u32[]{:S(2)}) collective-permute-start(bf16[144,384]{1,0:T(8,128)(2,1)S(1)} %get-tuple-element.34), channel_id=1, source_target_pairs={{0,2},{2,4},{4,6},{6,0},{1,3},{3,5},{5,7},{7,1},{8,10},{10,12},{12... | collective-permute-start | bytes 331784 | tf_op jit(solution)/shard_map/ppermute | solution.py:369
  45.4 8.3 %collective-permute-start.2 = (bf16[144,384]{1,0:T(8,128)(2,1)S(1)}, bf16[144,384]{1,0:T(8,128)(2,1)S(1)}, u32[]{:S(2)}, u32[]{:S(2)}) collective-permute-start(bf16[144,384]{1,0:T(8,128)(2,1)S(1)} %get-tuple-element.35), channel_id=1, source_target_pairs={{0,4},{2,6},{4,0},{6,2},{1,5},{3,7},{5,1},{7,3},{8,12},{10,14},{12... | collective-permute-start | bytes 331784 | tf_op jit(solution)/shard_map/ppermute | solution.py:369
  49.7 7.9 %collective-permute-start.3 = (bf16[144,384]{1,0:T(8,128)(2,1)S(1)}, bf16[144,384]{1,0:T(8,128)(2,1)S(1)}, u32[]{:S(2)}, u32[]{:S(2)}) collective-permute-start(bf16[144,384]{1,0:T(8,128)(2,1)S(1)} %get-tuple-element.36), channel_id=1, source_target_pairs={{0,6},{2,0},{4,2},{6,4},{1,7},{3,1},{5,3},{7,5},{8,14},{10,8},{12,... | collective-permute-start | bytes 331784 | tf_op jit(solution)/shard_map/ppermute | solution.py:369
  64.0 18.6 %all-to-all-start.2 = ((bf16[4,1040,128]{2,1,0:T(8,128)(2,1)}), bf16[4,1040,128]{2,1,0:T(8,128)(2,1)S(1)}, u32[]{:S(2)}, u32[]{:S(2)}) async-start(bf16[4,1040,128]{2,1,0:T(8,128)(2,1)} %get-tuple-element.40), calls=%async_computation.2 | async-start | bytes 2129920 | tf_op jit(solution)/shard_map/all_to_all | solution.py:19
  67.6 45.2 %copy-start.2 = (bf16[1,64,128]{2,1,0:T(8,128)(2,1)S(1)}, bf16[1,64,128]{2,1,0:T(8,128)(2,1)}, u32[]{:S(2)}) copy-start(bf16[1,64,128]{2,1,0:T(8,128)(2,1)} %param.5) | copy-start | bytes 49156

commit v10 on v8

--- a/solution.py
+++ b/solution.py
@@ -13,10 +13,14 @@
 
 
 PACKED = 16
-
-
-def exchange(parts, axis):
-    return lax.all_to_all(parts, axis, 0, 0, tiled=True)
+BOOK_FIRST = 10
+SUMS_FIRST = 2
+
+
+def exchange(parts, axis, first=0):
+    count = lax.axis_size(axis)
+    order = [[(first + i) % count for i in range(count)]]
+    return lax.all_to_all(parts, axis, 0, 0, axis_index_groups=order, tiled=True)
 
 
 def wide_row(columns):
@@ -207,7 +211,8 @@
             total = total + sums_ref[part, at, :].astype(jnp.float32)
         row = (even if target % 2 == 0 else odd)[target // 2 : target // 2 + 1]
         row = jnp.concatenate([row, jnp.zeros((7, sub), jnp.float32)], axis=0)
-        out_ref[target] = jnp.concatenate([total, row], axis=0).astype(jnp.bfloat16)
+        place = (target + BOOK_FIRST - SUMS_FIRST) % targets
+        out_ref[place] = jnp.concatenate([total, row], axis=0).astype(jnp.bfloat16)
 
 
 def last_kernel(sums_ref, own_ref, out_ref):
@@ -326,7 +331,7 @@
     place = jnp.stack([lax.axis_index("c"), lax.axis_index("x")]).astype(jnp.int32)
 
     own = codebook.reshape(book_rows, sub_width)
-    book = exchange(jnp.broadcast_to(own, (z_count, book_rows, sub_width)), "z")
+    book = exchange(jnp.broadcast_to(own, (z_count, book_rows, sub_width)), "z", BOOK_FIRST)
     book = book.reshape(words // y_count, sub_width)
 
     kept, sent, stats, base = coarse(embeddings, centroids, place)
@@ -349,7 +354,7 @@
     sums = call(
         middle_kernel, array((z_count, book_rows + 8, sub_width), jnp.bfloat16), [VMEM], sums
     )
-    sums = exchange(sums, "z")
+    sums = exchange(sums, "z", SUMS_FIRST)
     new_codebook = call(last_kernel, array((book_rows, sub_width)), [VMEM] * 2, sums, own)
     return (residual, new_codebook[None], pq_error)
 

time: 107 us -> 104 us (0.972)
  blocking collectives: 28.9 us -> 25.8 us
  waiting for transfers between devices: 18.9 us -> 17.5 us
  starting transfers between devices: 35 us -> 36.3 us
    all_to_all x1, blocking collectives: 28.9 us -> 25.8 us  [exchange(): lax.all_to_all(parts, axis, 0, 0, axis_index_groups=order, tiled=True)]
    all_to_all x3, waiting for transfers between devices: 12.9 us -> 11.6 us  [exchange(): lax.all_to_all(parts, axis, 0, 0, axis_index_groups=order, tiled=True)]
    all_to_all x3, starting transfers between devices: 24.5 us -> 25.8 us  [exchange(): lax.all_to_all(parts, axis, 0, 0, axis_index_groups=order, tiled=True)]
  transfers between devices with their start and end apart: 7 -> 7, of which waited for: 4 -> 5; matrix products, arithmetic and copies ran while one was open for 3% -> 3% of each run, Pallas kernels for 7% -> 8%
where the time goes in v10:
time: 104 us
  starting transfers between devices  36.3 us (35%)
  blocking collectives  25.8 us (25%)
  waiting for transfers between devices  17.5 us (17%)
  Pallas kernels  13.9 us (13%)
  local copies, waits for them, and re-layouts  6.49 us (6%)
  matrix products  2.65 us (3%)
    all_to_all x1, blocking collectives, exchange(): lax.all_to_all(parts, axis, 0, 0, axis_index_groups=order, tiled=True)  25.8 us
    all_to_all x3, starting transfers between devices, exchange(): lax.all_to_all(parts, axis, 0, 0, axis_index_groups=order, tiled=True)  25.8 us
    pallas_call x6, Pallas kernels, call(): pl.pallas_call(kernel, out_shape=out_shape, in_specs=ins, out_specs=outs...  13.9 us
    all_to_all x3, waiting for transfers between devices, exchange(): lax.all_to_all(parts, axis, 0, 0, axis_index_groups=order, tiled=True)  11.6 us
    ppermute x3, starting transfers between devices, local(): lax.ppermute(block, 'x', [(i, (i + step) % x_count) for i in range(x_coun...  8.62 us
    ppermute x3, waiting for transfers between devices, local(): lax.ppermute(block, 'x', [(i, (i + step) % x_count) for i in range(x_coun...  5.92 us
    unnamed x6, local copies, waits for them, and re-layouts  3.32 us
    dot_general x1, matrix products, local(): lax.dot_general(book, raised, (((0,), (0,)), ((), ())), preferred_element...  2.65 us
  transfers between devices with their start and end apart: 7, of which 5 were waited for; matrix products, arithmetic and copies ran while one was open for 3% of the time, Pallas kernels for 8%

profile of v10, /device:TPU:6, one launch (start us, length us, event | category | flops | bytes accessed | tf_op | source)
XLA Modules:
  0.0 103.6 jit_solution(4636510095326271231)
XLA Ops:
  0.6 1.5 %broadcast_in_dim.10 = bf16[16,64,128]{2,1,0:T(8,128)(2,1)} broadcast(bf16[64,128]{1,0:T(8,128)(2,1)} %bitcast.10), dimensions={1,2} | broadcast | bytes 278528 | tf_op jit(solution)/shard_map/broadcast_in_dim | solution.py:334
  2.1 17.1 %all-to-all-start = ((bf16[16,64,128]{2,1,0:T(8,128)(2,1)}), bf16[16,64,128]{2,1,0:T(8,128)(2,1)S(1)}, u32[]{:S(2)}, u32[]{:S(2)}) async-start(bf16[16,64,128]{2,1,0:T(8,128)(2,1)} %broadcast_in_dim.10), calls=%async_computation | async-start | bytes 524288 | tf_op jit(solution)/shard_map/all_to_all | solution.py:23
  19.2 0.1 pad_add_fusion.place_ref
  19.2 0.0 copy-start
  19.2 2.2 %copy-done = bf16[2048,1024]{1,0:T(8,128)(2,1)S(1)} copy-done((bf16[2048,1024]{1,0:T(8,128)(2,1)S(1)}, bf16[2048,1024]{1,0:T(8,128)(2,1)}, u32[]{:S(2)}) %copy-start) | copy-done | bytes 4194328
  21.4 0.0 copy-start.1
  21.4 1.1 %copy-done.1 = bf16[384,1024]{1,0:T(8,128)(2,1)S(1)} copy-done((bf16[384,1024]{1,0:T(8,128)(2,1)S(1)}, bf16[384,1024]{1,0:T(8,128)(2,1)}, u32[]{:S(2)}) %copy-start.1) | copy-done | bytes 786456
  22.6 5.3 %shard_map.58 = (bf16[528,384]{1,0:T(8,128)(2,1)S(1)}, f32[8,384]{1,0:T(8,128)S(1)}, bf16[384,2048]{1,0:T(8,128)(2,1)S(1)}, f32[384,128]{1,0:T(8,128)S(1)}) custom-call(s32[2]{0:T(128)S(1)} %pad_add_fusion.place_ref, bf16[384,1024]{1,0:T(8,128)(2,1)S(1)} %copy-done.1, bf16[2048,1024]{1,0:T(8,128)(2,1)S(1)} %copy-done), custom_call_target="tpu_custom_call" | custom-call | flops 1 | bytes 1 | tf_op jit(solution)/shard_map/pallas_call | solution.py:238
  27.8 1.9 %collective-permute-start = (bf16[528,384]{1,0:T(8,128)(2,1)S(1)}, bf16[528,384]{1,0:T(8,128)(2,1)S(1)}, u32[]{:S(2)}, u32[]{:S(2)}) collective-permute-start(bf16[528,384]{1,0:T(8,128)(2,1)S(1)} %get-tuple-element.27), channel_id=1, source_target_pairs={{0,1},{1,0},{2,3},{3,2},{4,5},{5,4},{6,7},{7,6},{8,9},{9,8},{10,11... | collective-permute-start | bytes 1216520 | tf_op jit(solution)/shard_map/ppermute | solution.py:338
  29.7 1.8 %shard_map.59 = (f32[512,384]{1,0:T(8,128)S(1)}, f32[128,384]{1,0:T(8,128)S(1)}) custom-call(s32[2]{0:T(128)S(1)} %pad_add_fusion.place_ref, bf16[384,2048]{1,0:T(8,128)(2,1)S(1)} %get-tuple-element.24.weights_ref, f32[384,128]{1,0:T(8,128)S(1)} %get-tuple-element.25.inverse_ref, bf16[2048,1024]{1,0:T(8,128)(2,1)S(1)} %copy-done, bf16[384,1024]{1,0:T(8,128)(2,1)S(1)} %copy-done.1), custom_call_target="tpu_custom_call" | custom-call | flops 1 | bytes 1 | tf_op jit(solution)/shard_map/pallas_call | solution.py:238
  31.6 0.0 collective-permute-done.got_ref
  31.6 0.7 shard_map.60
  32.3 0.6 all-to-all-done
  32.9 1.1 %broadcast_in_dim.11 = bf16[4,1024,128]{2,1,0:T(8,128)(2,1)} broadcast(bf16[1024,128]{1,0:T(8,128)(2,1)S(1)} %bitcast.12), dimensions={1,2} | broadcast | bytes 1310720 | tf_op jit(solution)/shard_map/broadcast_in_dim | solution.py:345
  34.0 4.5 %all-to-all-start.1 = ((bf16[4,1024,128]{2,1,0:T(8,128)(2,1)}), bf16[4,1024,128]{2,1,0:T(8,128)(2,1)S(1)}, u32[]{:S(2)}, u32[]{:S(2)}) async-start(bf16[4,1024,128]{2,1,0:T(8,128)(2,1)} %broadcast_in_dim.11), calls=%async_computation.1 | async-start | bytes 2097152 | tf_op jit(solution)/shard_map/all_to_all | solution.py:23
  38.5 2.4 %collective-permute-start.1 = (bf16[144,384]{1,0:T(8,128)(2,1)S(1)}, bf16[144,384]{1,0:T(8,128)(2,1)S(1)}, u32[]{:S(2)}, u32[]{:S(2)}) collective-permute-start(bf16[144,384]{1,0:T(8,128)(2,1)S(1)} %get-tuple-element.34), channel_id=1, source_target_pairs={{0,2},{2,4},{4,6},{6,0},{1,3},{3,5},{5,7},{7,1},{8,10},{10,12},{12... | collective-permute-start | bytes 331784 | tf_op jit(solution)/shard_map/ppermute | solution.py:342
  40.9 4.3 %collective-permute-start.2 = (bf16[144,384]{1,0:T(8,128)(2,1)S(1)}, bf16[144,384]{1,0:T(8,128)(2,1)S(1)}, u32[]{:S(2)}, u32[]{:S(2)}) collective-permute-start(bf16[144,384]{1,0:T(8,128)(2,1)S(1)} %get-tuple-element.35), channel_id=1, source_target_pairs={{0,4},{2,6},{4,0},{6,2},{1,5},{3,7},{5,1},{7,3},{8,12},{10,14},{12... | collective-permute-start | bytes 331784 | tf_op jit(solution)/shard_map/ppermute | solution.py:342
  45.2 1.9 %collective-permute-start.3 = (bf16[144,384]{1,0:T(8,128)(2,1)S(1)}, bf16[144,384]{1,0:T(8,128)(2,1)S(1)}, u32[]{:S(2)}, u32[]{:S(2)}) collective-permute-start(bf16[144,384]{1,0:T(8,128)(2,1)S(1)} %get-tuple-element.36), channel_id=1, source_target_pairs={{0,6},{2,0},{4,2},{6,4},{1,7},{3,1},{5,3},{7,5},{8,14},{10,8},{12,... | collective-permute-start | bytes 331784 | tf_op jit(solution)/shard_map/ppermute | solution.py:342
  47.1 0.0 collective-permute-done.1.refs_0_
  47.2 1.9 %collective-permute-done.2.refs_1_ = bf16[144,384]{1,0:T(8,128)(2,1)S(1)} collective-permute-done((bf16[144,384]{1,0:T(8,128)(2,1)S(1)}, bf16[144,384]{1,0:T(8,128)(2,1)S(1)}, u32[]{:S(2)}, u32[]{:S(2)}) %collective-permute-start.2) | collective-permute-done | bytes 110624 | tf_op jit(solution)/shard_map/ppermute | solution.py:342
  49.0 4.0 %collective-permute-done.3.refs_2_ = bf16[144,384]{1,0:T(8,128)(2,1)S(1)} collective-permute-done((bf16[144,384]{1,0:T(8,128)(2,1)S(1)}, bf16[144,384]{1,0:T(8,128)(2,1)S(1)}, u32[]{:S(2)}, u32[]{:S(2)}) %collective-permute-start.3) | collective-permute-done | bytes 110624 | tf_op jit(solution)/shard_map/ppermute | solution.py:342
  53.1 0.6 all-to-all-done.1
  53.6 5.2 %shard_map.61 = (bf16[128,384]{1,0:T(8,128)(2,1)}, bf16[4,1040,128]{2,1,0:T(8,128)(2,1)}, bf16[4096,384]{1,0:T(8,128)(2,1)}, f32[8,384]{1,0:T(8,128)S(1)}) custom-call(f32[128,384]{1,0:T(8,128)S(1)} %get-tuple-element.29.mean_ref, f32[8,384]{1,0:T(8,128)S(1)} %get-tuple-element.30.chip_ref, bf16[144,384]{1,0:T(8,128)(2,1)S(1)} %collective-permute-done.1.refs_0_, ...), custom_call_target="tpu_custom_call" | custom-call | flops 1 | bytes 1 | tf_op jit(solution)/shard_map/pallas_call | solution.py:238
  58.9 4.2 %all-to-all-start.2 = ((bf16[4,1040,128]{2,1,0:T(8,128)(2,1)}), bf16[4,1040,128]{2,1,0:T(8,128)(2,1)S(1)}, u32[]{:S(2)}, u32[]{:S(2)}) async-start(bf16[4,1040,128]{2,1,0:T(8,128)(2,1)} %get-tuple-element.40), calls=%async_computation.2 | async-start | bytes 2129920 | tf_op jit(solution)/shard_map/all_to_all | solution.py:23
  63.1 0.0 copy-start.2
  63.1 2.7 %multiply_reduce_fusion = f32[384]{0:T(512)S(1)} fusion(bf16[128,384]{1,0:T(8,128)(2,1)} %get-tuple-element.21, f32[384]{0:T(512)S(1)} %slice_reduce_fusion, bf16[4096,128]{1,0:T(8,128)(2,1)S(1)} %bitcast.9, bf16[4096,384]{1,0:T(8,128)(2,1)} %get-tuple-element.41), kind=kOutput, calls=%fused_computation.1 | convolution fusion | flops 402898560 | bytes 4295680 | tf_op jit(solution)/shard_map/dot_general | solution.py:349
  65.8 0.6 div.10
  66.4 10.4 %all-to-all-done.2.sums_ref = bf16[4,1040,128]{2,1,0:T(8,128)(2,1)S(1)} async-done(((bf16[4,1040,128]{2,1,0:T(8,128)(2,1)}), bf16[4,1040,128]{2,1,0:T(8,128)(2,1)S(1)}, u32[]{:S(2)}, u32[]{:S(2)}) %all-to-all-start.2) | async-done | bytes 1064992 | tf_op jit(solution)/shard_map/all_to_all | solution.py:23
  76.8 0.1 shard_map.62
  76.9 25.8 %all_to_all.20.sums_ref = bf16[16,72,128]{2,1,0:T(8,128)(2,1)S(1)} all-to-all(bf16[16,72,128]{2,1,0:T(8,128)(2,1)S(1)} %shard_map.62), channel_id=1, replica_groups={{16,24,32,40,48,56,64,72,80,88,96,104,112,120,0,8},{17,25,33,41,49,57,6..., dimensions={0} | all-to-all | bytes 589824 | tf_op jit(solution)/shard_map/all_to_all | solution.py:23
  102.8 0.0 copy-done.2
  102.8 0.8 shard_map.63
  (2 shorter events, 0.0 us)
Async XLA Ops:
  2.1 30.8 %all-to-all-start = ((bf16[16,64,128]{2,1,0:T(8,128)(2,1)}), bf16[16,64,128]{2,1,0:T(8,128)(2,1)S(1)}, u32[]{:S(2)}, u32[]{:S(2)}) async-start(bf16[16,64,128]{2,1,0:T(8,128)(2,1)} %broadcast_in_dim.10), calls=%async_computation | async-start | bytes 524288 | tf_op jit(solution)/shard_map/all_to_all | solution.py:23
  19.2 2.2 %copy-start = (bf16[2048,1024]{1,0:T(8,128)(2,1)S(1)}, bf16[2048,1024]{1,0:T(8,128)(2,1)}, u32[]{:S(2)}) copy-start(bf16[2048,1024]{1,0:T(8,128)(2,1)} %c_ref.3) | copy-start | bytes 12582916
  21.4 1.1 %copy-start.1 = (bf16[384,1024]{1,0:T(8,128)(2,1)S(1)}, bf16[384,1024]{1,0:T(8,128)(2,1)}, u32[]{:S(2)}) copy-start(bf16[384,1024]{1,0:T(8,128)(2,1)} %e_ref.3) | copy-start | bytes 2359300
  27.8 3.8 %collective-permute-start = (bf16[528,384]{1,0:T(8,128)(2,1)S(1)}, bf16[528,384]{1,0:T(8,128)(2,1)S(1)}, u32[]{:S(2)}, u32[]{:S(2)}) collective-permute-start(bf16[528,384]{1,0:T(8,128)(2,1)S(1)} %get-tuple-element.27), channel_id=1, source_target_pairs={{0,1},{1,0},{2,3},{3,2},{4,5},{5,4},{6,7},{7,6},{8,9},{9,8},{10,11... | collective-permute-start | bytes 1216520 | tf_op jit(solution)/shard_map/ppermute | solution.py:338
  34.0 19.6 %all-to-all-start.1 = ((bf16[4,1024,128]{2,1,0:T(8,128)(2,1)}), bf16[4,1024,128]{2,1,0:T(8,128)(2,1)S(1)}, u32[]{:S(2)}, u32[]{:S(2)}) async-start(bf16[4,1024,128]{2,1,0:T(8,128)(2,1)} %broadcast_in_dim.11), calls=%async_computation.1 | async-start | bytes 2097152 | tf_op jit(solution)/shard_map/all_to_all | solution.py:23
  38.5 8.6 %collective-permute-start.1 = (bf16[144,384]{1,0:T(8,128)(2,1)S(1)}, bf16[144,384]{1,0:T(8,128)(2,1)S(1)}, u32[]{:S(2)}, u32[]{:S(2)}) collective-permute-start(bf16[144,384]{1,0:T(8,128)(2,1)S(1)} %get-tuple-element.34), channel_id=1, source_target_pairs={{0,2},{2,4},{4,6},{6,0},{1,3},{3,5},{5,7},{7,1},{8,10},{10,12},{12... | collective-permute-start | bytes 331784 | tf_op jit(solution)/shard_map/ppermute | solution.py:342
  40.9 8.1 %collective-permute-start.2 = (bf16[144,384]{1,0:T(8,128)(2,1)S(1)}, bf16[144,384]{1,0:T(8,128)(2,1)S(1)}, u32[]{:S(2)}, u32[]{:S(2)}) collective-permute-start(bf16[144,384]{1,0:T(8,128)(2,1)S(1)} %get-tuple-element.35), channel_id=1, source_target_pairs={{0,4},{2,6},{4,0},{6,2},{1,5},{3,7},{5,1},{7,3},{8,12},{10,14},{12... | collective-permute-start | bytes 331784 | tf_op jit(solution)/shard_map/ppermute | solution.py:342
  45.2 7.9 %collective-permute-start.3 = (bf16[144,384]{1,0:T(8,128)(2,1)S(1)}, bf16[144,384]{1,0:T(8,128)(2,1)S(1)}, u32[]{:S(2)}, u32[]{:S(2)}) collective-permute-start(bf16[144,384]{1,0:T(8,128)(2,1)S(1)} %get-tuple-element.36), channel_id=1, source_target_pairs={{0,6},{2,0},{4,2},{6,4},{1,7},{3,1},{5,3},{7,5},{8,14},{10,8},{12,... | collective-permute-start | bytes 331784 | tf_op jit(solution)/shard_map/ppermute | solution.py:342
  58.9 17.9 %all-to-all-start.2 = ((bf16[4,1040,128]{2,1,0:T(8,128)(2,1)}), bf16[4,1040,128]{2,1,0:T(8,128)(2,1)S(1)}, u32[]{:S(2)}, u32[]{:S(2)}) async-start(bf16[4,1040,128]{2,1,0:T(8,128)(2,1)} %get-tuple-element.40), calls=%async_computation.2 | async-start | bytes 2129920 | tf_op jit(solution)/shard_map/all_to_all | solution.py:23
  63.1 39.7 %copy-start.2 = (bf16[1,64,128]{2,1,0:T(8,128)(2,1)S(1)}, bf16[1,64,128]{2,1,0:T(8,128)(2,1)}, u32[]{:S(2)}) copy-start(bf16[1,64,128]{2,1,0:T(8,128)(2,1)} %param.5) | copy-start | bytes 49156

commit v11 on v10

--- a/solution.py
+++ b/solution.py
@@ -34,7 +34,7 @@
     scale = 2.0 / math.sqrt(width)
 
     def score(j, peak):
-        block = c_ref[pl.ds(pl.multiple_of(j * chunk, chunk), chunk), :]
+        block = c_ref[slice(j * chunk, j * chunk + chunk), :]
         wide = block.astype(jnp.float32)
         half_norm = wide_row(0.5 * jnp.sum(wide * wide, axis=1, keepdims=True))
         products = lax.dot_general(
@@ -46,17 +46,21 @@
             peak = jnp.maximum(peak, logits[:, part * 128 : part * 128 + 128])
         return peak
 
-    peak = lax.fori_loop(0, chunks, score, jnp.full((rows, 128), -jnp.inf, jnp.float32), unroll=2)
+    peak = jnp.full((rows, 128), -jnp.inf, jnp.float32)
+    for j in range(chunks):
+        peak = score(j, peak)
     peak = jnp.max(peak, axis=1, keepdims=True)
 
     def raise_(j, total):
         shifted = jnp.exp(logits_ref[j] - peak)
-        weights_ref[:, pl.ds(pl.multiple_of(j * chunk, chunk), chunk)] = shifted.astype(jnp.bfloat16)
+        weights_ref[:, slice(j * chunk, j * chunk + chunk)] = shifted.astype(jnp.bfloat16)
         for part in range(chunk // 128):
             total = total + shifted[:, part * 128 : part * 128 + 128]
         return total
 
-    total = lax.fori_loop(0, chunks, raise_, jnp.zeros((rows, 128), jnp.float32), unroll=2)
+    total = jnp.zeros((rows, 128), jnp.float32)
+    for j in range(chunks):
+        total = raise_(j, total)
     total = jnp.sum(total, axis=1, keepdims=True)
     inverse_ref[...] = jnp.broadcast_to(1.0 / total, inverse_ref.shape)
     pull(1 - place_ref[0], weights_ref, inverse_ref, c_ref, sent_ref)
@@ -338,10 +342,11 @@
     got = lax.ppermute(sent, "c", [(0, 1), (1, 0)])
     mean, stats, *blocks = chip(place, kept, got, stats)
     book, *blocks = lax.optimization_barrier((book, *blocks))
-    gots = [
-        lax.ppermute(block, "x", [(i, (i + step) % x_count) for i in range(x_count)])
-        for step, block in enumerate(blocks, 1)
-    ]
+    gots = {}
+    for step in (2, 1, 3):
+        ring = [(i, (i + step) % x_count) for i in range(x_count)]
+        gots[step] = lax.ppermute(blocks[step - 1], "x", ring)
+    gots = [gots[step] for step in (1, 2, 3)]
     book = exchange(jnp.broadcast_to(book, (y_count,) + book.shape), "y").reshape(words, sub_width)
     residual, sums, raised, inverse = quantize(mean, stats, gots, base, book, y_count)
 

time: 104 us -> 104 us (level)
  blocking collectives: 25.8 us -> 27.1 us
    all_to_all x1, blocking collectives: 25.8 us -> 27.1 us  [exchange(): lax.all_to_all(parts, axis, 0, 0, axis_index_groups=order, tiled=True)]
  transfers between devices with their start and end apart: 7 -> 7, of which waited for: 5 -> 4; matrix products, arithmetic and copies ran while one was open for 3% -> 3% of each run, Pallas kernels for 8% -> 7%
where the time goes in v11:
time: 104 us
  starting transfers between devices  36.9 us (35%)
  blocking collectives  27.1 us (26%)
  waiting for transfers between devices  16.5 us (16%)
  Pallas kernels  13.1 us (13%)
  local copies, waits for them, and re-layouts  6.49 us (6%)
  matrix products  2.65 us (3%)
    all_to_all x1, blocking collectives, exchange(): lax.all_to_all(parts, axis, 0, 0, axis_index_groups=order, tiled=True)  27.1 us
    all_to_all x3, starting transfers between devices, exchange(): lax.all_to_all(parts, axis, 0, 0, axis_index_groups=order, tiled=True)  26.3 us
    pallas_call x6, Pallas kernels, call(): pl.pallas_call(kernel, out_shape=out_shape, in_specs=ins, out_specs=outs...  13.1 us
    all_to_all x3, waiting for transfers between devices, exchange(): lax.all_to_all(parts, axis, 0, 0, axis_index_groups=order, tiled=True)  10.6 us
    ppermute x3, starting transfers between devices, local(): gots[step] = lax.ppermute(blocks[step - 1], 'x', ring)  8.62 us
    ppermute x3, waiting for transfers between devices, local(): gots[step] = lax.ppermute(blocks[step - 1], 'x', ring)  5.92 us
    unnamed x6, local copies, waits for them, and re-layouts  3.32 us
    dot_general x1, matrix products, local(): lax.dot_general(book, raised, (((0,), (0,)), ((), ())), preferred_element...  2.65 us
  transfers between devices with their start and end apart: 7, of which 4 were waited for; matrix products, arithmetic and copies ran while one was open for 3% of the time, Pallas kernels for 7%

profile of v11, /device:TPU:6, one launch (start us, length us, event | category | flops | bytes accessed | tf_op | source)
XLA Modules:
  0.0 103.6 jit_solution(2618944014122843208)
XLA Ops:
  0.6 1.5 %broadcast_in_dim.10 = bf16[16,64,128]{2,1,0:T(8,128)(2,1)} broadcast(bf16[64,128]{1,0:T(8,128)(2,1)} %bitcast.10), dimensions={1,2} | broadcast | bytes 278528 | tf_op jit(solution)/shard_map/broadcast_in_dim | solution.py:338
  2.1 17.1 %all-to-all-start = ((bf16[16,64,128]{2,1,0:T(8,128)(2,1)}), bf16[16,64,128]{2,1,0:T(8,128)(2,1)S(1)}, u32[]{:S(2)}, u32[]{:S(2)}) async-start(bf16[16,64,128]{2,1,0:T(8,128)(2,1)} %broadcast_in_dim.10), calls=%async_computation | async-start | bytes 524288 | tf_op jit(solution)/shard_map/all_to_all | solution.py:23
  19.2 0.1 pad_add_fusion.place_ref
  19.2 0.0 copy-start
  19.2 2.2 %copy-done = bf16[2048,1024]{1,0:T(8,128)(2,1)S(1)} copy-done((bf16[2048,1024]{1,0:T(8,128)(2,1)S(1)}, bf16[2048,1024]{1,0:T(8,128)(2,1)}, u32[]{:S(2)}) %copy-start) | copy-done | bytes 4194328
  21.4 0.0 copy-start.1
  21.4 1.1 %copy-done.1 = bf16[384,1024]{1,0:T(8,128)(2,1)S(1)} copy-done((bf16[384,1024]{1,0:T(8,128)(2,1)S(1)}, bf16[384,1024]{1,0:T(8,128)(2,1)}, u32[]{:S(2)}) %copy-start.1) | copy-done | bytes 786456
  22.6 4.4 %shard_map.58 = (bf16[528,384]{1,0:T(8,128)(2,1)S(1)}, f32[8,384]{1,0:T(8,128)S(1)}, bf16[384,2048]{1,0:T(8,128)(2,1)S(1)}, f32[384,128]{1,0:T(8,128)S(1)}) custom-call(s32[2]{0:T(128)S(1)} %pad_add_fusion.place_ref, bf16[384,1024]{1,0:T(8,128)(2,1)S(1)} %copy-done.1, bf16[2048,1024]{1,0:T(8,128)(2,1)S(1)} %copy-done), custom_call_target="tpu_custom_call" | custom-call | flops 1 | bytes 1 | tf_op jit(solution)/shard_map/pallas_call | solution.py:242
  27.0 1.9 %collective-permute-start = (bf16[528,384]{1,0:T(8,128)(2,1)S(1)}, bf16[528,384]{1,0:T(8,128)(2,1)S(1)}, u32[]{:S(2)}, u32[]{:S(2)}) collective-permute-start(bf16[528,384]{1,0:T(8,128)(2,1)S(1)} %get-tuple-element.27), channel_id=1, source_target_pairs={{0,1},{1,0},{2,3},{3,2},{4,5},{5,4},{6,7},{7,6},{8,9},{9,8},{10,11... | collective-permute-start | bytes 1216520 | tf_op jit(solution)/shard_map/ppermute | solution.py:342
  28.9 1.8 %shard_map.59 = (f32[512,384]{1,0:T(8,128)S(1)}, f32[128,384]{1,0:T(8,128)S(1)}) custom-call(s32[2]{0:T(128)S(1)} %pad_add_fusion.place_ref, bf16[384,2048]{1,0:T(8,128)(2,1)S(1)} %get-tuple-element.24.weights_ref, f32[384,128]{1,0:T(8,128)S(1)} %get-tuple-element.25.inverse_ref, bf16[2048,1024]{1,0:T(8,128)(2,1)S(1)} %copy-done, bf16[384,1024]{1,0:T(8,128)(2,1)S(1)} %copy-done.1), custom_call_target="tpu_custom_call" | custom-call | flops 1 | bytes 1 | tf_op jit(solution)/shard_map/pallas_call | solution.py:242
  30.8 0.0 collective-permute-done.got_ref
  30.8 0.7 shard_map.60
  31.5 1.4 %all-to-all-done = bf16[16,64,128]{2,1,0:T(8,128)(2,1)S(1)} async-done(((bf16[16,64,128]{2,1,0:T(8,128)(2,1)}), bf16[16,64,128]{2,1,0:T(8,128)(2,1)S(1)}, u32[]{:S(2)}, u32[]{:S(2)}) %all-to-all-start) | async-done | bytes 262176 | tf_op jit(solution)/shard_map/all_to_all | solution.py:23
  32.9 1.1 %broadcast_in_dim.11 = bf16[4,1024,128]{2,1,0:T(8,128)(2,1)} broadcast(bf16[1024,128]{1,0:T(8,128)(2,1)S(1)} %bitcast.12), dimensions={1,2} | broadcast | bytes 1310720 | tf_op jit(solution)/shard_map/broadcast_in_dim | solution.py:350
  34.0 4.5 %all-to-all-start.1 = ((bf16[4,1024,128]{2,1,0:T(8,128)(2,1)}), bf16[4,1024,128]{2,1,0:T(8,128)(2,1)S(1)}, u32[]{:S(2)}, u32[]{:S(2)}) async-start(bf16[4,1024,128]{2,1,0:T(8,128)(2,1)} %broadcast_in_dim.11), calls=%async_computation.1 | async-start | bytes 2097152 | tf_op jit(solution)/shard_map/all_to_all | solution.py:23
  38.5 2.4 %collective-permute-start.1 = (bf16[144,384]{1,0:T(8,128)(2,1)S(1)}, bf16[144,384]{1,0:T(8,128)(2,1)S(1)}, u32[]{:S(2)}, u32[]{:S(2)}) collective-permute-start(bf16[144,384]{1,0:T(8,128)(2,1)S(1)} %get-tuple-element.34), channel_id=1, source_target_pairs={{0,2},{2,4},{4,6},{6,0},{1,3},{3,5},{5,7},{7,1},{8,10},{10,12},{12... | collective-permute-start | bytes 331784 | tf_op jit(solution)/shard_map/ppermute | solution.py:348
  40.9 4.3 %collective-permute-start.2 = (bf16[144,384]{1,0:T(8,128)(2,1)S(1)}, bf16[144,384]{1,0:T(8,128)(2,1)S(1)}, u32[]{:S(2)}, u32[]{:S(2)}) collective-permute-start(bf16[144,384]{1,0:T(8,128)(2,1)S(1)} %get-tuple-element.35), channel_id=1, source_target_pairs={{0,4},{2,6},{4,0},{6,2},{1,5},{3,7},{5,1},{7,3},{8,12},{10,14},{12... | collective-permute-start | bytes 331784 | tf_op jit(solution)/shard_map/ppermute | solution.py:348
  45.2 1.9 %collective-permute-start.3 = (bf16[144,384]{1,0:T(8,128)(2,1)S(1)}, bf16[144,384]{1,0:T(8,128)(2,1)S(1)}, u32[]{:S(2)}, u32[]{:S(2)}) collective-permute-start(bf16[144,384]{1,0:T(8,128)(2,1)S(1)} %get-tuple-element.36), channel_id=1, source_target_pairs={{0,6},{2,0},{4,2},{6,4},{1,7},{3,1},{5,3},{7,5},{8,14},{10,8},{12,... | collective-permute-start | bytes 331784 | tf_op jit(solution)/shard_map/ppermute | solution.py:348
  47.1 0.0 collective-permute-done.1.refs_0_
  47.2 1.9 %collective-permute-done.2.refs_1_ = bf16[144,384]{1,0:T(8,128)(2,1)S(1)} collective-permute-done((bf16[144,384]{1,0:T(8,128)(2,1)S(1)}, bf16[144,384]{1,0:T(8,128)(2,1)S(1)}, u32[]{:S(2)}, u32[]{:S(2)}) %collective-permute-start.2) | collective-permute-done | bytes 110624 | tf_op jit(solution)/shard_map/ppermute | solution.py:348
  49.0 4.0 %collective-permute-done.3.refs_2_ = bf16[144,384]{1,0:T(8,128)(2,1)S(1)} collective-permute-done((bf16[144,384]{1,0:T(8,128)(2,1)S(1)}, bf16[144,384]{1,0:T(8,128)(2,1)S(1)}, u32[]{:S(2)}, u32[]{:S(2)}) %collective-permute-start.3) | collective-permute-done | bytes 110624 | tf_op jit(solution)/shard_map/ppermute | solution.py:348
  53.1 0.0 all-to-all-done.1
  53.1 5.2 %shard_map.61 = (bf16[128,384]{1,0:T(8,128)(2,1)}, bf16[4,1040,128]{2,1,0:T(8,128)(2,1)}, bf16[4096,384]{1,0:T(8,128)(2,1)}, f32[8,384]{1,0:T(8,128)S(1)}) custom-call(f32[128,384]{1,0:T(8,128)S(1)} %get-tuple-element.29.mean_ref, f32[8,384]{1,0:T(8,128)S(1)} %get-tuple-element.30.chip_ref, bf16[144,384]{1,0:T(8,128)(2,1)S(1)} %collective-permute-done.1.refs_0_, ...), custom_call_target="tpu_custom_call" | custom-call | flops 1 | bytes 1 | tf_op jit(solution)/shard_map/pallas_call | solution.py:242
  58.3 4.8 %all-to-all-start.2 = ((bf16[4,1040,128]{2,1,0:T(8,128)(2,1)}), bf16[4,1040,128]{2,1,0:T(8,128)(2,1)S(1)}, u32[]{:S(2)}, u32[]{:S(2)}) async-start(bf16[4,1040,128]{2,1,0:T(8,128)(2,1)} %get-tuple-element.40), calls=%async_computation.2 | async-start | bytes 2129920 | tf_op jit(solution)/shard_map/all_to_all | solution.py:23
  63.1 0.0 copy-start.2
  63.1 2.7 %multiply_reduce_fusion = f32[384]{0:T(512)S(1)} fusion(bf16[128,384]{1,0:T(8,128)(2,1)} %get-tuple-element.21, f32[384]{0:T(512)S(1)} %slice_reduce_fusion, bf16[4096,128]{1,0:T(8,128)(2,1)S(1)} %bitcast.9, bf16[4096,384]{1,0:T(8,128)(2,1)} %get-tuple-element.41), kind=kOutput, calls=%fused_computation.1 | convolution fusion | flops 402898560 | bytes 4295680 | tf_op jit(solution)/shard_map/dot_general | solution.py:354
  65.8 0.6 div.10
  66.4 9.2 %all-to-all-done.2.sums_ref = bf16[4,1040,128]{2,1,0:T(8,128)(2,1)S(1)} async-done(((bf16[4,1040,128]{2,1,0:T(8,128)(2,1)}), bf16[4,1040,128]{2,1,0:T(8,128)(2,1)S(1)}, u32[]{:S(2)}, u32[]{:S(2)}) %all-to-all-start.2) | async-done | bytes 1064992 | tf_op jit(solution)/shard_map/all_to_all | solution.py:23
  75.5 0.1 shard_map.62
  75.6 27.1 %all_to_all.20.sums_ref = bf16[16,72,128]{2,1,0:T(8,128)(2,1)S(1)} all-to-all(bf16[16,72,128]{2,1,0:T(8,128)(2,1)S(1)} %shard_map.62), channel_id=1, replica_groups={{16,24,32,40,48,56,64,72,80,88,96,104,112,120,0,8},{17,25,33,41,49,57,6..., dimensions={0} | all-to-all | bytes 589824 | tf_op jit(solution)/shard_map/all_to_all | solution.py:23
  102.8 0.0 copy-done.2
  102.8 0.8 shard_map.63
  (2 shorter events, 0.0 us)
Async XLA Ops:
  2.1 30.8 %all-to-all-start = ((bf16[16,64,128]{2,1,0:T(8,128)(2,1)}), bf16[16,64,128]{2,1,0:T(8,128)(2,1)S(1)}, u32[]{:S(2)}, u32[]{:S(2)}) async-start(bf16[16,64,128]{2,1,0:T(8,128)(2,1)} %broadcast_in_dim.10), calls=%async_computation | async-start | bytes 524288 | tf_op jit(solution)/shard_map/all_to_all | solution.py:23
  19.2 2.2 %copy-start = (bf16[2048,1024]{1,0:T(8,128)(2,1)S(1)}, bf16[2048,1024]{1,0:T(8,128)(2,1)}, u32[]{:S(2)}) copy-start(bf16[2048,1024]{1,0:T(8,128)(2,1)} %c_ref.3) | copy-start | bytes 12582916
  21.4 1.1 %copy-start.1 = (bf16[384,1024]{1,0:T(8,128)(2,1)S(1)}, bf16[384,1024]{1,0:T(8,128)(2,1)}, u32[]{:S(2)}) copy-start(bf16[384,1024]{1,0:T(8,128)(2,1)} %e_ref.3) | copy-start | bytes 2359300
  27.0 3.8 %collective-permute-start = (bf16[528,384]{1,0:T(8,128)(2,1)S(1)}, bf16[528,384]{1,0:T(8,128)(2,1)S(1)}, u32[]{:S(2)}, u32[]{:S(2)}) collective-permute-start(bf16[528,384]{1,0:T(8,128)(2,1)S(1)} %get-tuple-element.27), channel_id=1, source_target_pairs={{0,1},{1,0},{2,3},{3,2},{4,5},{5,4},{6,7},{7,6},{8,9},{9,8},{10,11... | collective-permute-start | bytes 1216520 | tf_op jit(solution)/shard_map/ppermute | solution.py:342
  34.0 19.0 %all-to-all-start.1 = ((bf16[4,1024,128]{2,1,0:T(8,128)(2,1)}), bf16[4,1024,128]{2,1,0:T(8,128)(2,1)S(1)}, u32[]{:S(2)}, u32[]{:S(2)}) async-start(bf16[4,1024,128]{2,1,0:T(8,128)(2,1)} %broadcast_in_dim.11), calls=%async_computation.1 | async-start | bytes 2097152 | tf_op jit(solution)/shard_map/all_to_all | solution.py:23
  38.5 8.6 %collective-permute-start.1 = (bf16[144,384]{1,0:T(8,128)(2,1)S(1)}, bf16[144,384]{1,0:T(8,128)(2,1)S(1)}, u32[]{:S(2)}, u32[]{:S(2)}) collective-permute-start(bf16[144,384]{1,0:T(8,128)(2,1)S(1)} %get-tuple-element.34), channel_id=1, source_target_pairs={{0,2},{2,4},{4,6},{6,0},{1,3},{3,5},{5,7},{7,1},{8,10},{10,12},{12... | collective-permute-start | bytes 331784 | tf_op jit(solution)/shard_map/ppermute | solution.py:348
  40.9 8.1 %collective-permute-start.2 = (bf16[144,384]{1,0:T(8,128)(2,1)S(1)}, bf16[144,384]{1,0:T(8,128)(2,1)S(1)}, u32[]{:S(2)}, u32[]{:S(2)}) collective-permute-start(bf16[144,384]{1,0:T(8,128)(2,1)S(1)} %get-tuple-element.35), channel_id=1, source_target_pairs={{0,4},{2,6},{4,0},{6,2},{1,5},{3,7},{5,1},{7,3},{8,12},{10,14},{12... | collective-permute-start | bytes 331784 | tf_op jit(solution)/shard_map/ppermute | solution.py:348
  45.2 7.9 %collective-permute-start.3 = (bf16[144,384]{1,0:T(8,128)(2,1)S(1)}, bf16[144,384]{1,0:T(8,128)(2,1)S(1)}, u32[]{:S(2)}, u32[]{:S(2)}) collective-permute-start(bf16[144,384]{1,0:T(8,128)(2,1)S(1)} %get-tuple-element.36), channel_id=1, source_target_pairs={{0,6},{2,0},{4,2},{6,4},{1,7},{3,1},{5,3},{7,5},{8,14},{10,8},{12,... | collective-permute-start | bytes 331784 | tf_op jit(solution)/shard_map/ppermute | solution.py:348
  58.3 17.2 %all-to-all-start.2 = ((bf16[4,1040,128]{2,1,0:T(8,128)(2,1)}), bf16[4,1040,128]{2,1,0:T(8,128)(2,1)S(1)}, u32[]{:S(2)}, u32[]{:S(2)}) async-start(bf16[4,1040,128]{2,1,0:T(8,128)(2,1)} %get-tuple-element.40), calls=%async_computation.2 | async-start | bytes 2129920 | tf_op jit(solution)/shard_map/all_to_all | solution.py:23
  63.1 39.7 %copy-start.2 = (bf16[1,64,128]{2,1,0:T(8,128)(2,1)S(1)}, bf16[1,64,128]{2,1,0:T(8,128)(2,1)}, u32[]{:S(2)}) copy-start(bf16[1,64,128]{2,1,0:T(8,128)(2,1)} %param.5) | copy-start | bytes 49156

commit v12 on v11

--- a/solution.py
+++ b/solution.py
@@ -14,7 +14,7 @@
 
 PACKED = 16
 BOOK_FIRST = 10
-SUMS_FIRST = 2
+SUMS_FIRST = 8
 
 
 def exchange(parts, axis, first=0):

time: 104 us -> 102 us (0.981)
  blocking collectives: 27.1 us -> 25 us
    all_to_all x1, blocking collectives: 27.1 us -> 25 us  [exchange(): lax.all_to_all(parts, axis, 0, 0, axis_index_groups=order, tiled=True)]
where the time goes in v12:
time: 102 us; the launch traced here: 101 us
  starting transfers between devices  36.9 us (36%)
  blocking collectives  25 us (25%)
  waiting for transfers between devices  16.5 us (16%)
  Pallas kernels  13.1 us (13%)
  local copies, waits for them, and re-layouts  6.49 us (6%)
  matrix products  2.65 us (3%)
    all_to_all x3, starting transfers between devices, exchange(): lax.all_to_all(parts, axis, 0, 0, axis_index_groups=order, tiled=True)  26.3 us
    all_to_all x1, blocking collectives, exchange(): lax.all_to_all(parts, axis, 0, 0, axis_index_groups=order, tiled=True)  25 us
    pallas_call x6, Pallas kernels, call(): pl.pallas_call(kernel, out_shape=out_shape, in_specs=ins, out_specs=outs...  13.1 us
    all_to_all x3, waiting for transfers between devices, exchange(): lax.all_to_all(parts, axis, 0, 0, axis_index_groups=order, tiled=True)  10.6 us
    ppermute x3, starting transfers between devices, local(): gots[step] = lax.ppermute(blocks[step - 1], 'x', ring)  8.62 us
    ppermute x3, waiting for transfers between devices, local(): gots[step] = lax.ppermute(blocks[step - 1], 'x', ring)  5.92 us
    unnamed x6, local copies, waits for them, and re-layouts  3.32 us
    dot_general x1, matrix products, local(): lax.dot_general(book, raised, (((0,), (0,)), ((), ())), preferred_element...  2.65 us
  transfers between devices with their start and end apart: 7, of which 4 were waited for; matrix products, arithmetic and copies ran while one was open for 3% of the time, Pallas kernels for 7%

profile of v12, /device:TPU:6, one launch (start us, length us, event | category | flops | bytes accessed | tf_op | source)
XLA Modules:
  0.0 101.5 jit_solution(2159885297180337766)
XLA Ops:
  0.6 1.5 %broadcast_in_dim.10 = bf16[16,64,128]{2,1,0:T(8,128)(2,1)} broadcast(bf16[64,128]{1,0:T(8,128)(2,1)} %bitcast.10), dimensions={1,2} | broadcast | bytes 278528 | tf_op jit(solution)/shard_map/broadcast_in_dim | solution.py:338
  2.1 17.1 %all-to-all-start = ((bf16[16,64,128]{2,1,0:T(8,128)(2,1)}), bf16[16,64,128]{2,1,0:T(8,128)(2,1)S(1)}, u32[]{:S(2)}, u32[]{:S(2)}) async-start(bf16[16,64,128]{2,1,0:T(8,128)(2,1)} %broadcast_in_dim.10), calls=%async_computation | async-start | bytes 524288 | tf_op jit(solution)/shard_map/all_to_all | solution.py:23
  19.2 0.1 pad_add_fusion.place_ref
  19.2 0.0 copy-start
  19.2 2.2 %copy-done = bf16[2048,1024]{1,0:T(8,128)(2,1)S(1)} copy-done((bf16[2048,1024]{1,0:T(8,128)(2,1)S(1)}, bf16[2048,1024]{1,0:T(8,128)(2,1)}, u32[]{:S(2)}) %copy-start) | copy-done | bytes 4194328
  21.4 0.0 copy-start.1
  21.4 1.1 %copy-done.1 = bf16[384,1024]{1,0:T(8,128)(2,1)S(1)} copy-done((bf16[384,1024]{1,0:T(8,128)(2,1)S(1)}, bf16[384,1024]{1,0:T(8,128)(2,1)}, u32[]{:S(2)}) %copy-start.1) | copy-done | bytes 786456
  22.6 4.4 %shard_map.58 = (bf16[528,384]{1,0:T(8,128)(2,1)S(1)}, f32[8,384]{1,0:T(8,128)S(1)}, bf16[384,2048]{1,0:T(8,128)(2,1)S(1)}, f32[384,128]{1,0:T(8,128)S(1)}) custom-call(s32[2]{0:T(128)S(1)} %pad_add_fusion.place_ref, bf16[384,1024]{1,0:T(8,128)(2,1)S(1)} %copy-done.1, bf16[2048,1024]{1,0:T(8,128)(2,1)S(1)} %copy-done), custom_call_target="tpu_custom_call" | custom-call | flops 1 | bytes 1 | tf_op jit(solution)/shard_map/pallas_call | solution.py:242
  27.0 1.9 %collective-permute-start = (bf16[528,384]{1,0:T(8,128)(2,1)S(1)}, bf16[528,384]{1,0:T(8,128)(2,1)S(1)}, u32[]{:S(2)}, u32[]{:S(2)}) collective-permute-start(bf16[528,384]{1,0:T(8,128)(2,1)S(1)} %get-tuple-element.27), channel_id=1, source_target_pairs={{0,1},{1,0},{2,3},{3,2},{4,5},{5,4},{6,7},{7,6},{8,9},{9,8},{10,11... | collective-permute-start | bytes 1216520 | tf_op jit(solution)/shard_map/ppermute | solution.py:342
  28.9 1.8 %shard_map.59 = (f32[512,384]{1,0:T(8,128)S(1)}, f32[128,384]{1,0:T(8,128)S(1)}) custom-call(s32[2]{0:T(128)S(1)} %pad_add_fusion.place_ref, bf16[384,2048]{1,0:T(8,128)(2,1)S(1)} %get-tuple-element.24.weights_ref, f32[384,128]{1,0:T(8,128)S(1)} %get-tuple-element.25.inverse_ref, bf16[2048,1024]{1,0:T(8,128)(2,1)S(1)} %copy-done, bf16[384,1024]{1,0:T(8,128)(2,1)S(1)} %copy-done.1), custom_call_target="tpu_custom_call" | custom-call | flops 1 | bytes 1 | tf_op jit(solution)/shard_map/pallas_call | solution.py:242
  30.8 0.0 collective-permute-done.got_ref
  30.8 0.7 shard_map.60
  31.5 1.4 %all-to-all-done = bf16[16,64,128]{2,1,0:T(8,128)(2,1)S(1)} async-done(((bf16[16,64,128]{2,1,0:T(8,128)(2,1)}), bf16[16,64,128]{2,1,0:T(8,128)(2,1)S(1)}, u32[]{:S(2)}, u32[]{:S(2)}) %all-to-all-start) | async-done | bytes 262176 | tf_op jit(solution)/shard_map/all_to_all | solution.py:23
  32.9 1.1 %broadcast_in_dim.11 = bf16[4,1024,128]{2,1,0:T(8,128)(2,1)} broadcast(bf16[1024,128]{1,0:T(8,128)(2,1)S(1)} %bitcast.12), dimensions={1,2} | broadcast | bytes 1310720 | tf_op jit(solution)/shard_map/broadcast_in_dim | solution.py:350
  34.0 4.5 %all-to-all-start.1 = ((bf16[4,1024,128]{2,1,0:T(8,128)(2,1)}), bf16[4,1024,128]{2,1,0:T(8,128)(2,1)S(1)}, u32[]{:S(2)}, u32[]{:S(2)}) async-start(bf16[4,1024,128]{2,1,0:T(8,128)(2,1)} %broadcast_in_dim.11), calls=%async_computation.1 | async-start | bytes 2097152 | tf_op jit(solution)/shard_map/all_to_all | solution.py:23
  38.5 2.4 %collective-permute-start.1 = (bf16[144,384]{1,0:T(8,128)(2,1)S(1)}, bf16[144,384]{1,0:T(8,128)(2,1)S(1)}, u32[]{:S(2)}, u32[]{:S(2)}) collective-permute-start(bf16[144,384]{1,0:T(8,128)(2,1)S(1)} %get-tuple-element.34), channel_id=1, source_target_pairs={{0,2},{2,4},{4,6},{6,0},{1,3},{3,5},{5,7},{7,1},{8,10},{10,12},{12... | collective-permute-start | bytes 331784 | tf_op jit(solution)/shard_map/ppermute | solution.py:348
  40.9 4.3 %collective-permute-start.2 = (bf16[144,384]{1,0:T(8,128)(2,1)S(1)}, bf16[144,384]{1,0:T(8,128)(2,1)S(1)}, u32[]{:S(2)}, u32[]{:S(2)}) collective-permute-start(bf16[144,384]{1,0:T(8,128)(2,1)S(1)} %get-tuple-element.35), channel_id=1, source_target_pairs={{0,4},{2,6},{4,0},{6,2},{1,5},{3,7},{5,1},{7,3},{8,12},{10,14},{12... | collective-permute-start | bytes 331784 | tf_op jit(solution)/shard_map/ppermute | solution.py:348
  45.2 1.9 %collective-permute-start.3 = (bf16[144,384]{1,0:T(8,128)(2,1)S(1)}, bf16[144,384]{1,0:T(8,128)(2,1)S(1)}, u32[]{:S(2)}, u32[]{:S(2)}) collective-permute-start(bf16[144,384]{1,0:T(8,128)(2,1)S(1)} %get-tuple-element.36), channel_id=1, source_target_pairs={{0,6},{2,0},{4,2},{6,4},{1,7},{3,1},{5,3},{7,5},{8,14},{10,8},{12,... | collective-permute-start | bytes 331784 | tf_op jit(solution)/shard_map/ppermute | solution.py:348
  47.1 0.0 collective-permute-done.1.refs_0_
  47.2 1.9 %collective-permute-done.2.refs_1_ = bf16[144,384]{1,0:T(8,128)(2,1)S(1)} collective-permute-done((bf16[144,384]{1,0:T(8,128)(2,1)S(1)}, bf16[144,384]{1,0:T(8,128)(2,1)S(1)}, u32[]{:S(2)}, u32[]{:S(2)}) %collective-permute-start.2) | collective-permute-done | bytes 110624 | tf_op jit(solution)/shard_map/ppermute | solution.py:348
  49.0 4.0 %collective-permute-done.3.refs_2_ = bf16[144,384]{1,0:T(8,128)(2,1)S(1)} collective-permute-done((bf16[144,384]{1,0:T(8,128)(2,1)S(1)}, bf16[144,384]{1,0:T(8,128)(2,1)S(1)}, u32[]{:S(2)}, u32[]{:S(2)}) %collective-permute-start.3) | collective-permute-done | bytes 110624 | tf_op jit(solution)/shard_map/ppermute | solution.py:348
  53.1 0.0 all-to-all-done.1
  53.1 5.2 %shard_map.61 = (bf16[128,384]{1,0:T(8,128)(2,1)}, bf16[4,1040,128]{2,1,0:T(8,128)(2,1)}, bf16[4096,384]{1,0:T(8,128)(2,1)}, f32[8,384]{1,0:T(8,128)S(1)}) custom-call(f32[128,384]{1,0:T(8,128)S(1)} %get-tuple-element.29.mean_ref, f32[8,384]{1,0:T(8,128)S(1)} %get-tuple-element.30.chip_ref, bf16[144,384]{1,0:T(8,128)(2,1)S(1)} %collective-permute-done.1.refs_0_, ...), custom_call_target="tpu_custom_call" | custom-call | flops 1 | bytes 1 | tf_op jit(solution)/shard_map/pallas_call | solution.py:242
  58.3 4.8 %all-to-all-start.2 = ((bf16[4,1040,128]{2,1,0:T(8,128)(2,1)}), bf16[4,1040,128]{2,1,0:T(8,128)(2,1)S(1)}, u32[]{:S(2)}, u32[]{:S(2)}) async-start(bf16[4,1040,128]{2,1,0:T(8,128)(2,1)} %get-tuple-element.40), calls=%async_computation.2 | async-start | bytes 2129920 | tf_op jit(solution)/shard_map/all_to_all | solution.py:23
  63.1 0.0 copy-start.2
  63.1 2.7 %multiply_reduce_fusion = f32[384]{0:T(512)S(1)} fusion(bf16[128,384]{1,0:T(8,128)(2,1)} %get-tuple-element.21, f32[384]{0:T(512)S(1)} %slice_reduce_fusion, bf16[4096,128]{1,0:T(8,128)(2,1)S(1)} %bitcast.9, bf16[4096,384]{1,0:T(8,128)(2,1)} %get-tuple-element.41), kind=kOutput, calls=%fused_computation.1 | convolution fusion | flops 402898560 | bytes 4295680 | tf_op jit(solution)/shard_map/dot_general | solution.py:354
  65.8 0.6 div.10
  66.4 9.2 %all-to-all-done.2.sums_ref = bf16[4,1040,128]{2,1,0:T(8,128)(2,1)S(1)} async-done(((bf16[4,1040,128]{2,1,0:T(8,128)(2,1)}), bf16[4,1040,128]{2,1,0:T(8,128)(2,1)S(1)}, u32[]{:S(2)}, u32[]{:S(2)}) %all-to-all-start.2) | async-done | bytes 1064992 | tf_op jit(solution)/shard_map/all_to_all | solution.py:23
  75.5 0.1 shard_map.62
  75.6 25.0 %all_to_all.20.sums_ref = bf16[16,72,128]{2,1,0:T(8,128)(2,1)S(1)} all-to-all(bf16[16,72,128]{2,1,0:T(8,128)(2,1)S(1)} %shard_map.62), channel_id=1, replica_groups={{64,72,80,88,96,104,112,120,0,8,16,24,32,40,48,56},{65,73,81,89,97,105,..., dimensions={0} | all-to-all | bytes 589824 | tf_op jit(solution)/shard_map/all_to_all | solution.py:23
  100.7 0.0 copy-done.2
  100.7 0.8 shard_map.63
  (2 shorter events, 0.0 us)
Async XLA Ops:
  2.1 30.8 %all-to-all-start = ((bf16[16,64,128]{2,1,0:T(8,128)(2,1)}), bf16[16,64,128]{2,1,0:T(8,128)(2,1)S(1)}, u32[]{:S(2)}, u32[]{:S(2)}) async-start(bf16[16,64,128]{2,1,0:T(8,128)(2,1)} %broadcast_in_dim.10), calls=%async_computation | async-start | bytes 524288 | tf_op jit(solution)/shard_map/all_to_all | solution.py:23
  19.2 2.2 %copy-start = (bf16[2048,1024]{1,0:T(8,128)(2,1)S(1)}, bf16[2048,1024]{1,0:T(8,128)(2,1)}, u32[]{:S(2)}) copy-start(bf16[2048,1024]{1,0:T(8,128)(2,1)} %c_ref.3) | copy-start | bytes 12582916
  21.4 1.1 %copy-start.1 = (bf16[384,1024]{1,0:T(8,128)(2,1)S(1)}, bf16[384,1024]{1,0:T(8,128)(2,1)}, u32[]{:S(2)}) copy-start(bf16[384,1024]{1,0:T(8,128)(2,1)} %e_ref.3) | copy-start | bytes 2359300
  27.0 3.8 %collective-permute-start = (bf16[528,384]{1,0:T(8,128)(2,1)S(1)}, bf16[528,384]{1,0:T(8,128)(2,1)S(1)}, u32[]{:S(2)}, u32[]{:S(2)}) collective-permute-start(bf16[528,384]{1,0:T(8,128)(2,1)S(1)} %get-tuple-element.27), channel_id=1, source_target_pairs={{0,1},{1,0},{2,3},{3,2},{4,5},{5,4},{6,7},{7,6},{8,9},{9,8},{10,11... | collective-permute-start | bytes 1216520 | tf_op jit(solution)/shard_map/ppermute | solution.py:342
  34.0 19.0 %all-to-all-start.1 = ((bf16[4,1024,128]{2,1,0:T(8,128)(2,1)}), bf16[4,1024,128]{2,1,0:T(8,128)(2,1)S(1)}, u32[]{:S(2)}, u32[]{:S(2)}) async-start(bf16[4,1024,128]{2,1,0:T(8,128)(2,1)} %broadcast_in_dim.11), calls=%async_computation.1 | async-start | bytes 2097152 | tf_op jit(solution)/shard_map/all_to_all | solution.py:23
  38.5 8.6 %collective-permute-start.1 = (bf16[144,384]{1,0:T(8,128)(2,1)S(1)}, bf16[144,384]{1,0:T(8,128)(2,1)S(1)}, u32[]{:S(2)}, u32[]{:S(2)}) collective-permute-start(bf16[144,384]{1,0:T(8,128)(2,1)S(1)} %get-tuple-element.34), channel_id=1, source_target_pairs={{0,2},{2,4},{4,6},{6,0},{1,3},{3,5},{5,7},{7,1},{8,10},{10,12},{12... | collective-permute-start | bytes 331784 | tf_op jit(solution)/shard_map/ppermute | solution.py:348
  40.9 8.1 %collective-permute-start.2 = (bf16[144,384]{1,0:T(8,128)(2,1)S(1)}, bf16[144,384]{1,0:T(8,128)(2,1)S(1)}, u32[]{:S(2)}, u32[]{:S(2)}) collective-permute-start(bf16[144,384]{1,0:T(8,128)(2,1)S(1)} %get-tuple-element.35), channel_id=1, source_target_pairs={{0,4},{2,6},{4,0},{6,2},{1,5},{3,7},{5,1},{7,3},{8,12},{10,14},{12... | collective-permute-start | bytes 331784 | tf_op jit(solution)/shard_map/ppermute | solution.py:348
  45.2 7.9 %collective-permute-start.3 = (bf16[144,384]{1,0:T(8,128)(2,1)S(1)}, bf16[144,384]{1,0:T(8,128)(2,1)S(1)}, u32[]{:S(2)}, u32[]{:S(2)}) collective-permute-start(bf16[144,384]{1,0:T(8,128)(2,1)S(1)} %get-tuple-element.36), channel_id=1, source_target_pairs={{0,6},{2,0},{4,2},{6,4},{1,7},{3,1},{5,3},{7,5},{8,14},{10,8},{12,... | collective-permute-start | bytes 331784 | tf_op jit(solution)/shard_map/ppermute | solution.py:348
  58.3 17.2 %all-to-all-start.2 = ((bf16[4,1040,128]{2,1,0:T(8,128)(2,1)}), bf16[4,1040,128]{2,1,0:T(8,128)(2,1)S(1)}, u32[]{:S(2)}, u32[]{:S(2)}) async-start(bf16[4,1040,128]{2,1,0:T(8,128)(2,1)} %get-tuple-element.40), calls=%async_computation.2 | async-start | bytes 2129920 | tf_op jit(solution)/shard_map/all_to_all | solution.py:23
  63.1 37.6 %copy-start.2 = (bf16[1,64,128]{2,1,0:T(8,128)(2,1)S(1)}, bf16[1,64,128]{2,1,0:T(8,128)(2,1)}, u32[]{:S(2)}) copy-start(bf16[1,64,128]{2,1,0:T(8,128)(2,1)} %param.5) | copy-start | bytes 49156

commit v13 on v12

--- a/solution.py
+++ b/solution.py
@@ -15,6 +15,7 @@
 PACKED = 16
 BOOK_FIRST = 10
 SUMS_FIRST = 8
+Y_FIRST = 2
 
 
 def exchange(parts, axis, first=0):
@@ -347,10 +348,10 @@
         ring = [(i, (i + step) % x_count) for i in range(x_count)]
         gots[step] = lax.ppermute(blocks[step - 1], "x", ring)
     gots = [gots[step] for step in (1, 2, 3)]
-    book = exchange(jnp.broadcast_to(book, (y_count,) + book.shape), "y").reshape(words, sub_width)
+    book = exchange(jnp.broadcast_to(book, (y_count,) + book.shape), "y", Y_FIRST).reshape(words, sub_width)
     residual, sums, raised, inverse = quantize(mean, stats, gots, base, book, y_count)
 
-    sums = exchange(sums, "y")
+    sums = exchange(sums, "y", Y_FIRST)
     rebuilt = lax.dot_general(
         book, raised, (((0,), (0,)), ((), ())), preferred_element_type=jnp.float32
     ) * inverse[:1]

time: 102 us -> 103 us (level)
  waiting for transfers between devices: 16.5 us -> 13.8 us
  starting transfers between devices: 36.9 us -> 39.1 us
    all_to_all x3, waiting for transfers between devices: 10.6 us -> 7.85 us  [exchange(): lax.all_to_all(parts, axis, 0, 0, axis_index_groups=order, tiled=True)]
    all_to_all x3, starting transfers between devices: 26.3 us -> 28.5 us  [exchange(): lax.all_to_all(parts, axis, 0, 0, axis_index_groups=order, tiled=True)]
where the time goes in v13:
time: 103 us; the launch traced here: 102 us
  starting transfers between devices  39.1 us (38%)
  blocking collectives  26 us (25%)
  waiting for transfers between devices  13.8 us (13%)
  Pallas kernels  13.1 us (13%)
  local copies, waits for them, and re-layouts  6.49 us (6%)
  matrix products  2.65 us (3%)
    all_to_all x3, starting transfers between devices, exchange(): lax.all_to_all(parts, axis, 0, 0, axis_index_groups=order, tiled=True)  28.5 us
    all_to_all x1, blocking collectives, exchange(): lax.all_to_all(parts, axis, 0, 0, axis_index_groups=order, tiled=True)  26 us
    pallas_call x6, Pallas kernels, call(): pl.pallas_call(kernel, out_shape=out_shape, in_specs=ins, out_specs=outs...  13.1 us
    ppermute x3, starting transfers between devices, local(): gots[step] = lax.ppermute(blocks[step - 1], 'x', ring)  8.62 us
    all_to_all x3, waiting for transfers between devices, exchange(): lax.all_to_all(parts, axis, 0, 0, axis_index_groups=order, tiled=True)  7.85 us
    ppermute x3, waiting for transfers between devices, local(): gots[step] = lax.ppermute(blocks[step - 1], 'x', ring)  5.92 us
    unnamed x6, local copies, waits for them, and re-layouts  3.32 us
    dot_general x1, matrix products, local(): lax.dot_general(book, raised, (((0,), (0,)), ((), ())), preferred_element...  2.65 us
  transfers between devices with their start and end apart: 7, of which 4 were waited for; matrix products, arithmetic and copies ran while one was open for 3% of the time, Pallas kernels for 7%

profile of v13, /device:TPU:6, one launch (start us, length us, event | category | flops | bytes accessed | tf_op | source)
XLA Modules:
  0.0 101.9 jit_solution(549387306595002689)
XLA Ops:
  0.6 1.5 %broadcast_in_dim.10 = bf16[16,64,128]{2,1,0:T(8,128)(2,1)} broadcast(bf16[64,128]{1,0:T(8,128)(2,1)} %bitcast.10), dimensions={1,2} | broadcast | bytes 278528 | tf_op jit(solution)/shard_map/broadcast_in_dim | solution.py:339
  2.1 17.1 %all-to-all-start = ((bf16[16,64,128]{2,1,0:T(8,128)(2,1)}), bf16[16,64,128]{2,1,0:T(8,128)(2,1)S(1)}, u32[]{:S(2)}, u32[]{:S(2)}) async-start(bf16[16,64,128]{2,1,0:T(8,128)(2,1)} %broadcast_in_dim.10), calls=%async_computation | async-start | bytes 524288 | tf_op jit(solution)/shard_map/all_to_all | solution.py:24
  19.2 0.1 pad_add_fusion.place_ref
  19.2 0.0 copy-start
  19.2 2.2 %copy-done = bf16[2048,1024]{1,0:T(8,128)(2,1)S(1)} copy-done((bf16[2048,1024]{1,0:T(8,128)(2,1)S(1)}, bf16[2048,1024]{1,0:T(8,128)(2,1)}, u32[]{:S(2)}) %copy-start) | copy-done | bytes 4194328
  21.4 0.0 copy-start.1
  21.4 1.1 %copy-done.1 = bf16[384,1024]{1,0:T(8,128)(2,1)S(1)} copy-done((bf16[384,1024]{1,0:T(8,128)(2,1)S(1)}, bf16[384,1024]{1,0:T(8,128)(2,1)}, u32[]{:S(2)}) %copy-start.1) | copy-done | bytes 786456
  22.6 4.4 %shard_map.58 = (bf16[528,384]{1,0:T(8,128)(2,1)S(1)}, f32[8,384]{1,0:T(8,128)S(1)}, bf16[384,2048]{1,0:T(8,128)(2,1)S(1)}, f32[384,128]{1,0:T(8,128)S(1)}) custom-call(s32[2]{0:T(128)S(1)} %pad_add_fusion.place_ref, bf16[384,1024]{1,0:T(8,128)(2,1)S(1)} %copy-done.1, bf16[2048,1024]{1,0:T(8,128)(2,1)S(1)} %copy-done), custom_call_target="tpu_custom_call" | custom-call | flops 1 | bytes 1 | tf_op jit(solution)/shard_map/pallas_call | solution.py:243
  27.0 1.9 %collective-permute-start = (bf16[528,384]{1,0:T(8,128)(2,1)S(1)}, bf16[528,384]{1,0:T(8,128)(2,1)S(1)}, u32[]{:S(2)}, u32[]{:S(2)}) collective-permute-start(bf16[528,384]{1,0:T(8,128)(2,1)S(1)} %get-tuple-element.27), channel_id=1, source_target_pairs={{0,1},{1,0},{2,3},{3,2},{4,5},{5,4},{6,7},{7,6},{8,9},{9,8},{10,11... | collective-permute-start | bytes 1216520 | tf_op jit(solution)/shard_map/ppermute | solution.py:343
  28.9 1.8 %shard_map.59 = (f32[512,384]{1,0:T(8,128)S(1)}, f32[128,384]{1,0:T(8,128)S(1)}) custom-call(s32[2]{0:T(128)S(1)} %pad_add_fusion.place_ref, bf16[384,2048]{1,0:T(8,128)(2,1)S(1)} %get-tuple-element.24.weights_ref, f32[384,128]{1,0:T(8,128)S(1)} %get-tuple-element.25.inverse_ref, bf16[2048,1024]{1,0:T(8,128)(2,1)S(1)} %copy-done, bf16[384,1024]{1,0:T(8,128)(2,1)S(1)} %copy-done.1), custom_call_target="tpu_custom_call" | custom-call | flops 1 | bytes 1 | tf_op jit(solution)/shard_map/pallas_call | solution.py:243
  30.8 0.0 collective-permute-done.got_ref
  30.8 0.7 shard_map.60
  31.5 1.4 %all-to-all-done = bf16[16,64,128]{2,1,0:T(8,128)(2,1)S(1)} async-done(((bf16[16,64,128]{2,1,0:T(8,128)(2,1)}), bf16[16,64,128]{2,1,0:T(8,128)(2,1)S(1)}, u32[]{:S(2)}, u32[]{:S(2)}) %all-to-all-start) | async-done | bytes 262176 | tf_op jit(solution)/shard_map/all_to_all | solution.py:24
  32.9 1.1 %broadcast_in_dim.11 = bf16[4,1024,128]{2,1,0:T(8,128)(2,1)} broadcast(bf16[1024,128]{1,0:T(8,128)(2,1)S(1)} %bitcast.12), dimensions={1,2} | broadcast | bytes 1310720 | tf_op jit(solution)/shard_map/broadcast_in_dim | solution.py:351
  34.0 6.7 %all-to-all-start.1 = ((bf16[4,1024,128]{2,1,0:T(8,128)(2,1)}), bf16[4,1024,128]{2,1,0:T(8,128)(2,1)S(1)}, u32[]{:S(2)}, u32[]{:S(2)}) async-start(bf16[4,1024,128]{2,1,0:T(8,128)(2,1)} %broadcast_in_dim.11), calls=%async_computation.1 | async-start | bytes 2097152 | tf_op jit(solution)/shard_map/all_to_all | solution.py:24
  40.7 2.4 %collective-permute-start.1 = (bf16[144,384]{1,0:T(8,128)(2,1)S(1)}, bf16[144,384]{1,0:T(8,128)(2,1)S(1)}, u32[]{:S(2)}, u32[]{:S(2)}) collective-permute-start(bf16[144,384]{1,0:T(8,128)(2,1)S(1)} %get-tuple-element.34), channel_id=1, source_target_pairs={{0,2},{2,4},{4,6},{6,0},{1,3},{3,5},{5,7},{7,1},{8,10},{10,12},{12... | collective-permute-start | bytes 331784 | tf_op jit(solution)/shard_map/ppermute | solution.py:349
  43.1 4.3 %collective-permute-start.2 = (bf16[144,384]{1,0:T(8,128)(2,1)S(1)}, bf16[144,384]{1,0:T(8,128)(2,1)S(1)}, u32[]{:S(2)}, u32[]{:S(2)}) collective-permute-start(bf16[144,384]{1,0:T(8,128)(2,1)S(1)} %get-tuple-element.35), channel_id=1, source_target_pairs={{0,4},{2,6},{4,0},{6,2},{1,5},{3,7},{5,1},{7,3},{8,12},{10,14},{12... | collective-permute-start | bytes 331784 | tf_op jit(solution)/shard_map/ppermute | solution.py:349
  47.4 1.9 %collective-permute-start.3 = (bf16[144,384]{1,0:T(8,128)(2,1)S(1)}, bf16[144,384]{1,0:T(8,128)(2,1)S(1)}, u32[]{:S(2)}, u32[]{:S(2)}) collective-permute-start(bf16[144,384]{1,0:T(8,128)(2,1)S(1)} %get-tuple-element.36), channel_id=1, source_target_pairs={{0,6},{2,0},{4,2},{6,4},{1,7},{3,1},{5,3},{7,5},{8,14},{10,8},{12,... | collective-permute-start | bytes 331784 | tf_op jit(solution)/shard_map/ppermute | solution.py:349
  49.4 0.0 collective-permute-done.1.refs_0_
  49.4 1.9 %collective-permute-done.2.refs_1_ = bf16[144,384]{1,0:T(8,128)(2,1)S(1)} collective-permute-done((bf16[144,384]{1,0:T(8,128)(2,1)S(1)}, bf16[144,384]{1,0:T(8,128)(2,1)S(1)}, u32[]{:S(2)}, u32[]{:S(2)}) %collective-permute-start.2) | collective-permute-done | bytes 110624 | tf_op jit(solution)/shard_map/ppermute | solution.py:349
  51.2 4.0 %collective-permute-done.3.refs_2_ = bf16[144,384]{1,0:T(8,128)(2,1)S(1)} collective-permute-done((bf16[144,384]{1,0:T(8,128)(2,1)S(1)}, bf16[144,384]{1,0:T(8,128)(2,1)S(1)}, u32[]{:S(2)}, u32[]{:S(2)}) %collective-permute-start.3) | collective-permute-done | bytes 110624 | tf_op jit(solution)/shard_map/ppermute | solution.py:349
  55.3 0.0 all-to-all-done.1
  55.3 5.2 %shard_map.61 = (bf16[128,384]{1,0:T(8,128)(2,1)}, bf16[4,1040,128]{2,1,0:T(8,128)(2,1)}, bf16[4096,384]{1,0:T(8,128)(2,1)}, f32[8,384]{1,0:T(8,128)S(1)}) custom-call(f32[128,384]{1,0:T(8,128)S(1)} %get-tuple-element.29.mean_ref, f32[8,384]{1,0:T(8,128)S(1)} %get-tuple-element.30.chip_ref, bf16[144,384]{1,0:T(8,128)(2,1)S(1)} %collective-permute-done.1.refs_0_, ...), custom_call_target="tpu_custom_call" | custom-call | flops 1 | bytes 1 | tf_op jit(solution)/shard_map/pallas_call | solution.py:243
  60.5 4.8 %all-to-all-start.2 = ((bf16[4,1040,128]{2,1,0:T(8,128)(2,1)}), bf16[4,1040,128]{2,1,0:T(8,128)(2,1)S(1)}, u32[]{:S(2)}, u32[]{:S(2)}) async-start(bf16[4,1040,128]{2,1,0:T(8,128)(2,1)} %get-tuple-element.40), calls=%async_computation.2 | async-start | bytes 2129920 | tf_op jit(solution)/shard_map/all_to_all | solution.py:24
  65.3 0.0 copy-start.2
  65.3 2.6 %multiply_reduce_fusion = f32[384]{0:T(512)S(1)} fusion(bf16[128,384]{1,0:T(8,128)(2,1)} %get-tuple-element.21, f32[384]{0:T(512)S(1)} %slice_reduce_fusion, bf16[4096,128]{1,0:T(8,128)(2,1)S(1)} %bitcast.9, bf16[4096,384]{1,0:T(8,128)(2,1)} %get-tuple-element.41), kind=kOutput, calls=%fused_computation.1 | convolution fusion | flops 402898560 | bytes 4295680 | tf_op jit(solution)/shard_map/dot_general | solution.py:355
  68.0 0.6 div.10
  68.6 6.4 %all-to-all-done.2.sums_ref = bf16[4,1040,128]{2,1,0:T(8,128)(2,1)S(1)} async-done(((bf16[4,1040,128]{2,1,0:T(8,128)(2,1)}), bf16[4,1040,128]{2,1,0:T(8,128)(2,1)S(1)}, u32[]{:S(2)}, u32[]{:S(2)}) %all-to-all-start.2) | async-done | bytes 1064992 | tf_op jit(solution)/shard_map/all_to_all | solution.py:24
  75.0 0.1 shard_map.62
  75.1 26.0 %all_to_all.20.sums_ref = bf16[16,72,128]{2,1,0:T(8,128)(2,1)S(1)} all-to-all(bf16[16,72,128]{2,1,0:T(8,128)(2,1)S(1)} %shard_map.62), channel_id=1, replica_groups={{64,72,80,88,96,104,112,120,0,8,16,24,32,40,48,56},{65,73,81,89,97,105,..., dimensions={0} | all-to-all | bytes 589824 | tf_op jit(solution)/shard_map/all_to_all | solution.py:24
  101.1 0.0 copy-done.2
  101.1 0.8 shard_map.63
  (2 shorter events, 0.0 us)
Async XLA Ops:
  2.1 30.8 %all-to-all-start = ((bf16[16,64,128]{2,1,0:T(8,128)(2,1)}), bf16[16,64,128]{2,1,0:T(8,128)(2,1)S(1)}, u32[]{:S(2)}, u32[]{:S(2)}) async-start(bf16[16,64,128]{2,1,0:T(8,128)(2,1)} %broadcast_in_dim.10), calls=%async_computation | async-start | bytes 524288 | tf_op jit(solution)/shard_map/all_to_all | solution.py:24
  19.2 2.2 %copy-start = (bf16[2048,1024]{1,0:T(8,128)(2,1)S(1)}, bf16[2048,1024]{1,0:T(8,128)(2,1)}, u32[]{:S(2)}) copy-start(bf16[2048,1024]{1,0:T(8,128)(2,1)} %c_ref.3) | copy-start | bytes 12582916
  21.4 1.1 %copy-start.1 = (bf16[384,1024]{1,0:T(8,128)(2,1)S(1)}, bf16[384,1024]{1,0:T(8,128)(2,1)}, u32[]{:S(2)}) copy-start(bf16[384,1024]{1,0:T(8,128)(2,1)} %e_ref.3) | copy-start | bytes 2359300
  27.0 3.8 %collective-permute-start = (bf16[528,384]{1,0:T(8,128)(2,1)S(1)}, bf16[528,384]{1,0:T(8,128)(2,1)S(1)}, u32[]{:S(2)}, u32[]{:S(2)}) collective-permute-start(bf16[528,384]{1,0:T(8,128)(2,1)S(1)} %get-tuple-element.27), channel_id=1, source_target_pairs={{0,1},{1,0},{2,3},{3,2},{4,5},{5,4},{6,7},{7,6},{8,9},{9,8},{10,11... | collective-permute-start | bytes 1216520 | tf_op jit(solution)/shard_map/ppermute | solution.py:343
  34.0 21.3 %all-to-all-start.1 = ((bf16[4,1024,128]{2,1,0:T(8,128)(2,1)}), bf16[4,1024,128]{2,1,0:T(8,128)(2,1)S(1)}, u32[]{:S(2)}, u32[]{:S(2)}) async-start(bf16[4,1024,128]{2,1,0:T(8,128)(2,1)} %broadcast_in_dim.11), calls=%async_computation.1 | async-start | bytes 2097152 | tf_op jit(solution)/shard_map/all_to_all | solution.py:24
  40.7 8.6 %collective-permute-start.1 = (bf16[144,384]{1,0:T(8,128)(2,1)S(1)}, bf16[144,384]{1,0:T(8,128)(2,1)S(1)}, u32[]{:S(2)}, u32[]{:S(2)}) collective-permute-start(bf16[144,384]{1,0:T(8,128)(2,1)S(1)} %get-tuple-element.34), channel_id=1, source_target_pairs={{0,2},{2,4},{4,6},{6,0},{1,3},{3,5},{5,7},{7,1},{8,10},{10,12},{12... | collective-permute-start | bytes 331784 | tf_op jit(solution)/shard_map/ppermute | solution.py:349
  43.1 8.1 %collective-permute-start.2 = (bf16[144,384]{1,0:T(8,128)(2,1)S(1)}, bf16[144,384]{1,0:T(8,128)(2,1)S(1)}, u32[]{:S(2)}, u32[]{:S(2)}) collective-permute-start(bf16[144,384]{1,0:T(8,128)(2,1)S(1)} %get-tuple-element.35), channel_id=1, source_target_pairs={{0,4},{2,6},{4,0},{6,2},{1,5},{3,7},{5,1},{7,3},{8,12},{10,14},{12... | collective-permute-start | bytes 331784 | tf_op jit(solution)/shard_map/ppermute | solution.py:349
  47.4 7.9 %collective-permute-start.3 = (bf16[144,384]{1,0:T(8,128)(2,1)S(1)}, bf16[144,384]{1,0:T(8,128)(2,1)S(1)}, u32[]{:S(2)}, u32[]{:S(2)}) collective-permute-start(bf16[144,384]{1,0:T(8,128)(2,1)S(1)} %get-tuple-element.36), channel_id=1, source_target_pairs={{0,6},{2,0},{4,2},{6,4},{1,7},{3,1},{5,3},{7,5},{8,14},{10,8},{12,... | collective-permute-start | bytes 331784 | tf_op jit(solution)/shard_map/ppermute | solution.py:349
  60.5 14.5 %all-to-all-start.2 = ((bf16[4,1040,128]{2,1,0:T(8,128)(2,1)}), bf16[4,1040,128]{2,1,0:T(8,128)(2,1)S(1)}, u32[]{:S(2)}, u32[]{:S(2)}) async-start(bf16[4,1040,128]{2,1,0:T(8,128)(2,1)} %get-tuple-element.40), calls=%async_computation.2 | async-start | bytes 2129920 | tf_op jit(solution)/shard_map/all_to_all | solution.py:24
  65.3 35.8 %copy-start.2 = (bf16[1,64,128]{2,1,0:T(8,128)(2,1)S(1)}, bf16[1,64,128]{2,1,0:T(8,128)(2,1)}, u32[]{:S(2)}) copy-start(bf16[1,64,128]{2,1,0:T(8,128)(2,1)} %param.5) | copy-start | bytes 49156
